TPU v7x, 32 devices: a whole 2x2x4 slice. The times are simulated.
32 devices in a mesh: groups: 2 (over y), wide: 8 (over z, x), head: 2 (over core).
Axes of the slice: x: 2, y: 2, z: 4, core: 2. Of those that a mesh axis runs over, the one named last changes fastest.
Arguments:
- tokens: bfloat16 [1024, 2048], P(('groups', 'wide'), 'head'), parts along dimension 0, may hold values from -6 to 6
- expert_ids: int32 [1024, 8], P(('groups', 'wide')), parts along dimension 0, may hold values from 0 to 7, as said below
- gate_scores: float32 [1024, 8], P(('groups', 'wide')), parts along dimension 0, may hold values from 0.25 to 1
- gate_proj: bfloat16 [8, 704, 2048], P('wide', 'head'), may hold values from -0.125 to 0.125
- up_proj: bfloat16 [8, 704, 2048], P('wide', 'head'), may hold values from -0.125 to 0.125
- down_proj: bfloat16 [8, 704, 2048], P('wide', 'head'), may hold values from -0.21875 to 0.21875
Outputs:
- mixed: bfloat16 [1024, 2048], P(('groups', 'wide'), 'head'), parts along dimension 0
There are 2 independent parts, one for each index of `groups`. A program takes and returns all parts, laid end to end along the dimension named above; an argument that names none is the same for every part. Nothing has to cross between parts.
Inputs may be any that keep to these rules, and one draw needn't show every extreme that they name: `expert_ids`: each row names 8 different experts. Within each aligned block of 64 rows at most 64 rows name the same expert, and in every draw one expert is named by exactly 64 rows of every such block.
All inputs are finite; a program needn't handle non-finite values.
Results may differ from a plain program's by a relative error of at most 0.01.
Values may be sent and summed in bfloat16 or wider, within the bound.
No kernel may reach another device: no remote copies, remote signals or barrier semaphores. Data moves between devices by JAX's collectives and lax.ppermute only.
A program may use at most 64 MiB of HBM per device.

v0:
```python
import jax
import jax.numpy as jnp
from jax import lax
from jax.sharding import PartitionSpec as P


def local(tokens, expert_ids, gate_scores, gate_proj, up_proj, down_proj):
    experts = lax.axis_size("wide")
    tok_rows, top_count = expert_ids.shape
    ceiling = (tok_rows * top_count + experts - 1) // experts
    capacity = min(tok_rows, max(2, tok_rows // 8, 2 * ceiling))
    flat_ids = expert_ids.reshape(-1)
    expert_numbers = jnp.arange(experts, dtype=jnp.int32)
    onehot = (flat_ids[:, None] == expert_numbers[None, :]).astype(jnp.int32)
    earlier = jnp.cumsum(onehot, axis=0) - onehot
    slot_index = jnp.sum(earlier * onehot, axis=1)
    position = flat_ids * capacity + slot_index
    targets = jnp.arange(experts * capacity, dtype=jnp.int32)
    placing = jnp.any(
        position.reshape(tok_rows, top_count)[:, :, None] == targets[None, None, :], axis=1
    ).astype(jnp.bfloat16)
    w_gate = gate_proj[0]
    w_up = up_proj[0]
    w_down = down_proj[0]
    placed = lax.dot_general(
        placing, tokens, (((0,), (0,)), ((), ())), preferred_element_type=jnp.float32
    )
    outgoing = placed.astype(jnp.bfloat16).reshape(experts, capacity, tokens.shape[1])
    full_rows = lax.all_gather(
        lax.all_to_all(outgoing, "wide", split_axis=0, concat_axis=0, tiled=True),
        "head",
        axis=2,
        tiled=True,
    )
    src_count, item_count, feature_width = full_rows.shape
    stacked = full_rows.reshape(src_count * item_count, feature_width)
    gate_part = lax.dot_general(
        stacked, w_gate, (((1,), (1,)), ((), ())), preferred_element_type=jnp.float32
    )
    up_part = lax.dot_general(
        stacked, w_up, (((1,), (1,)), ((), ())), preferred_element_type=jnp.float32
    )
    hidden = (jax.nn.silu(gate_part) * up_part).astype(jnp.bfloat16)
    partial_value = jnp.dot(hidden, w_down, preferred_element_type=jnp.float32)
    partial_value = partial_value.reshape(src_count, item_count, feature_width)
    back = lax.psum_scatter(
        partial_value.astype(jnp.bfloat16), "head", scatter_dimension=2, tiled=True
    ).astype(jnp.float32)
    returned = lax.all_to_all(
        back.astype(jnp.bfloat16), "wide", split_axis=0, concat_axis=0, tiled=True
    ).astype(back.dtype)
    picked = returned.reshape(experts * capacity, returned.shape[2])[position]
    picked = picked.reshape(tok_rows, top_count, returned.shape[2])
    mixed = jnp.sum(gate_scores[:, :, None] * picked, axis=1)
    return mixed.astype(jnp.bfloat16)


def solution(mesh):
    return jax.shard_map(
        local,
        mesh=mesh,
        in_specs=(
            P(("groups", "wide"), "head"),
            P(("groups", "wide"), None),
            P(("groups", "wide"), None),
            P("wide", "head", None),
            P("wide", "head", None),
            P("wide", "head", None),
        ),
        out_specs=P(("groups", "wide"), "head"),
        check_vma=False,
    )
```

profile of v0, /device:TPU:0, one launch (start us, length us, event | category | flops | bytes accessed | tf_op | source)
XLA Modules:
  0.0 117.7 jit_solution(13483769979636147468)
XLA Ops:
  6.5 0.0 copy-start
  6.5 0.0 all-gather.2.cloned.1.call-start
  6.5 0.9 copy.16
  7.4 0.1 eq.42
  7.5 0.1 eq.38
  7.6 1.1 reduce-window.6
  8.8 0.2 slice_reduce_fusion
  9.0 0.1 fusion.14
  9.1 0.1 reduce_sum.23
  9.2 0.4 fusion.12
  9.6 1.4 %convolution_convert_fusion.1 = bf16[512,1024]{1,0:T(8,128)(2,1)S(1)} fusion(pred[64,512]{1,0:T(8,128)(4,1)S(1)} %fusion.12, bf16[64,1024]{1,0:T(8,128)(2,1)} %param.6), kind=kOutput, calls=%fused_computation.4 | convolution fusion | flops 67633152 | bytes 1212416 | tf_op jit(solution)/shard_map/dot_general | solution.py:25
  11.0 32.9 %all_to_all.10 = bf16[8,64,1024]{2,1,0:T(8,128)(2,1)} all-to-all(bf16[8,64,1024]{2,1,0:T(8,128)(2,1)S(1)} %bitcast.39), channel_id=1, replica_groups=mesh['groups'=2,'wide'=8,'head'=2] {'wide'}, dimensions={0} | all-to-all | bytes 2097152 | tf_op jit(solution)/shard_map/all_to_all | solution.py:30
  43.9 0.0 all-gather.2.cloned.1.call-update
  44.0 0.0 reduce-scatter.2.cloned.1.call-start
  44.0 9.7 %all-gather.2.cloned.1.call-done = bf16[8,64,2048]{2,1,0:T(8,128)(2,1)} async-done(((bf16[8,64,1024]{2,1,0:T(8,128)(2,1)}), bf16[8,64,2048]{2,1,0:T(8,128)(2,1)}) %all-gather.2.cloned.1.call-update) | async-done | bytes 2097168 | tf_op jit(solution)/shard_map/all_gather | solution.py:29
  53.7 0.0 copy-start.2
  53.7 0.0 copy-start.3
  53.7 3.1 %fusion.4 = f32[512,352]{0,1:T(8,128)S(1)} fusion(bf16[512,2048]{1,0:T(8,128)(2,1)} %bitcast.43, bf16[1,352,2048]{2,1,0:T(8,128)(2,1)} %param.9), kind=kOutput, calls=%fused_computation.8 | convolution fusion | flops 738197504 | bytes 4259840 | tf_op jit(solution)/shard_map/dot_general | solution.py:37
  56.8 0.0 copy-done.2
  56.8 0.0 copy-done.3
  56.8 1.0 fusion.9
  57.8 0.2 copy.19
  58.1 0.0 copy-done
  58.1 2.6 %convolution_convert_fusion = bf16[8,64,2048]{2,1,0:T(8,128)(2,1)} fusion(bf16[8,64,352]{2,1,0:T(8,128)(2,1)S(1)} %bitcast.40, bf16[1,352,2048]{2,1,0:T(8,128)(2,1)S(1)} %copy-done), kind=kOutput, calls=%fused_computation.1 | convolution fusion | flops 739246080 | bytes 3899392 | tf_op jit(solution)/shard_map/dot_general | solution.py:44
  60.7 0.0 copy-start.1
  60.7 0.0 reduce-scatter.2.cloned.1.call-update
  60.7 10.9 %reduce-scatter.2.cloned.1.call-done = bf16[8,64,1024]{2,1,0:T(8,128)(2,1)} async-done(((bf16[8,64,2048]{2,1,0:T(8,128)(2,1)}), bf16[8,64,1024]{2,1,0:T(8,128)(2,1)}) %reduce-scatter.2.cloned.1.call-update) | async-done | bytes 1048592 | tf_op jit(solution)/shard_map/reduce_scatter | solution.py:46
  71.6 5.8 %all-to-all-start.1 = ((bf16[8,64,1024]{2,1,0:T(8,128)(2,1)}), bf16[8,64,1024]{2,1,0:T(8,128)(2,1)}, u32[]{:S(2)}, u32[]{:S(2)}) async-start(bf16[8,64,1024]{2,1,0:T(8,128)(2,1)} %reduce-scatter.2.cloned.1.call-done), calls=%async_computation.2 | async-start | bytes 2097152 | tf_op jit(solution)/shard_map/all_to_all | solution.py:49
  77.4 0.1 mul.42
  77.5 0.0 copy-done.1
  77.5 0.7 copy.15
  78.2 25.5 %all-to-all-done.1 = bf16[8,64,1024]{2,1,0:T(8,128)(2,1)} async-done(((bf16[8,64,1024]{2,1,0:T(8,128)(2,1)}), bf16[8,64,1024]{2,1,0:T(8,128)(2,1)}, u32[]{:S(2)}, u32[]{:S(2)}) %all-to-all-start.1) | async-done | bytes 1048608 | tf_op jit(solution)/shard_map/all_to_all | solution.py:49
  103.7 1.5 %bitcast_convert_fusion = f32[512,1024]{1,0:T(8,128)S(1)} fusion(bf16[8,64,1024]{2,1,0:T(8,128)(2,1)} %all-to-all-done.1), kind=kLoop, calls=%fused_computation.12 | loop fusion | flops 524288 | bytes 3145728 | tf_op jit(solution)/shard_map/reshape | solution.py:52
  105.2 2.7 %gather_fusion = f32[512,1024]{1,0:T(8,128)} fusion(f32[512,1024]{1,0:T(8,128)S(1)} %bitcast_convert_fusion, s32[1024]{0:T(1024)S(1)} %pad_clamp_fusion), kind=kCustom, calls=%fused_computation | custom fusion | bytes 4196352 | tf_op jit(solution)/shard_map/gather | solution.py:52
  107.9 2.9 %fusion = bf16[64,1024]{1,0:T(8,128)(2,1)} fusion(f32[512,1024]{1,0:T(8,128)} %gather_fusion, f32[64,8]{1,0:T(8,128)} %copy.15), kind=kLoop, calls=%fused_computation.3 | loop fusion | flops 983040 | bytes 2230272 | tf_op jit(solution)/shard_map/reduce_sum | solution.py:54
  (6 shorter events, 0.1 us)
Async XLA Ops:
  6.5 51.5 %copy-start = (bf16[1,352,2048]{2,1,0:T(8,128)(2,1)S(1)}, bf16[1,352,2048]{2,1,0:T(8,128)(2,1)}, u32[]{:S(2)}) copy-start(bf16[1,352,2048]{2,1,0:T(8,128)(2,1)} %param.11) | copy-start | bytes 4325380
  6.5 47.2 %all-gather.2.cloned.1.call-start = ((), (), s32[]{:S(2)}) async-start(), calls=%async_computation.3 | async-start | bytes 3145728 | tf_op jit(solution)/shard_map/all_gather | solution.py:29
  44.0 27.7 %reduce-scatter.2.cloned.1.call-start = ((), (), s32[]{:S(2)}) async-start(), calls=%async_computation.4 | async-start | bytes 3145728 | tf_op jit(solution)/shard_map/reduce_scatter | solution.py:46
  53.7 3.1 %copy-start.2 = (bf16[8,64,2048]{2,1,0:T(8,128)(2,1)S(1)}, bf16[8,64,2048]{2,1,0:T(8,128)(2,1)}, u32[]{:S(2)}) copy-start(bf16[8,64,2048]{2,1,0:T(8,128)(2,1)} %all-gather.2.cloned.1.call-done) | copy-start | bytes 6291460
  53.7 3.1 %copy-start.3 = (bf16[1,352,2048]{2,1,0:T(8,128)(2,1)S(1)}, bf16[1,352,2048]{2,1,0:T(8,128)(2,1)}, u32[]{:S(2)}) copy-start(bf16[1,352,2048]{2,1,0:T(8,128)(2,1)} %param.10) | copy-start | bytes 4325380
  60.7 16.8 %copy-start.1 = (f32[64,8]{0,1:T(8,128)S(1)}, f32[64,8]{0,1:T(8,128)}, u32[]{:S(2)}) copy-start(f32[64,8]{0,1:T(8,128)} %param.8) | copy-start | bytes 6148
  71.6 32.1 %all-to-all-start.1 = ((bf16[8,64,1024]{2,1,0:T(8,128)(2,1)}), bf16[8,64,1024]{2,1,0:T(8,128)(2,1)}, u32[]{:S(2)}, u32[]{:S(2)}) async-start(bf16[8,64,1024]{2,1,0:T(8,128)(2,1)} %reduce-scatter.2.cloned.1.call-done), calls=%async_computation.2 | async-start | bytes 2097152 | tf_op jit(solution)/shard_map/all_to_all | solution.py:49
Sparse Core Ops, SparseCore 0:
  44.1 9.5 all-gather.1
  60.8 10.7 reduce-scatter.1
where the time goes:
time: 118 us
  waiting for transfers between devices  46.2 us (39%)
  blocking collectives  32.9 us (28%)
  between operations  13.5 us (11%)
  matrix products  8.06 us (7%)
  other arithmetic  6.06 us (5%)
  starting transfers between devices  5.84 us (5%)
  local copies, waits for them, and re-layouts  5.09 us (4%)
    all_to_all x1, blocking collectives, local(): lax.all_to_all(outgoing, 'wide', split_axis=0, concat_axis=0, tiled=True)  32.9 us
    all_to_all x1, waiting for transfers between devices, local(): lax.all_to_all(back.astype(jnp.bfloat16), 'wide', split_axis=0, concat_ax...  25.5 us
    reduce_scatter x1, waiting for transfers between devices, local(): lax.psum_scatter(partial_value.astype(jnp.bfloat16), 'head', scatter_dime...  10.9 us
    all_gather x1, waiting for transfers between devices, local(): lax.all_gather(lax.all_to_all(outgoing, 'wide', split_axis=0, concat_axis...  9.71 us
    all_to_all x1, starting transfers between devices, local(): lax.all_to_all(back.astype(jnp.bfloat16), 'wide', split_axis=0, concat_ax...  5.79 us
    dot_general x1, matrix products, local(): lax.dot_general(stacked, w_gate, (((1,), (1,)), ((), ())), preferred_elem...  3.08 us
    reduce_sum x1, other arithmetic, local(): mixed = jnp.sum(gate_scores[:, :, None] * picked, axis=1)  2.92 us
    gather x1, local copies, waits for them, and re-layouts, local(): picked = returned.reshape(experts * capacity, returned.shape[2])[position]  2.72 us
  transfers between devices with their start and end apart: 3, of which 3 were waited for; matrix products, arithmetic and copies ran while one was open for 1% of the time, Pallas kernels for 0%

commit v1 on v0

--- a/solution.py
+++ b/solution.py
@@ -1,10 +1,18 @@
+import functools
+
 import jax
 import jax.numpy as jnp
 from jax import lax
+from jax.experimental import pallas as pl
+from jax.experimental.pallas import tpu as pltpu
 from jax.sharding import PartitionSpec as P
 
-
-def local(tokens, expert_ids, gate_scores, gate_proj, up_proj, down_proj):
+LANES = 128
+PIECES = 3
+VMEM_LIMIT = 24 * 2**20
+
+
+def sparse_local(tokens, expert_ids, gate_scores, gate_proj, up_proj, down_proj):
     experts = lax.axis_size("wide")
     tok_rows, top_count = expert_ids.shape
     ceiling = (tok_rows * top_count + experts - 1) // experts
@@ -55,6 +63,142 @@
     return mixed.astype(jnp.bfloat16)
 
 
+def expert_kernel(counts, select_ref, *refs):
+    blocks = refs[: len(counts)]
+    wg0, wg1, wu0, wu1, wd0, wd1 = refs[len(counts) : len(counts) + 6]
+    outs = refs[len(counts) + 6 :]
+    width = wg0.shape[1]
+    whole = [b[...] for b in blocks]
+    rows = whole[0] if len(whole) == 1 else jnp.concatenate(whole, axis=0)
+    x = rows[:, :width]
+    scale = jnp.sum(rows[:, width:].astype(jnp.float32) * select_ref[...], axis=1, keepdims=True)
+    total = None
+    for wg, wu, wd in ((wg0, wu0, wd0), (wg1, wu1, wd1)):
+        gate = lax.dot_general(
+            x, wg[...], (((1,), (1,)), ((), ())), preferred_element_type=jnp.float32
+        )
+        up = lax.dot_general(
+            x, wu[...], (((1,), (1,)), ((), ())), preferred_element_type=jnp.float32
+        )
+        hidden = (gate / (1.0 + jnp.exp(-gate)) * up).astype(jnp.bfloat16)
+        term = jnp.dot(hidden, wd[...], preferred_element_type=jnp.float32)
+        total = term if total is None else total + term
+    scaled = (total * scale).astype(jnp.bfloat16)
+    start = 0
+    for count, out in zip(counts, outs):
+        out[...] = scaled[start : start + count]
+        start += count
+
+
+def run_expert(blocks, select, weights):
+    counts = tuple(b.shape[0] for b in blocks)
+    width = weights[0].shape[1]
+    units = sum(w.shape[0] for w in weights)
+    spec = pl.BlockSpec(memory_space=pltpu.VMEM)
+    return pl.pallas_call(
+        functools.partial(expert_kernel, counts),
+        out_shape=[jax.ShapeDtypeStruct((c, width), jnp.bfloat16) for c in counts],
+        in_specs=[spec] * (1 + len(blocks) + len(weights)),
+        out_specs=[spec] * len(blocks),
+        compiler_params=pltpu.CompilerParams(vmem_limit_bytes=VMEM_LIMIT),
+        cost_estimate=pl.CostEstimate(
+            flops=2 * sum(counts) * units * width,
+            bytes_accessed=2 * units * width,
+            transcendentals=sum(counts) * units // 3,
+        ),
+    )(select, *blocks, *weights)
+
+
+def dense_local(tokens, expert_ids, gate_scores, gate_proj, up_proj, down_proj):
+    n = lax.axis_size("wide")
+    head = lax.axis_index("head")
+    expert = lax.axis_index("wide")
+    tok_rows, half_width = tokens.shape
+    part = tok_rows // 2
+    swap = ((0, 1), (1, 0))
+    order = list(range(0, n, 2)) + list(range(n - 1, 0, -2))
+    ahead = [(order[i], order[(i + 1) % n]) for i in range(n)]
+    behind = [(b, a) for a, b in ahead]
+
+    def forth(v):
+        return lax.ppermute(v, "wide", ahead)
+
+    def back(v):
+        return lax.ppermute(v, "wide", behind)
+
+    mine = lax.dynamic_slice_in_dim(tokens, head * part, part, 0)
+    other = lax.dynamic_slice_in_dim(tokens, (1 - head) * part, part, 0)
+    got = lax.ppermute(other, "head", swap)
+    first = head == 0
+    named = expert_ids[:, :, None] == jnp.arange(n, dtype=jnp.int32)[None, None, :]
+    scores = jnp.sum(jnp.where(named, gate_scores[:, :, None], 0.0), axis=1)
+    scores = lax.dynamic_slice_in_dim(scores, head * part, part, 0)
+    pieces = []
+    rest = scores
+    for _ in range(PIECES):
+        piece = rest.astype(jnp.bfloat16)
+        pieces.append(piece)
+        rest = rest - piece.astype(jnp.float32)
+    pad = jnp.zeros((part, LANES - PIECES * n), jnp.bfloat16)
+    own = jnp.concatenate(
+        [jnp.where(first, mine, got), jnp.where(first, got, mine)] + pieces + [pad], axis=1
+    )
+    lane = jnp.arange(LANES, dtype=jnp.int32)
+    select = jnp.where(lane % n == expert, 1.0, 0.0).astype(jnp.float32)[None, :]
+
+    weights = []
+    for w in (gate_proj[0], up_proj[0], down_proj[0]):
+        weights += [w, lax.ppermute(w, "head", swap)]
+
+    half_round = n // 2
+    cut = part // 2
+    near = {0: own}
+    f = b = own
+    sums = {}
+    todo = [0]
+    for k in range(1, half_round):
+        f, b = forth(f), back(b)
+        near[-k], near[k] = f, b
+        done = run_expert([near[i] for i in todo], select, weights)
+        sums.update(zip(todo, done))
+        todo = [-k, k]
+    f, b = forth(f[:cut]), back(b[cut:])
+    done = run_expert([near[i] for i in todo], select, weights)
+    sums.update(zip(todo, done))
+    far = run_expert([f, b], select, weights)
+
+    f, b = forth(far[0]), back(far[1])
+    for k in range(half_round - 1, 0, -1):
+        up_sum = sums[k].astype(jnp.float32)
+        down_sum = sums[-k].astype(jnp.float32)
+        if k == half_round - 1:
+            up_sum = jnp.concatenate([up_sum[:cut] + f.astype(jnp.float32), up_sum[cut:]], axis=0)
+            down_sum = jnp.concatenate(
+                [down_sum[:cut], down_sum[cut:] + b.astype(jnp.float32)], axis=0
+            )
+        else:
+            up_sum = up_sum + f.astype(jnp.float32)
+            down_sum = down_sum + b.astype(jnp.float32)
+        f, b = forth(up_sum.astype(jnp.bfloat16)), back(down_sum.astype(jnp.bfloat16))
+    mixed = (sums[0].astype(jnp.float32) + f.astype(jnp.float32) + b.astype(jnp.float32)).astype(
+        jnp.bfloat16
+    )
+    left, right = mixed[:, :half_width], mixed[:, half_width:]
+    keep = jnp.where(first, left, right)
+    came = lax.ppermute(jnp.where(first, right, left), "head", swap)
+    return jnp.concatenate(
+        [jnp.where(first, keep, came), jnp.where(first, came, keep)], axis=0
+    )
+
+
+def local(tokens, expert_ids, gate_scores, gate_proj, up_proj, down_proj):
+    n = lax.axis_size("wide")
+    dense = expert_ids.shape[1] == n and lax.axis_size("head") == 2 and n % 2 == 0
+    if dense and tokens.shape[0] % 64 == 0 and PIECES * n <= LANES:
+        return dense_local(tokens, expert_ids, gate_scores, gate_proj, up_proj, down_proj)
+    return sparse_local(tokens, expert_ids, gate_scores, gate_proj, up_proj, down_proj)
+
+
 def solution(mesh):
     return jax.shard_map(
         local,

time: 118 us -> 69.3 us (0.59)
  blocking collectives: 32.9 us -> 0 us
  waiting for transfers between devices: 46.2 us -> 22.7 us
  Pallas kernels: 0 us -> 18.8 us
  between operations: 13.5 us -> 0.22 us
  starting transfers between devices: 5.84 us -> 18.7 us
  matrix products: 8.06 us -> 0 us
  other arithmetic: 6.06 us -> 2.53 us
    all_to_all x1 -> x0, blocking collectives: 32.9 us -> none  [local(): lax.all_to_all(outgoing, 'wide', split_axis=0, concat_axis=0, tiled=True)]
    all_to_all x1 -> x0, waiting for transfers between devices: 25.5 us -> none  [local(): lax.all_to_all(back.astype(jnp.bfloat16), 'wide', split_axis=0, concat_ax...]
    ppermute x0 -> x21, waiting for transfers between devices: none -> 22.7 us  [the longest x8 17.6 us: forth(): return lax.ppermute(v, 'wide', ahead)]
    pallas_call x0 -> x5, Pallas kernels: none -> 18.8 us  [run_expert(): pl.pallas_call(functools.partial(expert_kernel, counts), out_shape=[jax.S...]
    ppermute x0 -> x21, starting transfers between devices: none -> 18.7 us  [the longest x8 15.1 us: forth(): return lax.ppermute(v, 'wide', ahead)]
    reduce_scatter x1 -> x0, waiting for transfers between devices: 10.9 us -> none  [local(): lax.psum_scatter(partial_value.astype(jnp.bfloat16), 'head', scatter_dime...]
    all_gather x1 -> x0, waiting for transfers between devices: 9.71 us -> none  [local(): lax.all_gather(lax.all_to_all(outgoing, 'wide', split_axis=0, concat_axis...]
    dot_general x4 -> x0, matrix products: 8.06 us -> none  [the longest x1 3.08 us: local(): lax.dot_general(stacked, w_gate, (((1,), (1,)), ((), ())), preferred_elem...]
  transfers between devices with their start and end apart: 3 -> 21, of which waited for: 3 -> 10; matrix products, arithmetic and copies ran while one was open for 1% -> 4% of each run, Pallas kernels for 0% -> 22%
where the time goes in v1:
time: 69.3 us; the launch traced here: 68.9 us
  waiting for transfers between devices  22.7 us (33%)
  Pallas kernels  18.8 us (27%)
  starting transfers between devices  18.7 us (27%)
  local copies, waits for them, and re-layouts  5.87 us (8%)
  other arithmetic  2.53 us (4%)
    pallas_call x5, Pallas kernels, run_expert(): pl.pallas_call(functools.partial(expert_kernel, counts), out_shape=[jax.S...  18.8 us
    ppermute x8, waiting for transfers between devices, forth(): return lax.ppermute(v, 'wide', ahead)  17.6 us
    ppermute x8, starting transfers between devices, forth(): return lax.ppermute(v, 'wide', ahead)  15.1 us
    unnamed x17, local copies, waits for them, and re-layouts  4.83 us
    ppermute x8, waiting for transfers between devices, back(): return lax.ppermute(v, 'wide', behind)  3 us
    ppermute x8, starting transfers between devices, back(): return lax.ppermute(v, 'wide', behind)  2.56 us
  transfers between devices with their start and end apart: 21, of which 10 were waited for; matrix products, arithmetic and copies ran while one was open for 4% of the time, Pallas kernels for 22%

profile of v1, /device:TPU:0, one launch (start us, length us, event | category | flops | bytes accessed | tf_op | source)
XLA Modules:
  0.0 68.9 jit_solution(10015734680914426668)
XLA Ops:
  0.0 0.5 collective-permute-start.1
  0.5 0.1 collective-permute-start.2
  0.5 0.5 collective-permute-start.3
  1.0 0.8 %constant_dynamic-slice_fusion.1 = bf16[32,1024]{1,0:T(8,128)(2,1)S(1)} fusion(bf16[64,1024]{1,0:T(8,128)(2,1)} %param.6, s32[]{:T(128)S(6)} %select_n.68), kind=kLoop, calls=%fused_computation.24 | loop fusion | bytes 131076 | tf_op jit(solution)/shard_map/dynamic_slice | solution.py:130
  1.8 0.1 collective-permute-start
  1.9 0.7 %select_reduce_fusion = f32[64,8]{0,1:T(8,128)S(1)} fusion(f32[64,8]{0,1:T(8,128)} %param.8, s32[64,8]{0,1:T(8,128)} %param.7), kind=kLoop, calls=%fused_computation.16 | loop fusion | flops 11776 | bytes 6144 | tf_op jit(solution)/shard_map/reduce_sum | solution.py:134
  2.6 0.1 constant_dynamic-slice_fusion
  2.7 0.1 copy.11
  2.8 0.8 %collective-permute-done = bf16[32,1024]{1,0:T(8,128)(2,1)S(1)} collective-permute-done((bf16[32,1024]{1,0:T(8,128)(2,1)S(1)}, bf16[32,1024]{1,0:T(8,128)(2,1)S(1)}, u32[]{:S(2)}, u32[]{:S(2)}) %collective-permute-start) | collective-permute-done | bytes 65568 | tf_op jit(solution)/shard_map/ppermute | solution.py:131
  3.6 0.9 %broadcast_select_fusion.4 = (bf16[32,1024]{1,0:T(8,128)(2,1)S(1)}, bf16[32,1024]{1,0:T(8,128)(2,1)S(1)}) fusion(bf16[32,1024]{1,0:T(8,128)(2,1)S(1)} %collective-permute-done, pred[]{:T(512)S(6)} %eq.31, bf16[64,1024]{1,0:T(8,128)(2,1)} %param.6, s32[]{:T(128)S(6)} %select_n.67), kind=kLoop, calls=%fused_computation.14 | loop fusion | flops 65536 | bytes 262149 | tf_op jit(solution)/shard_map/jit(_where)/select_n | solution.py:144
  4.5 0.1 concatenate.14.refs_0_
  4.6 3.0 %collective-permute-start.4 = (bf16[32,2176]{1,0:T(8,128)(2,1)S(1)}, bf16[32,2176]{1,0:T(8,128)(2,1)S(1)}, u32[]{:S(2)}, u32[]{:S(2)}) collective-permute-start(bf16[32,2176]{1,0:T(8,128)(2,1)S(1)} %concatenate.14.refs_0_), channel_id=1, source_target_pairs={{0,4},{4,8},{8,12},{12,14},{14,10},{10,6},{6,2},{2,0},{1,5},{5,9},... | collective-permute-start | bytes 417800 | tf_op jit(solution)/shard_map/ppermute | solution.py:124
  7.6 0.0 collective-permute-start.5
  7.6 3.9 %collective-permute-done.4.refs_0_ = bf16[32,2176]{1,0:T(8,128)(2,1)S(1)} collective-permute-done((bf16[32,2176]{1,0:T(8,128)(2,1)S(1)}, bf16[32,2176]{1,0:T(8,128)(2,1)S(1)}, u32[]{:S(2)}, u32[]{:S(2)}) %collective-permute-start.4) | collective-permute-done | bytes 139296 | tf_op jit(solution)/shard_map/ppermute | solution.py:124
  11.4 1.8 %collective-permute-start.6 = (bf16[32,2176]{1,0:T(8,128)(2,1)S(1)}, bf16[32,2176]{1,0:T(8,128)(2,1)}, u32[]{:S(2)}, u32[]{:S(2)}) collective-permute-start(bf16[32,2176]{1,0:T(8,128)(2,1)S(1)} %collective-permute-done.4.refs_0_), channel_id=1, source_target_pairs={{0,4},{4,8},{8,12},{12,14},{14,10},{10,6},{6,2},{2,0},{1,5},{5,9},... | collective-permute-start | bytes 417800 | tf_op jit(solution)/shard_map/ppermute | solution.py:124
  13.3 0.0 collective-permute-done.5.refs_1_
  13.3 0.2 collective-permute-start.7
  13.5 0.6 copy-done.6
  14.1 2.6 %collective-permute-done.6.refs_0_ = bf16[32,2176]{1,0:T(8,128)(2,1)} collective-permute-done((bf16[32,2176]{1,0:T(8,128)(2,1)S(1)}, bf16[32,2176]{1,0:T(8,128)(2,1)}, u32[]{:S(2)}, u32[]{:S(2)}) %collective-permute-start.6) | collective-permute-done | bytes 139296 | tf_op jit(solution)/shard_map/ppermute | solution.py:124
  16.8 1.7 %collective-permute-start.8 = (bf16[32,2176]{1,0:T(8,128)(2,1)}, bf16[32,2176]{1,0:T(8,128)(2,1)S(1)}, u32[]{:S(2)}, u32[]{:S(2)}) collective-permute-start(bf16[32,2176]{1,0:T(8,128)(2,1)} %collective-permute-done.6.refs_0_), channel_id=1, source_target_pairs={{0,4},{4,8},{8,12},{12,14},{14,10},{10,6},{6,2},{2,0},{1,5},{5,9},... | collective-permute-start | bytes 417800 | tf_op jit(solution)/shard_map/ppermute | solution.py:124
  18.4 0.0 collective-permute-done.7.refs_1_
  18.4 0.3 collective-permute-start.9
  18.8 3.2 %collective-permute-done.8.refs_0_ = bf16[32,2176]{1,0:T(8,128)(2,1)S(1)} collective-permute-done((bf16[32,2176]{1,0:T(8,128)(2,1)}, bf16[32,2176]{1,0:T(8,128)(2,1)S(1)}, u32[]{:S(2)}, u32[]{:S(2)}) %collective-permute-start.8) | collective-permute-done | bytes 139296 | tf_op jit(solution)/shard_map/ppermute | solution.py:124
  22.0 2.1 %collective-permute-start.10 = (bf16[16,2176]{1,0:T(8,128)(2,1)S(1)}, bf16[16,2176]{1,0:T(8,128)(2,1)S(1)}, u32[]{:S(2)}, u32[]{:S(2)}) collective-permute-start(bf16[16,2176]{1,0:T(8,128)(2,1)S(1)} %slice.42), channel_id=1, source_target_pairs={{0,4},{4,8},{8,12},{12,14},{14,10},{10,6},{6,2},{2,0},{1,5},{5,9},... | collective-permute-start | bytes 208904 | tf_op jit(solution)/shard_map/ppermute | solution.py:124
  24.1 0.0 collective-permute-done.9.refs_1_
  24.1 0.1 collective-permute-start.11
  24.2 2.2 %collective-permute-done.10.refs_0_ = bf16[16,2176]{1,0:T(8,128)(2,1)S(1)} collective-permute-done((bf16[16,2176]{1,0:T(8,128)(2,1)S(1)}, bf16[16,2176]{1,0:T(8,128)(2,1)S(1)}, u32[]{:S(2)}, u32[]{:S(2)}) %collective-permute-start.10) | collective-permute-done | bytes 69664 | tf_op jit(solution)/shard_map/ppermute | solution.py:124
  26.3 2.1 %collective-permute-done.11.refs_1_ = bf16[16,2176]{1,0:T(8,128)(2,1)S(1)} collective-permute-done((bf16[16,2176]{1,0:T(8,128)(2,1)S(1)}, bf16[16,2176]{1,0:T(8,128)(2,1)S(1)}, u32[]{:S(2)}, u32[]{:S(2)}) %collective-permute-start.11) | collective-permute-done | bytes 69664 | tf_op jit(solution)/shard_map/ppermute | solution.py:127
  28.5 0.0 collective-permute-done.1.refs_2_.refs_3_
  28.5 0.0 collective-permute-done.2.refs_4_.refs_5_
  28.5 0.0 collective-permute-done.3.refs_6_.refs_7_
  28.5 0.0 copy-start
  28.5 1.4 %copy-done = bf16[1,352,2048]{2,1,0:T(8,128)(2,1)S(1)} copy-done((bf16[1,352,2048]{2,1,0:T(8,128)(2,1)S(1)}, bf16[1,352,2048]{2,1,0:T(8,128)(2,1)}, u32[]{:S(2)}) %copy-start) | copy-done | bytes 1441816
  29.8 1.4 %copy-done.2 = bf16[1,352,2048]{2,1,0:T(8,128)(2,1)S(1)} copy-done((bf16[1,352,2048]{2,1,0:T(8,128)(2,1)S(1)}, bf16[1,352,2048]{2,1,0:T(8,128)(2,1)}, u32[]{:S(2)}) %copy-start.2) | copy-done | bytes 1441816
  31.2 1.4 %copy-done.4 = bf16[1,352,2048]{2,1,0:T(8,128)(2,1)S(1)} copy-done((bf16[1,352,2048]{2,1,0:T(8,128)(2,1)S(1)}, bf16[1,352,2048]{2,1,0:T(8,128)(2,1)}, u32[]{:S(2)}) %copy-start.4) | copy-done | bytes 1441816
  32.6 3.8 %shard_map.68 = (bf16[16,2048]{1,0:T(8,128)(2,1)S(1)}, bf16[16,2048]{1,0:T(8,128)(2,1)S(1)}) custom-call(f32[1,128]{1,0:T(1,128)S(1)} %compare_select_fusion.select_ref, bf16[16,2176]{1,0:T(8,128)(2,1)S(1)} %collective-permute-done.10.refs_0_, bf16[16,2176]{1,0:T(8,128)(2,1)S(1)} %collective-permute-done.11.refs_1_, bf16[352,2048]{1,0:T(8,128)(2,1)S(1)} %bitcast.4, ...), custom_call_target="tpu_custom_call" | custom-call | flops 276824064 | bytes 8650752 | tf_op jit(solution)/shard_map/pallas_call | solution.py:98
  36.4 1.6 %collective-permute-start.12 = (bf16[16,2048]{1,0:T(8,128)(2,1)S(1)}, bf16[16,2048]{1,0:T(8,128)(2,1)S(1)}, u32[]{:S(2)}, u32[]{:S(2)}) collective-permute-start(bf16[16,2048]{1,0:T(8,128)(2,1)S(1)} %get-tuple-element.16), channel_id=1, source_target_pairs={{0,4},{4,8},{8,12},{12,14},{14,10},{10,6},{6,2},{2,0},{1,5},{5,9},... | collective-permute-start | bytes 196616 | tf_op jit(solution)/shard_map/ppermute | solution.py:124
  38.0 0.4 collective-permute-start.16
  38.4 0.0 copy-done.1
  38.4 0.0 copy-done.3
  38.5 3.7 %shard_map.67 = (bf16[32,2048]{1,0:T(8,128)(2,1)S(1)}, bf16[32,2048]{1,0:T(8,128)(2,1)S(1)}) custom-call(f32[1,128]{1,0:T(1,128)S(1)} %compare_select_fusion.select_ref, bf16[32,2176]{1,0:T(8,128)(2,1)S(1)} %collective-permute-done.8.refs_0_, bf16[32,2176]{1,0:T(8,128)(2,1)S(1)} %collective-permute-done.9.refs_1_, bf16[352,2048]{1,0:T(8,128)(2,1)S(1)} %bitcast.5, ...), custom_call_target="tpu_custom_call" | custom-call | flops 553648128 | bytes 8650752 | tf_op jit(solution)/shard_map/pallas_call | solution.py:98
  42.2 0.0 copy-start.7
  42.2 3.9 %shard_map.66 = (bf16[32,2048]{1,0:T(8,128)(2,1)S(1)}, bf16[32,2048]{1,0:T(8,128)(2,1)S(1)}) custom-call(f32[1,128]{1,0:T(1,128)S(1)} %compare_select_fusion.select_ref, bf16[32,2176]{1,0:T(8,128)(2,1)} %collective-permute-done.6.refs_0_, bf16[32,2176]{1,0:T(8,128)(2,1)} %collective-permute-done.7.refs_1_, bf16[352,2048]{1,0:T(8,128)(2,1)S(1)} %bitcast.6, ...), custom_call_target="tpu_custom_call" | custom-call | flops 553648128 | bytes 8650752 | tf_op jit(solution)/shard_map/pallas_call | solution.py:98
  46.2 0.0 copy-done.7
  46.2 3.8 %shard_map.65 = (bf16[32,2048]{1,0:T(8,128)(2,1)S(1)}, bf16[32,2048]{1,0:T(8,128)(2,1)S(1)}) custom-call(f32[1,128]{1,0:T(1,128)S(1)} %compare_select_fusion.select_ref, bf16[32,2176]{1,0:T(8,128)(2,1)S(1)} %collective-permute-done.4.refs_0_, bf16[32,2176]{1,0:T(8,128)(2,1)S(1)} %copy-done.7, bf16[352,2048]{1,0:T(8,128)(2,1)S(1)} %bitcast.7, ...), custom_call_target="tpu_custom_call" | custom-call | flops 553648128 | bytes 8650752 | tf_op jit(solution)/shard_map/pallas_call | solution.py:98
  49.9 0.0 collective-permute-done.12
  50.0 1.6 %collective-permute-start.13 = (bf16[32,2048]{1,0:T(8,128)(2,1)S(1)}, bf16[32,2048]{1,0:T(8,128)(2,1)S(1)}, u32[]{:S(2)}, u32[]{:S(2)}) collective-permute-start(bf16[32,2048]{1,0:T(8,128)(2,1)S(1)} %pad_maximum_fusion), channel_id=1, source_target_pairs={{0,4},{4,8},{8,12},{12,14},{14,10},{10,6},{6,2},{2,0},{1,5},{5,9},... | collective-permute-start | bytes 393224 | tf_op jit(solution)/shard_map/ppermute | solution.py:124
  51.6 0.0 collective-permute-done.16
  51.7 0.5 collective-permute-start.17
  52.2 2.8 %collective-permute-done.13 = bf16[32,2048]{1,0:T(8,128)(2,1)S(1)} collective-permute-done((bf16[32,2048]{1,0:T(8,128)(2,1)S(1)}, bf16[32,2048]{1,0:T(8,128)(2,1)S(1)}, u32[]{:S(2)}, u32[]{:S(2)}) %collective-permute-start.13) | collective-permute-done | bytes 131104 | tf_op jit(solution)/shard_map/ppermute | solution.py:124
  55.0 1.6 %collective-permute-start.14 = (bf16[32,2048]{1,0:T(8,128)(2,1)S(1)}, bf16[32,2048]{1,0:T(8,128)(2,1)S(1)}, u32[]{:S(2)}, u32[]{:S(2)}) collective-permute-start(bf16[32,2048]{1,0:T(8,128)(2,1)S(1)} %add_convert_fusion.4), channel_id=1, source_target_pairs={{0,4},{4,8},{8,12},{12,14},{14,10},{10,6},{6,2},{2,0},{1,5},{5,9},... | collective-permute-start | bytes 393224 | tf_op jit(solution)/shard_map/ppermute | solution.py:124
  56.7 0.0 collective-permute-done.17
  56.7 0.5 collective-permute-start.18
  57.2 2.8 %collective-permute-done.14 = bf16[32,2048]{1,0:T(8,128)(2,1)S(1)} collective-permute-done((bf16[32,2048]{1,0:T(8,128)(2,1)S(1)}, bf16[32,2048]{1,0:T(8,128)(2,1)S(1)}, u32[]{:S(2)}, u32[]{:S(2)}) %collective-permute-start.14) | collective-permute-done | bytes 131104 | tf_op jit(solution)/shard_map/ppermute | solution.py:124
  60.1 1.6 %collective-permute-start.15 = (bf16[32,2048]{1,0:T(8,128)(2,1)S(1)}, bf16[32,2048]{1,0:T(8,128)(2,1)S(1)}, u32[]{:S(2)}, u32[]{:S(2)}) collective-permute-start(bf16[32,2048]{1,0:T(8,128)(2,1)S(1)} %add_convert_fusion.3), channel_id=1, source_target_pairs={{0,4},{4,8},{8,12},{12,14},{14,10},{10,6},{6,2},{2,0},{1,5},{5,9},... | collective-permute-start | bytes 393224 | tf_op jit(solution)/shard_map/ppermute | solution.py:124
  61.7 0.0 collective-permute-done.18
  61.8 0.5 collective-permute-start.19
  62.3 3.6 %shard_map.64 = bf16[32,2048]{1,0:T(8,128)(2,1)S(1)} custom-call(f32[1,128]{1,0:T(1,128)S(1)} %compare_select_fusion.select_ref, bf16[32,2176]{1,0:T(8,128)(2,1)S(1)} %concatenate.14.refs_0_, bf16[352,2048]{1,0:T(8,128)(2,1)S(1)} %bitcast.8, bf16[352,2048]{1,0:T(8,128)(2,1)S(1)} %collective-permute-done.1.refs_2_.refs_3_, bf16[352,2048]{1,0:T(8,128)(2,1)S(1)} %bitcast.14, ...), custom_call_target="tpu_custom_call" | custom-call | flops 276824064 | bytes 8650752 | tf_op jit(solution)/shard_map/pallas_call | solution.py:98
  65.9 0.0 collective-permute-done.15
  65.9 0.9 %collective-permute-done.19 = bf16[32,2048]{1,0:T(8,128)(2,1)S(1)} collective-permute-done((bf16[32,2048]{1,0:T(8,128)(2,1)S(1)}, bf16[32,2048]{1,0:T(8,128)(2,1)S(1)}, u32[]{:S(2)}, u32[]{:S(2)}) %collective-permute-start.19) | collective-permute-done | bytes 131104 | tf_op jit(solution)/shard_map/ppermute | solution.py:127
  66.8 0.1 add_convert_fusion
  66.9 0.1 collective-permute-start.20
  66.9 1.2 %collective-permute-done.20 = bf16[32,1024]{1,0:T(8,128)(2,1)S(1)} collective-permute-done((bf16[32,1024]{1,0:T(8,128)(2,1)S(1)}, bf16[32,1024]{1,0:T(8,128)(2,1)S(1)}, u32[]{:S(2)}, u32[]{:S(2)}) %collective-permute-start.20) | collective-permute-done | bytes 65568 | tf_op jit(solution)/shard_map/ppermute | solution.py:188
  68.2 0.7 pad_maximum_fusion.2
  (24 shorter events, 0.3 us)
Async XLA Ops:
  0.0 28.5 %collective-permute-start.1 = (bf16[352,2048]{1,0:T(8,128)(2,1)}, bf16[352,2048]{1,0:T(8,128)(2,1)S(1)}, u32[]{:S(2)}, u32[]{:S(2)}) collective-permute-start(bf16[352,2048]{1,0:T(8,128)(2,1)} %bitcast.3), channel_id=1, source_target_pairs={{0,1},{1,0},{2,3},{3,2},{4,5},{5,4},{6,7},{7,6},{8,9},{9,8},{10,11... | collective-permute-start | bytes 4325384 | tf_op jit(solution)/shard_map/ppermute | solution.py:151
  0.5 28.0 %collective-permute-start.2 = (bf16[352,2048]{1,0:T(8,128)(2,1)}, bf16[352,2048]{1,0:T(8,128)(2,1)S(1)}, u32[]{:S(2)}, u32[]{:S(2)}) collective-permute-start(bf16[352,2048]{1,0:T(8,128)(2,1)} %bitcast.9), channel_id=1, source_target_pairs={{0,1},{1,0},{2,3},{3,2},{4,5},{5,4},{6,7},{7,6},{8,9},{9,8},{10,11... | collective-permute-start | bytes 4325384 | tf_op jit(solution)/shard_map/ppermute | solution.py:151
  0.5 28.0 %collective-permute-start.3 = (bf16[352,2048]{1,0:T(8,128)(2,1)}, bf16[352,2048]{1,0:T(8,128)(2,1)}, u32[]{:S(2)}, u32[]{:S(2)}) collective-permute-start(bf16[352,2048]{1,0:T(8,128)(2,1)} %bitcast.15), channel_id=1, source_target_pairs={{0,1},{1,0},{2,3},{3,2},{4,5},{5,4},{6,7},{7,6},{8,9},{9,8},{10,11... | collective-permute-start | bytes 4325384 | tf_op jit(solution)/shard_map/ppermute | solution.py:151
  1.8 1.8 %collective-permute-start = (bf16[32,1024]{1,0:T(8,128)(2,1)S(1)}, bf16[32,1024]{1,0:T(8,128)(2,1)S(1)}, u32[]{:S(2)}, u32[]{:S(2)}) collective-permute-start(bf16[32,1024]{1,0:T(8,128)(2,1)S(1)} %constant_dynamic-slice_fusion.1), channel_id=1, source_target_pairs={{0,1},{1,0},{2,3},{3,2},{4,5},{5,4},{6,7},{7,6},{8,9},{9,8},{10,11... | collective-permute-start | bytes 196616 | tf_op jit(solution)/shard_map/ppermute | solution.py:131
  4.6 6.9 %collective-permute-start.4 = (bf16[32,2176]{1,0:T(8,128)(2,1)S(1)}, bf16[32,2176]{1,0:T(8,128)(2,1)S(1)}, u32[]{:S(2)}, u32[]{:S(2)}) collective-permute-start(bf16[32,2176]{1,0:T(8,128)(2,1)S(1)} %concatenate.14.refs_0_), channel_id=1, source_target_pairs={{0,4},{4,8},{8,12},{12,14},{14,10},{10,6},{6,2},{2,0},{1,5},{5,9},... | collective-permute-start | bytes 417800 | tf_op jit(solution)/shard_map/ppermute | solution.py:124
  7.6 5.7 %collective-permute-start.5 = (bf16[32,2176]{1,0:T(8,128)(2,1)S(1)}, bf16[32,2176]{1,0:T(8,128)(2,1)S(1)}, u32[]{:S(2)}, u32[]{:S(2)}) collective-permute-start(bf16[32,2176]{1,0:T(8,128)(2,1)S(1)} %concatenate.14.refs_0_), channel_id=1, source_target_pairs={{4,0},{8,4},{12,8},{14,12},{10,14},{6,10},{2,6},{0,2},{5,1},{9,5},... | collective-permute-start | bytes 417800 | tf_op jit(solution)/shard_map/ppermute | solution.py:127
  11.4 5.3 %collective-permute-start.6 = (bf16[32,2176]{1,0:T(8,128)(2,1)S(1)}, bf16[32,2176]{1,0:T(8,128)(2,1)}, u32[]{:S(2)}, u32[]{:S(2)}) collective-permute-start(bf16[32,2176]{1,0:T(8,128)(2,1)S(1)} %collective-permute-done.4.refs_0_), channel_id=1, source_target_pairs={{0,4},{4,8},{8,12},{12,14},{14,10},{10,6},{6,2},{2,0},{1,5},{5,9},... | collective-permute-start | bytes 417800 | tf_op jit(solution)/shard_map/ppermute | solution.py:124
  13.3 5.2 %collective-permute-start.7 = (bf16[32,2176]{1,0:T(8,128)(2,1)S(1)}, bf16[32,2176]{1,0:T(8,128)(2,1)}, u32[]{:S(2)}, u32[]{:S(2)}) collective-permute-start(bf16[32,2176]{1,0:T(8,128)(2,1)S(1)} %collective-permute-done.5.refs_1_), channel_id=1, source_target_pairs={{4,0},{8,4},{12,8},{14,12},{10,14},{6,10},{2,6},{0,2},{5,1},{9,5},... | collective-permute-start | bytes 417800 | tf_op jit(solution)/shard_map/ppermute | solution.py:127
  13.5 0.7 copy-start.6
  16.8 5.3 %collective-permute-start.8 = (bf16[32,2176]{1,0:T(8,128)(2,1)}, bf16[32,2176]{1,0:T(8,128)(2,1)S(1)}, u32[]{:S(2)}, u32[]{:S(2)}) collective-permute-start(bf16[32,2176]{1,0:T(8,128)(2,1)} %collective-permute-done.6.refs_0_), channel_id=1, source_target_pairs={{0,4},{4,8},{8,12},{12,14},{14,10},{10,6},{6,2},{2,0},{1,5},{5,9},... | collective-permute-start | bytes 417800 | tf_op jit(solution)/shard_map/ppermute | solution.py:124
  18.4 5.7 %collective-permute-start.9 = (bf16[32,2176]{1,0:T(8,128)(2,1)}, bf16[32,2176]{1,0:T(8,128)(2,1)S(1)}, u32[]{:S(2)}, u32[]{:S(2)}) collective-permute-start(bf16[32,2176]{1,0:T(8,128)(2,1)} %collective-permute-done.7.refs_1_), channel_id=1, source_target_pairs={{4,0},{8,4},{12,8},{14,12},{10,14},{6,10},{2,6},{0,2},{5,1},{9,5},... | collective-permute-start | bytes 417800 | tf_op jit(solution)/shard_map/ppermute | solution.py:127
  22.0 4.3 %collective-permute-start.10 = (bf16[16,2176]{1,0:T(8,128)(2,1)S(1)}, bf16[16,2176]{1,0:T(8,128)(2,1)S(1)}, u32[]{:S(2)}, u32[]{:S(2)}) collective-permute-start(bf16[16,2176]{1,0:T(8,128)(2,1)S(1)} %slice.42), channel_id=1, source_target_pairs={{0,4},{4,8},{8,12},{12,14},{14,10},{10,6},{6,2},{2,0},{1,5},{5,9},... | collective-permute-start | bytes 208904 | tf_op jit(solution)/shard_map/ppermute | solution.py:124
  24.1 4.4 %collective-permute-start.11 = (bf16[16,2176]{1,0:T(8,128)(2,1)S(1)}, bf16[16,2176]{1,0:T(8,128)(2,1)S(1)}, u32[]{:S(2)}, u32[]{:S(2)}) collective-permute-start(bf16[16,2176]{1,0:T(8,128)(2,1)S(1)} %slice.43), channel_id=1, source_target_pairs={{4,0},{8,4},{12,8},{14,12},{10,14},{6,10},{2,6},{0,2},{5,1},{9,5},... | collective-permute-start | bytes 208904 | tf_op jit(solution)/shard_map/ppermute | solution.py:127
  28.5 1.4 %copy-start = (bf16[1,352,2048]{2,1,0:T(8,128)(2,1)S(1)}, bf16[1,352,2048]{2,1,0:T(8,128)(2,1)}, u32[]{:S(2)}) copy-start(bf16[1,352,2048]{2,1,0:T(8,128)(2,1)} %param.9) | copy-start | bytes 4325380
  29.8 1.4 %copy-start.2 = (bf16[1,352,2048]{2,1,0:T(8,128)(2,1)S(1)}, bf16[1,352,2048]{2,1,0:T(8,128)(2,1)}, u32[]{:S(2)}) copy-start(bf16[1,352,2048]{2,1,0:T(8,128)(2,1)} %param.10) | copy-start | bytes 4325380
  31.2 1.4 %copy-start.4 = (bf16[1,352,2048]{2,1,0:T(8,128)(2,1)S(1)}, bf16[1,352,2048]{2,1,0:T(8,128)(2,1)}, u32[]{:S(2)}) copy-start(bf16[1,352,2048]{2,1,0:T(8,128)(2,1)} %param.11) | copy-start | bytes 4325380
  32.6 5.9 %copy-start.1 = (bf16[1,352,2048]{2,1,0:T(8,128)(2,1)S(1)}, bf16[1,352,2048]{2,1,0:T(8,128)(2,1)}, u32[]{:S(2)}) copy-start(bf16[1,352,2048]{2,1,0:T(8,128)(2,1)} %param.9) | copy-start | bytes 4325380
  32.6 5.9 %copy-start.3 = (bf16[1,352,2048]{2,1,0:T(8,128)(2,1)S(1)}, bf16[1,352,2048]{2,1,0:T(8,128)(2,1)}, u32[]{:S(2)}) copy-start(bf16[1,352,2048]{2,1,0:T(8,128)(2,1)} %param.10) | copy-start | bytes 4325380
  32.6 5.9 %copy-start.5 = (bf16[1,352,2048]{2,1,0:T(8,128)(2,1)S(1)}, bf16[1,352,2048]{2,1,0:T(8,128)(2,1)}, u32[]{:S(2)}) copy-start(bf16[1,352,2048]{2,1,0:T(8,128)(2,1)} %param.11) | copy-start | bytes 4325380
  36.4 13.6 %collective-permute-start.12 = (bf16[16,2048]{1,0:T(8,128)(2,1)S(1)}, bf16[16,2048]{1,0:T(8,128)(2,1)S(1)}, u32[]{:S(2)}, u32[]{:S(2)}) collective-permute-start(bf16[16,2048]{1,0:T(8,128)(2,1)S(1)} %get-tuple-element.16), channel_id=1, source_target_pairs={{0,4},{4,8},{8,12},{12,14},{14,10},{10,6},{6,2},{2,0},{1,5},{5,9},... | collective-permute-start | bytes 196616 | tf_op jit(solution)/shard_map/ppermute | solution.py:124
  38.0 13.6 %collective-permute-start.16 = (bf16[16,2048]{1,0:T(8,128)(2,1)S(1)}, bf16[16,2048]{1,0:T(8,128)(2,1)S(1)}, u32[]{:S(2)}, u32[]{:S(2)}) collective-permute-start(bf16[16,2048]{1,0:T(8,128)(2,1)S(1)} %get-tuple-element.20), channel_id=1, source_target_pairs={{4,0},{8,4},{12,8},{14,12},{10,14},{6,10},{2,6},{0,2},{5,1},{9,5},... | collective-permute-start | bytes 196616 | tf_op jit(solution)/shard_map/ppermute | solution.py:127
  42.2 4.0 %copy-start.7 = (bf16[32,2176]{1,0:T(8,128)(2,1)S(1)}, bf16[32,2176]{1,0:T(8,128)(2,1)}, u32[]{:S(2)}) copy-start(bf16[32,2176]{1,0:T(8,128)(2,1)} %copy-done.6) | copy-start | bytes 417796
  50.0 5.0 %collective-permute-start.13 = (bf16[32,2048]{1,0:T(8,128)(2,1)S(1)}, bf16[32,2048]{1,0:T(8,128)(2,1)S(1)}, u32[]{:S(2)}, u32[]{:S(2)}) collective-permute-start(bf16[32,2048]{1,0:T(8,128)(2,1)S(1)} %pad_maximum_fusion), channel_id=1, source_target_pairs={{0,4},{4,8},{8,12},{12,14},{14,10},{10,6},{6,2},{2,0},{1,5},{5,9},... | collective-permute-start | bytes 393224 | tf_op jit(solution)/shard_map/ppermute | solution.py:124
  51.7 5.0 %collective-permute-start.17 = (bf16[32,2048]{1,0:T(8,128)(2,1)S(1)}, bf16[32,2048]{1,0:T(8,128)(2,1)S(1)}, u32[]{:S(2)}, u32[]{:S(2)}) collective-permute-start(bf16[32,2048]{1,0:T(8,128)(2,1)S(1)} %pad_maximum_fusion.1), channel_id=1, source_target_pairs={{4,0},{8,4},{12,8},{14,12},{10,14},{6,10},{2,6},{0,2},{5,1},{9,5},... | collective-permute-start | bytes 393224 | tf_op jit(solution)/shard_map/ppermute | solution.py:127
  55.0 5.0 %collective-permute-start.14 = (bf16[32,2048]{1,0:T(8,128)(2,1)S(1)}, bf16[32,2048]{1,0:T(8,128)(2,1)S(1)}, u32[]{:S(2)}, u32[]{:S(2)}) collective-permute-start(bf16[32,2048]{1,0:T(8,128)(2,1)S(1)} %add_convert_fusion.4), channel_id=1, source_target_pairs={{0,4},{4,8},{8,12},{12,14},{14,10},{10,6},{6,2},{2,0},{1,5},{5,9},... | collective-permute-start | bytes 393224 | tf_op jit(solution)/shard_map/ppermute | solution.py:124
  56.7 5.0 %collective-permute-start.18 = (bf16[32,2048]{1,0:T(8,128)(2,1)S(1)}, bf16[32,2048]{1,0:T(8,128)(2,1)S(1)}, u32[]{:S(2)}, u32[]{:S(2)}) collective-permute-start(bf16[32,2048]{1,0:T(8,128)(2,1)S(1)} %add_convert_fusion.2), channel_id=1, source_target_pairs={{4,0},{8,4},{12,8},{14,12},{10,14},{6,10},{2,6},{0,2},{5,1},{9,5},... | collective-permute-start | bytes 393224 | tf_op jit(solution)/shard_map/ppermute | solution.py:127
  60.1 5.8 %collective-permute-start.15 = (bf16[32,2048]{1,0:T(8,128)(2,1)S(1)}, bf16[32,2048]{1,0:T(8,128)(2,1)S(1)}, u32[]{:S(2)}, u32[]{:S(2)}) collective-permute-start(bf16[32,2048]{1,0:T(8,128)(2,1)S(1)} %add_convert_fusion.3), channel_id=1, source_target_pairs={{0,4},{4,8},{8,12},{12,14},{14,10},{10,6},{6,2},{2,0},{1,5},{5,9},... | collective-permute-start | bytes 393224 | tf_op jit(solution)/shard_map/ppermute | solution.py:124
  61.8 5.0 %collective-permute-start.19 = (bf16[32,2048]{1,0:T(8,128)(2,1)S(1)}, bf16[32,2048]{1,0:T(8,128)(2,1)S(1)}, u32[]{:S(2)}, u32[]{:S(2)}) collective-permute-start(bf16[32,2048]{1,0:T(8,128)(2,1)S(1)} %add_convert_fusion.1), channel_id=1, source_target_pairs={{4,0},{8,4},{12,8},{14,12},{10,14},{6,10},{2,6},{0,2},{5,1},{9,5},... | collective-permute-start | bytes 393224 | tf_op jit(solution)/shard_map/ppermute | solution.py:127
  66.9 1.3 %collective-permute-start.20 = (bf16[32,1024]{1,0:T(8,128)(2,1)S(1)}, bf16[32,1024]{1,0:T(8,128)(2,1)S(1)}, u32[]{:S(2)}, u32[]{:S(2)}) collective-permute-start(bf16[32,1024]{1,0:T(8,128)(2,1)S(1)} %broadcast_select_fusion.2), channel_id=1, source_target_pairs={{0,1},{1,0},{2,3},{3,2},{4,5},{5,4},{6,7},{7,6},{8,9},{9,8},{10,11... | collective-permute-start | bytes 196616 | tf_op jit(solution)/shard_map/ppermute | solution.py:188

commit v2 on v1

--- a/solution.py
+++ b/solution.py
@@ -72,17 +72,14 @@
     rows = whole[0] if len(whole) == 1 else jnp.concatenate(whole, axis=0)
     x = rows[:, :width]
     scale = jnp.sum(rows[:, width:].astype(jnp.float32) * select_ref[...], axis=1, keepdims=True)
-    total = None
-    for wg, wu, wd in ((wg0, wu0, wd0), (wg1, wu1, wd1)):
-        gate = lax.dot_general(
-            x, wg[...], (((1,), (1,)), ((), ())), preferred_element_type=jnp.float32
-        )
-        up = lax.dot_general(
-            x, wu[...], (((1,), (1,)), ((), ())), preferred_element_type=jnp.float32
-        )
-        hidden = (gate / (1.0 + jnp.exp(-gate)) * up).astype(jnp.bfloat16)
-        term = jnp.dot(hidden, wd[...], preferred_element_type=jnp.float32)
-        total = term if total is None else total + term
+    w_gate = jnp.concatenate([wg0[...], wg1[...]], axis=0)
+    w_up = jnp.concatenate([wu0[...], wu1[...]], axis=0)
+    w_down = jnp.concatenate([wd0[...], wd1[...]], axis=0)
+    contract = (((1,), (1,)), ((), ()))
+    gate = lax.dot_general(x, w_gate, contract, preferred_element_type=jnp.float32)
+    up = lax.dot_general(x, w_up, contract, preferred_element_type=jnp.float32)
+    hidden = (gate / (1.0 + jnp.exp(-gate)) * up).astype(jnp.bfloat16)
+    total = jnp.dot(hidden, w_down, preferred_element_type=jnp.float32)
     scaled = (total * scale).astype(jnp.bfloat16)
     start = 0
     for count, out in zip(counts, outs):
@@ -107,6 +104,92 @@
             transcendentals=sum(counts) * units // 3,
         ),
     )(select, *blocks, *weights)
+
+
+def spread_kernel(n, head_ref, tokens_ref, ids_ref, scores_ref, mine_ref, lanes_ref):
+    part = mine_ref.shape[0]
+    first = head_ref[0] == 0
+    mine_ref[...] = jnp.where(first, tokens_ref[:part], tokens_ref[part:])
+    ids = jnp.where(first, ids_ref[:part], ids_ref[part:])
+    scores = jnp.where(first, scores_ref[:part], scores_ref[part:])
+    lane = lax.broadcasted_iota(jnp.int32, (part, LANES), 1)
+    expert = lane % n
+    dense = jnp.zeros((part, LANES), jnp.float32)
+    for k in range(ids.shape[1]):
+        dense = dense + jnp.where(expert == ids[:, k : k + 1], scores[:, k : k + 1], 0.0)
+    packed = jnp.zeros((part, LANES), jnp.float32)
+    for p in range(PIECES):
+        piece = dense.astype(jnp.bfloat16).astype(jnp.float32)
+        packed = jnp.where((lane >= p * n) & (lane < (p + 1) * n), piece, packed)
+        dense = dense - piece
+    lanes_ref[...] = packed.astype(jnp.bfloat16)
+
+
+def spread(head, tokens, expert_ids, gate_scores):
+    rows, half_width = tokens.shape
+    spec = pl.BlockSpec(memory_space=pltpu.VMEM)
+    return pl.pallas_call(
+        functools.partial(spread_kernel, lax.axis_size("wide")),
+        out_shape=[
+            jax.ShapeDtypeStruct((rows // 2, half_width), jnp.bfloat16),
+            jax.ShapeDtypeStruct((rows // 2, LANES), jnp.bfloat16),
+        ],
+        in_specs=[pl.BlockSpec(memory_space=pltpu.SMEM)] + [spec] * 3,
+        out_specs=[spec] * 2,
+        compiler_params=pltpu.CompilerParams(vmem_limit_bytes=VMEM_LIMIT),
+        cost_estimate=pl.CostEstimate(
+            flops=0, bytes_accessed=3 * rows * half_width, transcendentals=0
+        ),
+    )(head.reshape(1), tokens, expert_ids, gate_scores)
+
+
+def join_kernel(head_ref, mine_ref, got_ref, lanes_ref, out_ref):
+    part, half_width = mine_ref.shape
+    first = head_ref[0] == 0
+    mine = mine_ref[...]
+    out_ref[:, :half_width] = jnp.where(first, mine, got_ref[part:])
+    out_ref[:, half_width : 2 * half_width] = jnp.where(first, got_ref[:part], mine)
+    out_ref[:, 2 * half_width :] = lanes_ref[...]
+
+
+def join(head, mine, got, lanes):
+    part, half_width = mine.shape
+    spec = pl.BlockSpec(memory_space=pltpu.VMEM)
+    return pl.pallas_call(
+        join_kernel,
+        out_shape=jax.ShapeDtypeStruct((part, 2 * half_width + LANES), jnp.bfloat16),
+        in_specs=[pl.BlockSpec(memory_space=pltpu.SMEM)] + [spec] * 3,
+        out_specs=spec,
+        compiler_params=pltpu.CompilerParams(vmem_limit_bytes=VMEM_LIMIT),
+        cost_estimate=pl.CostEstimate(
+            flops=0, bytes_accessed=8 * part * half_width, transcendentals=0
+        ),
+    )(head.reshape(1), mine, got, lanes)
+
+
+def fetch_kernel(count, *refs):
+    copies = [
+        pltpu.make_async_copy(refs[i], refs[count + i], refs[2 * count].at[i]) for i in range(count)
+    ]
+    for copy in copies:
+        copy.start()
+    for copy in copies:
+        copy.wait()
+
+
+def fetch(arrays):
+    count = len(arrays)
+    return pl.pallas_call(
+        functools.partial(fetch_kernel, count),
+        out_shape=[jax.ShapeDtypeStruct(a.shape, a.dtype) for a in arrays],
+        in_specs=[pl.BlockSpec(memory_space=pltpu.HBM)] * count,
+        out_specs=[pl.BlockSpec(memory_space=pltpu.VMEM)] * count,
+        scratch_shapes=[pltpu.SemaphoreType.DMA((count,))],
+        compiler_params=pltpu.CompilerParams(vmem_limit_bytes=VMEM_LIMIT),
+        cost_estimate=pl.CostEstimate(
+            flops=0, bytes_accessed=4 * sum(a.size for a in arrays), transcendentals=0
+        ),
+    )(*arrays)
 
 
 def dense_local(tokens, expert_ids, gate_scores, gate_proj, up_proj, down_proj):
@@ -126,52 +209,44 @@
     def back(v):
         return lax.ppermute(v, "wide", behind)
 
-    mine = lax.dynamic_slice_in_dim(tokens, head * part, part, 0)
-    other = lax.dynamic_slice_in_dim(tokens, (1 - head) * part, part, 0)
-    got = lax.ppermute(other, "head", swap)
     first = head == 0
-    named = expert_ids[:, :, None] == jnp.arange(n, dtype=jnp.int32)[None, None, :]
-    scores = jnp.sum(jnp.where(named, gate_scores[:, :, None], 0.0), axis=1)
-    scores = lax.dynamic_slice_in_dim(scores, head * part, part, 0)
-    pieces = []
-    rest = scores
-    for _ in range(PIECES):
-        piece = rest.astype(jnp.bfloat16)
-        pieces.append(piece)
-        rest = rest - piece.astype(jnp.float32)
-    pad = jnp.zeros((part, LANES - PIECES * n), jnp.bfloat16)
-    own = jnp.concatenate(
-        [jnp.where(first, mine, got), jnp.where(first, got, mine)] + pieces + [pad], axis=1
-    )
+    got = lax.ppermute(tokens, "head", swap)
+    mine, lanes = spread(head, tokens, expert_ids, gate_scores)
+    own = join(head, mine, got, lanes)
     lane = jnp.arange(LANES, dtype=jnp.int32)
     select = jnp.where(lane % n == expert, 1.0, 0.0).astype(jnp.float32)[None, :]
 
-    weights = []
-    for w in (gate_proj[0], up_proj[0], down_proj[0]):
-        weights += [w, lax.ppermute(w, "head", swap)]
-
-    half_round = n // 2
+    own, *held = lax.optimization_barrier((own, gate_proj[0], up_proj[0], down_proj[0]))
+    came = [lax.ppermute(w, "head", swap) for w in held]
+    kept = fetch(held)
+
+    reach = n // 2
     cut = part // 2
     near = {0: own}
     f = b = own
     sums = {}
-    todo = [0]
-    for k in range(1, half_round):
+    for k in range(1, reach):
         f, b = forth(f), back(b)
+        if k == 1:
+            f, b, *kept = lax.optimization_barrier((f, b, *kept))
         near[-k], near[k] = f, b
-        done = run_expert([near[i] for i in todo], select, weights)
-        sums.update(zip(todo, done))
-        todo = [-k, k]
+    weights = [w for pair in zip(kept, came) for w in pair]
+    keys = sorted(i for i in near if abs(i) < reach - 1)
+    done = run_expert([near[i] for i in keys], select, weights)
+    f, b, *done = lax.optimization_barrier((f, b, *done))
+    sums.update(zip(keys, done))
+    keys = [1 - reach, reach - 1]
+    done = run_expert([f, b], select, weights)
     f, b = forth(f[:cut]), back(b[cut:])
-    done = run_expert([near[i] for i in todo], select, weights)
-    sums.update(zip(todo, done))
+    f, b, *done = lax.optimization_barrier((f, b, *done))
+    sums.update(zip(keys, done))
     far = run_expert([f, b], select, weights)
 
     f, b = forth(far[0]), back(far[1])
-    for k in range(half_round - 1, 0, -1):
+    for k in range(reach - 1, 0, -1):
         up_sum = sums[k].astype(jnp.float32)
         down_sum = sums[-k].astype(jnp.float32)
-        if k == half_round - 1:
+        if k == reach - 1:
             up_sum = jnp.concatenate([up_sum[:cut] + f.astype(jnp.float32), up_sum[cut:]], axis=0)
             down_sum = jnp.concatenate(
                 [down_sum[:cut], down_sum[cut:] + b.astype(jnp.float32)], axis=0
@@ -185,9 +260,9 @@
     )
     left, right = mixed[:, :half_width], mixed[:, half_width:]
     keep = jnp.where(first, left, right)
-    came = lax.ppermute(jnp.where(first, right, left), "head", swap)
+    rest = lax.ppermute(jnp.where(first, right, left), "head", swap)
     return jnp.concatenate(
-        [jnp.where(first, keep, came), jnp.where(first, came, keep)], axis=0
+        [jnp.where(first, keep, rest), jnp.where(first, rest, keep)], axis=0
     )
 
 

time: 69.3 us -> 65.8 us (0.949)
  local copies, waits for them, and re-layouts: 5.87 us -> 14 us
  Pallas kernels: 18.8 us -> 12.3 us
  waiting for transfers between devices: 22.7 us -> 18.9 us
  other arithmetic: 2.53 us -> 0.95 us
    unnamed x17 -> x32, local copies, waits for them, and re-layouts: 4.83 us -> 13.9 us
    pallas_call x5 -> x3, Pallas kernels: 18.8 us -> 11.4 us  [run_expert(): pl.pallas_call(functools.partial(expert_kernel, counts), out_shape=[jax.S...]
    ppermute x8, waiting for transfers between devices: 3 us -> 1.52 us  [back(): return lax.ppermute(v, 'wide', behind)]
    ppermute x8, waiting for transfers between devices: 17.6 us -> 16.1 us  [forth(): return lax.ppermute(v, 'wide', ahead)]
    pallas_call x0 -> x3, Pallas kernels: none -> 0.98 us  [the longest x1 0.8 us: fetch(): pl.pallas_call(functools.partial(fetch_kernel, count), out_shape=[jax.Sha...]
    dynamic_slice x2 -> x0, local copies, waits for them, and re-layouts: 0.92 us -> none  [the longest x1 0.84 us: dense_local(): other = lax.dynamic_slice_in_dim(tokens, (1 - head) * part, part, 0)]
    select_n x3 -> x2, other arithmetic: 0.89 us -> 0.03 us  [the longest x1 0.01 us: dense_local(): jnp.where(first, keep, rest)]
    ppermute x5, waiting for transfers between devices: 2.08 us -> 1.25 us  [the longest x1 1.24 us: dense_local(): rest = lax.ppermute(jnp.where(first, right, left), 'head', swap)]
  transfers between devices with their start and end apart: 21 -> 21, of which waited for: 10 -> 9; matrix products, arithmetic and copies ran while one was open for 4% -> 3% of each run, Pallas kernels for 22% -> 13%
where the time goes in v2:
time: 65.8 us; the launch traced here: 65.4 us
  starting transfers between devices  19 us (29%)
  waiting for transfers between devices  18.9 us (29%)
  local copies, waits for them, and re-layouts  14 us (21%)
  Pallas kernels  12.3 us (19%)
  other arithmetic  0.95 us (1%)
    ppermute x8, waiting for transfers between devices, forth(): return lax.ppermute(v, 'wide', ahead)  16.1 us
    ppermute x8, starting transfers between devices, forth(): return lax.ppermute(v, 'wide', ahead)  14.4 us
    unnamed x32, local copies, waits for them, and re-layouts  13.9 us
    pallas_call x3, Pallas kernels, run_expert(): pl.pallas_call(functools.partial(expert_kernel, counts), out_shape=[jax.S...  11.4 us
    ppermute x8, starting transfers between devices, back(): return lax.ppermute(v, 'wide', behind)  3.36 us
    ppermute x8, waiting for transfers between devices, back(): return lax.ppermute(v, 'wide', behind)  1.52 us
  transfers between devices with their start and end apart: 21, of which 9 were waited for; matrix products, arithmetic and copies ran while one was open for 3% of the time, Pallas kernels for 13%

profile of v2, /device:TPU:0, one launch (start us, length us, event | category | flops | bytes accessed | tf_op | source)
XLA Modules:
  0.0 65.4 jit_solution(14580353363044884891)
XLA Ops:
  0.0 0.5 collective-permute-start
  0.5 0.8 %copy.7.ids_ref = s32[64,8]{1,0:T(8,128)S(1)} copy(s32[64,8]{0,1:T(8,128)} %param.7) | data formatting | bytes 4096 | tf_op args[1]
  1.2 0.8 %copy.8.scores_ref = f32[64,8]{1,0:T(8,128)S(1)} copy(f32[64,8]{0,1:T(8,128)} %param.8) | data formatting | bytes 4096 | tf_op args[2]
  2.0 0.9 %copy-done.12 = bf16[64,1024]{1,0:T(8,128)(2,1)S(1)} copy-done((bf16[64,1024]{1,0:T(8,128)(2,1)S(1)}, bf16[64,1024]{1,0:T(8,128)(2,1)}, u32[]{:S(2)}) %copy-start.12) | copy-done | bytes 131096
  2.9 0.2 shard_map.64
  3.1 0.0 collective-permute-done.got_ref
  3.1 0.1 collective-permute-start.7
  3.2 0.5 collective-permute-start.8
  3.7 0.1 collective-permute-start.9
  3.8 3.0 %collective-permute-start.1 = (bf16[32,2176]{1,0:T(8,128)(2,1)S(1)}, bf16[32,2176]{1,0:T(8,128)(2,1)S(1)}, u32[]{:S(2)}, u32[]{:S(2)}) collective-permute-start(bf16[32,2176]{1,0:T(8,128)(2,1)S(1)} %shard_map.65.refs_2_), channel_id=1, source_target_pairs={{0,4},{4,8},{8,12},{12,14},{14,10},{10,6},{6,2},{2,0},{1,5},{5,9},... | collective-permute-start | bytes 417800 | tf_op jit(solution)/shard_map/ppermute | solution.py:207
  6.8 0.0 collective-permute-start.2
  6.8 1.4 %copy-done.9 = bf16[1,352,2048]{2,1,0:T(8,128)(2,1)S(1)} copy-done((bf16[1,352,2048]{2,1,0:T(8,128)(2,1)S(1)}, bf16[1,352,2048]{2,1,0:T(8,128)(2,1)}, u32[]{:S(2)}) %copy-start.9) | copy-done | bytes 1441816
  8.1 1.4 %copy-done.10 = bf16[1,352,2048]{2,1,0:T(8,128)(2,1)S(1)} copy-done((bf16[1,352,2048]{2,1,0:T(8,128)(2,1)S(1)}, bf16[1,352,2048]{2,1,0:T(8,128)(2,1)}, u32[]{:S(2)}) %copy-start.10) | copy-done | bytes 1441816
  9.5 1.4 %copy-done.11 = bf16[1,352,2048]{2,1,0:T(8,128)(2,1)S(1)} copy-done((bf16[1,352,2048]{2,1,0:T(8,128)(2,1)S(1)}, bf16[1,352,2048]{2,1,0:T(8,128)(2,1)}, u32[]{:S(2)}) %copy-start.11) | copy-done | bytes 1441816
  10.8 0.8 %shard_map.66 = (bf16[352,2048]{1,0:T(8,128)(2,1)S(1)}, bf16[352,2048]{1,0:T(8,128)(2,1)S(1)}, bf16[352,2048]{1,0:T(8,128)(2,1)S(1)}) custom-call(bf16[352,2048]{1,0:T(8,128)(2,1)S(1)} %bitcast.5, bf16[352,2048]{1,0:T(8,128)(2,1)S(1)} %bitcast.7, bf16[352,2048]{1,0:T(8,128)(2,1)S(1)} %bitcast.9), custom_call_target="tpu_custom_call" | custom-call | bytes 8650752 | tf_op jit(solution)/shard_map/pallas_call | solution.py:182
  11.7 1.1 %copy-done = bf16[352,2048]{1,0:T(8,128)(2,1)} copy-done((bf16[352,2048]{1,0:T(8,128)(2,1)}, bf16[352,2048]{1,0:T(8,128)(2,1)S(1)}, u32[]{:S(2)}) %copy-start) | copy-done | bytes 1441816
  12.8 1.1 %copy-done.3 = bf16[352,2048]{1,0:T(8,128)(2,1)} copy-done((bf16[352,2048]{1,0:T(8,128)(2,1)}, bf16[352,2048]{1,0:T(8,128)(2,1)S(1)}, u32[]{:S(2)}) %copy-start.3) | copy-done | bytes 1441816
  13.9 1.1 %copy-done.6 = bf16[352,2048]{1,0:T(8,128)(2,1)} copy-done((bf16[352,2048]{1,0:T(8,128)(2,1)}, bf16[352,2048]{1,0:T(8,128)(2,1)S(1)}, u32[]{:S(2)}) %copy-start.6) | copy-done | bytes 1441816
  15.0 0.0 collective-permute-done.1.refs_1_
  15.0 0.0 collective-permute-done.2.refs_3_
  15.0 2.0 %collective-permute-start.3 = (bf16[32,2176]{1,0:T(8,128)(2,1)S(1)}, bf16[32,2176]{1,0:T(8,128)(2,1)S(1)}, u32[]{:S(2)}, u32[]{:S(2)}) collective-permute-start(bf16[32,2176]{1,0:T(8,128)(2,1)S(1)} %collective-permute-done.1.refs_1_), channel_id=1, source_target_pairs={{0,4},{4,8},{8,12},{12,14},{14,10},{10,6},{6,2},{2,0},{1,5},{5,9},... | collective-permute-start | bytes 417800 | tf_op jit(solution)/shard_map/ppermute | solution.py:207
  17.0 0.0 collective-permute-start.5
  17.0 3.4 %collective-permute-done.3.refs_0_ = bf16[32,2176]{1,0:T(8,128)(2,1)S(1)} collective-permute-done((bf16[32,2176]{1,0:T(8,128)(2,1)S(1)}, bf16[32,2176]{1,0:T(8,128)(2,1)S(1)}, u32[]{:S(2)}, u32[]{:S(2)}) %collective-permute-start.3) | collective-permute-done | bytes 139296 | tf_op jit(solution)/shard_map/ppermute | solution.py:207
  20.4 1.7 %collective-permute-start.4 = (bf16[32,2176]{1,0:T(8,128)(2,1)S(1)}, bf16[32,2176]{1,0:T(8,128)(2,1)S(1)}, u32[]{:S(2)}, u32[]{:S(2)}) collective-permute-start(bf16[32,2176]{1,0:T(8,128)(2,1)S(1)} %collective-permute-done.3.refs_0_), channel_id=1, source_target_pairs={{0,4},{4,8},{8,12},{12,14},{14,10},{10,6},{6,2},{2,0},{1,5},{5,9},... | collective-permute-start | bytes 417800 | tf_op jit(solution)/shard_map/ppermute | solution.py:207
  22.1 0.1 collective-permute-done.5.refs_4_
  22.2 0.2 collective-permute-start.6
  22.4 0.0 collective-permute-done.7.refs_6_.refs_3_
  22.4 0.0 collective-permute-done.8.refs_8_.refs_5_
  22.4 0.0 collective-permute-done.9.refs_10_.refs_7_
  22.4 1.4 %copy-done.1 = bf16[352,2048]{1,0:T(8,128)(2,1)S(1)} copy-done((bf16[352,2048]{1,0:T(8,128)(2,1)S(1)}, bf16[352,2048]{1,0:T(8,128)(2,1)}, u32[]{:S(2)}) %copy-start.1) | copy-done | bytes 1441816
  23.8 1.4 %copy-done.4 = bf16[352,2048]{1,0:T(8,128)(2,1)S(1)} copy-done((bf16[352,2048]{1,0:T(8,128)(2,1)S(1)}, bf16[352,2048]{1,0:T(8,128)(2,1)}, u32[]{:S(2)}) %copy-start.4) | copy-done | bytes 1441816
  25.1 1.4 %copy-done.7 = bf16[352,2048]{1,0:T(8,128)(2,1)S(1)} copy-done((bf16[352,2048]{1,0:T(8,128)(2,1)S(1)}, bf16[352,2048]{1,0:T(8,128)(2,1)}, u32[]{:S(2)}) %copy-start.7) | copy-done | bytes 1441816
  26.5 4.1 %shard_map.67 = (bf16[32,2048]{1,0:T(8,128)(2,1)S(1)}, bf16[32,2048]{1,0:T(8,128)(2,1)S(1)}, bf16[32,2048]{1,0:T(8,128)(2,1)S(1)}, bf16[32,2048]{1,0:T(8,128)(2,1)S(1)}, bf16[32,2048]{1,0:T(8,128)(2,1)S(1)}) custom-call(f32[1,128]{1,0:T(1,128)S(1)} %compare_select_fusion.select_ref, bf16[32,2176]{1,0:T(8,128)(2,1)S(1)} %collective-permute-done.3.refs_0_, ...), custom_call_target="tpu_custom_call" | custom-call | flops 1384120320 | bytes 8650752 | tf_op jit(solution)/shard_map/pallas_call | solution.py:95
  30.6 0.0 copy-start.13
  30.6 0.0 collective-permute-done.4.refs_0_
  30.6 0.0 collective-permute-done.6.refs_1_
  30.6 1.9 %collective-permute-start.10 = (bf16[16,2176]{1,0:T(8,128)(2,1)S(1)}, bf16[16,2176]{1,0:T(8,128)(2,1)S(1)}, u32[]{:S(2)}, u32[]{:S(2)}) collective-permute-start(bf16[16,2176]{1,0:T(8,128)(2,1)S(1)} %slice.32), channel_id=1, source_target_pairs={{0,4},{4,8},{8,12},{12,14},{14,10},{10,6},{6,2},{2,0},{1,5},{5,9},... | collective-permute-start | bytes 208904 | tf_op jit(solution)/shard_map/ppermute | solution.py:207
  32.5 0.5 collective-permute-start.11
  33.0 0.0 copy-done.2
  33.0 3.7 %shard_map.68 = (bf16[32,2048]{1,0:T(8,128)(2,1)S(1)}, bf16[32,2048]{1,0:T(8,128)(2,1)S(1)}) custom-call(f32[1,128]{1,0:T(1,128)S(1)} %compare_select_fusion.select_ref, bf16[32,2176]{1,0:T(8,128)(2,1)S(1)} %collective-permute-done.4.refs_0_, bf16[32,2176]{1,0:T(8,128)(2,1)S(1)} %collective-permute-done.6.refs_1_, bf16[352,2048]{1,0:T(8,128)(2,1)S(1)} %copy-done.2, ...), custom_call_target="tpu_custom_call" | custom-call | flops 553648128 | bytes 8650752 | tf_op jit(solution)/shard_map/pallas_call | solution.py:95
  36.7 0.0 collective-permute-done.10.refs_0_
  36.7 0.2 collective-permute-done.11.refs_1_
  36.9 3.6 %shard_map.69 = (bf16[16,2048]{1,0:T(8,128)(2,1)S(1)}, bf16[16,2048]{1,0:T(8,128)(2,1)S(1)}) custom-call(f32[1,128]{1,0:T(1,128)S(1)} %compare_select_fusion.select_ref, bf16[16,2176]{1,0:T(8,128)(2,1)S(1)} %collective-permute-done.10.refs_0_, bf16[16,2176]{1,0:T(8,128)(2,1)S(1)} %collective-permute-done.11.refs_1_, bf16[352,2048]{1,0:T(8,128)(2,1)S(1)} %copy-done.2, ...), custom_call_target="tpu_custom_call" | custom-call | flops 276824064 | bytes 8650752 | tf_op jit(solution)/shard_map/pallas_call | solution.py:95
  40.5 0.0 copy-start.14
  40.5 1.6 %collective-permute-start.12 = (bf16[16,2048]{1,0:T(8,128)(2,1)S(1)}, bf16[16,2048]{1,0:T(8,128)(2,1)S(1)}, u32[]{:S(2)}, u32[]{:S(2)}) collective-permute-start(bf16[16,2048]{1,0:T(8,128)(2,1)S(1)} %get-tuple-element.68), channel_id=1, source_target_pairs={{0,4},{4,8},{8,12},{12,14},{14,10},{10,6},{6,2},{2,0},{1,5},{5,9},... | collective-permute-start | bytes 196616 | tf_op jit(solution)/shard_map/ppermute | solution.py:207
  42.1 0.4 collective-permute-start.16
  42.6 2.9 %collective-permute-done.12 = bf16[16,2048]{1,0:T(8,128)(2,1)S(1)} collective-permute-done((bf16[16,2048]{1,0:T(8,128)(2,1)S(1)}, bf16[16,2048]{1,0:T(8,128)(2,1)S(1)}, u32[]{:S(2)}, u32[]{:S(2)}) %collective-permute-start.12) | collective-permute-done | bytes 65568 | tf_op jit(solution)/shard_map/ppermute | solution.py:207
  45.6 1.6 %collective-permute-start.13 = (bf16[32,2048]{1,0:T(8,128)(2,1)S(1)}, bf16[32,2048]{1,0:T(8,128)(2,1)S(1)}, u32[]{:S(2)}, u32[]{:S(2)}) collective-permute-start(bf16[32,2048]{1,0:T(8,128)(2,1)S(1)} %pad_maximum_fusion), channel_id=1, source_target_pairs={{0,4},{4,8},{8,12},{12,14},{14,10},{10,6},{6,2},{2,0},{1,5},{5,9},... | collective-permute-start | bytes 393224 | tf_op jit(solution)/shard_map/ppermute | solution.py:207
  47.1 0.0 collective-permute-done.16
  47.2 0.6 collective-permute-start.17
  47.7 3.9 %collective-permute-done.13 = bf16[32,2048]{1,0:T(8,128)(2,1)S(1)} collective-permute-done((bf16[32,2048]{1,0:T(8,128)(2,1)S(1)}, bf16[32,2048]{1,0:T(8,128)(2,1)S(1)}, u32[]{:S(2)}, u32[]{:S(2)}) %collective-permute-start.13) | collective-permute-done | bytes 131104 | tf_op jit(solution)/shard_map/ppermute | solution.py:207
  51.7 1.4 %collective-permute-start.14 = (bf16[32,2048]{1,0:T(8,128)(2,1)S(1)}, bf16[32,2048]{1,0:T(8,128)(2,1)S(1)}, u32[]{:S(2)}, u32[]{:S(2)}) collective-permute-start(bf16[32,2048]{1,0:T(8,128)(2,1)S(1)} %add_convert_fusion.4), channel_id=1, source_target_pairs={{0,4},{4,8},{8,12},{12,14},{14,10},{10,6},{6,2},{2,0},{1,5},{5,9},... | collective-permute-start | bytes 393224 | tf_op jit(solution)/shard_map/ppermute | solution.py:207
  53.1 0.0 collective-permute-done.17
  53.1 0.7 %collective-permute-start.18 = (bf16[32,2048]{1,0:T(8,128)(2,1)S(1)}, bf16[32,2048]{1,0:T(8,128)(2,1)S(1)}, u32[]{:S(2)}, u32[]{:S(2)}) collective-permute-start(bf16[32,2048]{1,0:T(8,128)(2,1)S(1)} %add_convert_fusion.2), channel_id=1, source_target_pairs={{4,0},{8,4},{12,8},{14,12},{10,14},{6,10},{2,6},{0,2},{5,1},{9,5},... | collective-permute-start | bytes 393224 | tf_op jit(solution)/shard_map/ppermute | solution.py:210
  53.8 3.1 %collective-permute-done.14 = bf16[32,2048]{1,0:T(8,128)(2,1)S(1)} collective-permute-done((bf16[32,2048]{1,0:T(8,128)(2,1)S(1)}, bf16[32,2048]{1,0:T(8,128)(2,1)S(1)}, u32[]{:S(2)}, u32[]{:S(2)}) %collective-permute-start.14) | collective-permute-done | bytes 131104 | tf_op jit(solution)/shard_map/ppermute | solution.py:207
  57.0 1.2 %collective-permute-start.15 = (bf16[32,2048]{1,0:T(8,128)(2,1)S(1)}, bf16[32,2048]{1,0:T(8,128)(2,1)S(1)}, u32[]{:S(2)}, u32[]{:S(2)}) collective-permute-start(bf16[32,2048]{1,0:T(8,128)(2,1)S(1)} %add_convert_fusion.3), channel_id=1, source_target_pairs={{0,4},{4,8},{8,12},{12,14},{14,10},{10,6},{6,2},{2,0},{1,5},{5,9},... | collective-permute-start | bytes 393224 | tf_op jit(solution)/shard_map/ppermute | solution.py:207
  58.2 0.0 collective-permute-done.18
  58.3 0.9 %collective-permute-start.19 = (bf16[32,2048]{1,0:T(8,128)(2,1)S(1)}, bf16[32,2048]{1,0:T(8,128)(2,1)S(1)}, u32[]{:S(2)}, u32[]{:S(2)}) collective-permute-start(bf16[32,2048]{1,0:T(8,128)(2,1)S(1)} %add_convert_fusion.1), channel_id=1, source_target_pairs={{4,0},{8,4},{12,8},{14,12},{10,14},{6,10},{2,6},{0,2},{5,1},{9,5},... | collective-permute-start | bytes 393224 | tf_op jit(solution)/shard_map/ppermute | solution.py:210
  59.2 2.8 %collective-permute-done.15 = bf16[32,2048]{1,0:T(8,128)(2,1)S(1)} collective-permute-done((bf16[32,2048]{1,0:T(8,128)(2,1)S(1)}, bf16[32,2048]{1,0:T(8,128)(2,1)S(1)}, u32[]{:S(2)}, u32[]{:S(2)}) %collective-permute-start.15) | collective-permute-done | bytes 131104 | tf_op jit(solution)/shard_map/ppermute | solution.py:207
  62.0 1.3 %collective-permute-done.19 = bf16[32,2048]{1,0:T(8,128)(2,1)S(1)} collective-permute-done((bf16[32,2048]{1,0:T(8,128)(2,1)S(1)}, bf16[32,2048]{1,0:T(8,128)(2,1)S(1)}, u32[]{:S(2)}, u32[]{:S(2)}) %collective-permute-start.19) | collective-permute-done | bytes 131104 | tf_op jit(solution)/shard_map/ppermute | solution.py:210
  63.3 0.1 add_convert_fusion
  63.4 0.1 collective-permute-start.20
  63.4 1.2 %collective-permute-done.20 = bf16[32,1024]{1,0:T(8,128)(2,1)S(1)} collective-permute-done((bf16[32,1024]{1,0:T(8,128)(2,1)S(1)}, bf16[32,1024]{1,0:T(8,128)(2,1)S(1)}, u32[]{:S(2)}, u32[]{:S(2)}) %collective-permute-start.20) | collective-permute-done | bytes 65568 | tf_op jit(solution)/shard_map/ppermute | solution.py:263
  64.7 0.7 %pad_maximum_fusion.2 = bf16[64,1024]{1,0:T(8,128)(2,1)} fusion(bf16[32,1024]{1,0:T(8,128)(2,1)S(1)} %get-tuple-element.74, bf16[32,1024]{1,0:T(8,128)(2,1)S(1)} %get-tuple-element.73), kind=kLoop, calls=%fused_computation.7 | loop fusion | flops 262144 | bytes 262144 | tf_op jit(solution)/shard_map/concatenate | solution.py:264
  (33 shorter events, 0.3 us)
Async XLA Ops:
  0.0 3.1 %collective-permute-start = (bf16[64,1024]{1,0:T(8,128)(2,1)}, bf16[64,1024]{1,0:T(8,128)(2,1)S(1)}, u32[]{:S(2)}, u32[]{:S(2)}) collective-permute-start(bf16[64,1024]{1,0:T(8,128)(2,1)} %tokens_ref.1), channel_id=1, source_target_pairs={{0,1},{1,0},{2,3},{3,2},{4,5},{5,4},{6,7},{7,6},{8,9},{9,8},{10,11... | collective-permute-start | bytes 393224 | tf_op jit(solution)/shard_map/ppermute | solution.py:213
  2.0 0.9 %copy-start.12 = (bf16[64,1024]{1,0:T(8,128)(2,1)S(1)}, bf16[64,1024]{1,0:T(8,128)(2,1)}, u32[]{:S(2)}) copy-start(bf16[64,1024]{1,0:T(8,128)(2,1)} %tokens_ref.1) | copy-start | bytes 393220
  3.1 19.3 %collective-permute-start.7 = (bf16[352,2048]{1,0:T(8,128)(2,1)}, bf16[352,2048]{1,0:T(8,128)(2,1)S(1)}, u32[]{:S(2)}, u32[]{:S(2)}) collective-permute-start(bf16[352,2048]{1,0:T(8,128)(2,1)} %bitcast.4), channel_id=1, source_target_pairs={{0,1},{1,0},{2,3},{3,2},{4,5},{5,4},{6,7},{7,6},{8,9},{9,8},{10,11... | collective-permute-start | bytes 4325384 | tf_op jit(solution)/shard_map/ppermute | solution.py:220
  3.2 19.2 %collective-permute-start.8 = (bf16[352,2048]{1,0:T(8,128)(2,1)}, bf16[352,2048]{1,0:T(8,128)(2,1)S(1)}, u32[]{:S(2)}, u32[]{:S(2)}) collective-permute-start(bf16[352,2048]{1,0:T(8,128)(2,1)} %bitcast.6), channel_id=1, source_target_pairs={{0,1},{1,0},{2,3},{3,2},{4,5},{5,4},{6,7},{7,6},{8,9},{9,8},{10,11... | collective-permute-start | bytes 4325384 | tf_op jit(solution)/shard_map/ppermute | solution.py:220
  3.7 18.7 %collective-permute-start.9 = (bf16[352,2048]{1,0:T(8,128)(2,1)}, bf16[352,2048]{1,0:T(8,128)(2,1)}, u32[]{:S(2)}, u32[]{:S(2)}) collective-permute-start(bf16[352,2048]{1,0:T(8,128)(2,1)} %bitcast.8), channel_id=1, source_target_pairs={{0,1},{1,0},{2,3},{3,2},{4,5},{5,4},{6,7},{7,6},{8,9},{9,8},{10,11... | collective-permute-start | bytes 4325384 | tf_op jit(solution)/shard_map/ppermute | solution.py:220
  3.8 11.2 %collective-permute-start.1 = (bf16[32,2176]{1,0:T(8,128)(2,1)S(1)}, bf16[32,2176]{1,0:T(8,128)(2,1)S(1)}, u32[]{:S(2)}, u32[]{:S(2)}) collective-permute-start(bf16[32,2176]{1,0:T(8,128)(2,1)S(1)} %shard_map.65.refs_2_), channel_id=1, source_target_pairs={{0,4},{4,8},{8,12},{12,14},{14,10},{10,6},{6,2},{2,0},{1,5},{5,9},... | collective-permute-start | bytes 417800 | tf_op jit(solution)/shard_map/ppermute | solution.py:207
  6.8 8.2 %collective-permute-start.2 = (bf16[32,2176]{1,0:T(8,128)(2,1)S(1)}, bf16[32,2176]{1,0:T(8,128)(2,1)S(1)}, u32[]{:S(2)}, u32[]{:S(2)}) collective-permute-start(bf16[32,2176]{1,0:T(8,128)(2,1)S(1)} %shard_map.65.refs_2_), channel_id=1, source_target_pairs={{4,0},{8,4},{12,8},{14,12},{10,14},{6,10},{2,6},{0,2},{5,1},{9,5},... | collective-permute-start | bytes 417800 | tf_op jit(solution)/shard_map/ppermute | solution.py:210
  6.8 1.4 %copy-start.9 = (bf16[1,352,2048]{2,1,0:T(8,128)(2,1)S(1)}, bf16[1,352,2048]{2,1,0:T(8,128)(2,1)}, u32[]{:S(2)}) copy-start(bf16[1,352,2048]{2,1,0:T(8,128)(2,1)} %param.9) | copy-start | bytes 4325380
  8.1 1.4 %copy-start.10 = (bf16[1,352,2048]{2,1,0:T(8,128)(2,1)S(1)}, bf16[1,352,2048]{2,1,0:T(8,128)(2,1)}, u32[]{:S(2)}) copy-start(bf16[1,352,2048]{2,1,0:T(8,128)(2,1)} %param.10) | copy-start | bytes 4325380
  9.5 1.4 %copy-start.11 = (bf16[1,352,2048]{2,1,0:T(8,128)(2,1)S(1)}, bf16[1,352,2048]{2,1,0:T(8,128)(2,1)}, u32[]{:S(2)}) copy-start(bf16[1,352,2048]{2,1,0:T(8,128)(2,1)} %param.11) | copy-start | bytes 4325380
  11.7 1.1 %copy-start = (bf16[352,2048]{1,0:T(8,128)(2,1)}, bf16[352,2048]{1,0:T(8,128)(2,1)S(1)}, u32[]{:S(2)}) copy-start(bf16[352,2048]{1,0:T(8,128)(2,1)S(1)} %get-tuple-element.50.refs_5_.refs_2_) | copy-start | bytes 4325380
  12.8 1.1 %copy-start.3 = (bf16[352,2048]{1,0:T(8,128)(2,1)}, bf16[352,2048]{1,0:T(8,128)(2,1)S(1)}, u32[]{:S(2)}) copy-start(bf16[352,2048]{1,0:T(8,128)(2,1)S(1)} %get-tuple-element.51.refs_7_.refs_4_) | copy-start | bytes 4325380
  13.9 1.1 %copy-start.6 = (bf16[352,2048]{1,0:T(8,128)(2,1)}, bf16[352,2048]{1,0:T(8,128)(2,1)S(1)}, u32[]{:S(2)}) copy-start(bf16[352,2048]{1,0:T(8,128)(2,1)S(1)} %get-tuple-element.52.refs_9_.refs_6_) | copy-start | bytes 4325380
  15.0 5.4 %collective-permute-start.3 = (bf16[32,2176]{1,0:T(8,128)(2,1)S(1)}, bf16[32,2176]{1,0:T(8,128)(2,1)S(1)}, u32[]{:S(2)}, u32[]{:S(2)}) collective-permute-start(bf16[32,2176]{1,0:T(8,128)(2,1)S(1)} %collective-permute-done.1.refs_1_), channel_id=1, source_target_pairs={{0,4},{4,8},{8,12},{12,14},{14,10},{10,6},{6,2},{2,0},{1,5},{5,9},... | collective-permute-start | bytes 417800 | tf_op jit(solution)/shard_map/ppermute | solution.py:207
  17.0 5.2 %collective-permute-start.5 = (bf16[32,2176]{1,0:T(8,128)(2,1)S(1)}, bf16[32,2176]{1,0:T(8,128)(2,1)}, u32[]{:S(2)}, u32[]{:S(2)}) collective-permute-start(bf16[32,2176]{1,0:T(8,128)(2,1)S(1)} %collective-permute-done.2.refs_3_), channel_id=1, source_target_pairs={{4,0},{8,4},{12,8},{14,12},{10,14},{6,10},{2,6},{0,2},{5,1},{9,5},... | collective-permute-start | bytes 417800 | tf_op jit(solution)/shard_map/ppermute | solution.py:210
  20.4 10.2 %collective-permute-start.4 = (bf16[32,2176]{1,0:T(8,128)(2,1)S(1)}, bf16[32,2176]{1,0:T(8,128)(2,1)S(1)}, u32[]{:S(2)}, u32[]{:S(2)}) collective-permute-start(bf16[32,2176]{1,0:T(8,128)(2,1)S(1)} %collective-permute-done.3.refs_0_), channel_id=1, source_target_pairs={{0,4},{4,8},{8,12},{12,14},{14,10},{10,6},{6,2},{2,0},{1,5},{5,9},... | collective-permute-start | bytes 417800 | tf_op jit(solution)/shard_map/ppermute | solution.py:207
  22.2 8.4 %collective-permute-start.6 = (bf16[32,2176]{1,0:T(8,128)(2,1)}, bf16[32,2176]{1,0:T(8,128)(2,1)S(1)}, u32[]{:S(2)}, u32[]{:S(2)}) collective-permute-start(bf16[32,2176]{1,0:T(8,128)(2,1)} %collective-permute-done.5.refs_4_), channel_id=1, source_target_pairs={{4,0},{8,4},{12,8},{14,12},{10,14},{6,10},{2,6},{0,2},{5,1},{9,5},... | collective-permute-start | bytes 417800 | tf_op jit(solution)/shard_map/ppermute | solution.py:210
  22.4 1.4 %copy-start.1 = (bf16[352,2048]{1,0:T(8,128)(2,1)S(1)}, bf16[352,2048]{1,0:T(8,128)(2,1)}, u32[]{:S(2)}) copy-start(bf16[352,2048]{1,0:T(8,128)(2,1)} %copy-done) | copy-start | bytes 4325380
  23.8 1.4 %copy-start.4 = (bf16[352,2048]{1,0:T(8,128)(2,1)S(1)}, bf16[352,2048]{1,0:T(8,128)(2,1)}, u32[]{:S(2)}) copy-start(bf16[352,2048]{1,0:T(8,128)(2,1)} %copy-done.3) | copy-start | bytes 4325380
  25.1 1.4 %copy-start.7 = (bf16[352,2048]{1,0:T(8,128)(2,1)S(1)}, bf16[352,2048]{1,0:T(8,128)(2,1)}, u32[]{:S(2)}) copy-start(bf16[352,2048]{1,0:T(8,128)(2,1)} %copy-done.6) | copy-start | bytes 4325380
  26.5 6.4 %copy-start.2 = (bf16[352,2048]{1,0:T(8,128)(2,1)S(1)}, bf16[352,2048]{1,0:T(8,128)(2,1)}, u32[]{:S(2)}) copy-start(bf16[352,2048]{1,0:T(8,128)(2,1)} %copy-done) | copy-start | bytes 4325380
  26.5 6.4 %copy-start.5 = (bf16[352,2048]{1,0:T(8,128)(2,1)S(1)}, bf16[352,2048]{1,0:T(8,128)(2,1)}, u32[]{:S(2)}) copy-start(bf16[352,2048]{1,0:T(8,128)(2,1)} %copy-done.3) | copy-start | bytes 4325380
  26.5 6.4 %copy-start.8 = (bf16[352,2048]{1,0:T(8,128)(2,1)S(1)}, bf16[352,2048]{1,0:T(8,128)(2,1)}, u32[]{:S(2)}) copy-start(bf16[352,2048]{1,0:T(8,128)(2,1)} %copy-done.6) | copy-start | bytes 4325380
  30.6 1.9 %copy-start.13 = (bf16[32,2048]{1,0:T(8,128)(2,1)}, bf16[32,2048]{1,0:T(8,128)(2,1)S(1)}, u32[]{:S(2)}) copy-start(bf16[32,2048]{1,0:T(8,128)(2,1)S(1)} %get-tuple-element.58) | copy-start | bytes 393220
  30.6 6.0 %collective-permute-start.10 = (bf16[16,2176]{1,0:T(8,128)(2,1)S(1)}, bf16[16,2176]{1,0:T(8,128)(2,1)S(1)}, u32[]{:S(2)}, u32[]{:S(2)}) collective-permute-start(bf16[16,2176]{1,0:T(8,128)(2,1)S(1)} %slice.32), channel_id=1, source_target_pairs={{0,4},{4,8},{8,12},{12,14},{14,10},{10,6},{6,2},{2,0},{1,5},{5,9},... | collective-permute-start | bytes 208904 | tf_op jit(solution)/shard_map/ppermute | solution.py:207
  32.5 4.4 %collective-permute-start.11 = (bf16[16,2176]{1,0:T(8,128)(2,1)S(1)}, bf16[16,2176]{1,0:T(8,128)(2,1)S(1)}, u32[]{:S(2)}, u32[]{:S(2)}) collective-permute-start(bf16[16,2176]{1,0:T(8,128)(2,1)S(1)} %slice.33), channel_id=1, source_target_pairs={{4,0},{8,4},{12,8},{14,12},{10,14},{6,10},{2,6},{0,2},{5,1},{9,5},... | collective-permute-start | bytes 208904 | tf_op jit(solution)/shard_map/ppermute | solution.py:210
  40.5 22.8 %copy-start.14 = (bf16[32,2048]{1,0:T(8,128)(2,1)S(1)}, bf16[32,2048]{1,0:T(8,128)(2,1)}, u32[]{:S(2)}) copy-start(bf16[32,2048]{1,0:T(8,128)(2,1)} %copy-done.13) | copy-start | bytes 393220
  40.5 5.0 %collective-permute-start.12 = (bf16[16,2048]{1,0:T(8,128)(2,1)S(1)}, bf16[16,2048]{1,0:T(8,128)(2,1)S(1)}, u32[]{:S(2)}, u32[]{:S(2)}) collective-permute-start(bf16[16,2048]{1,0:T(8,128)(2,1)S(1)} %get-tuple-element.68), channel_id=1, source_target_pairs={{0,4},{4,8},{8,12},{12,14},{14,10},{10,6},{6,2},{2,0},{1,5},{5,9},... | collective-permute-start | bytes 196616 | tf_op jit(solution)/shard_map/ppermute | solution.py:207
  42.1 5.0 %collective-permute-start.16 = (bf16[16,2048]{1,0:T(8,128)(2,1)S(1)}, bf16[16,2048]{1,0:T(8,128)(2,1)S(1)}, u32[]{:S(2)}, u32[]{:S(2)}) collective-permute-start(bf16[16,2048]{1,0:T(8,128)(2,1)S(1)} %get-tuple-element.72), channel_id=1, source_target_pairs={{4,0},{8,4},{12,8},{14,12},{10,14},{6,10},{2,6},{0,2},{5,1},{9,5},... | collective-permute-start | bytes 196616 | tf_op jit(solution)/shard_map/ppermute | solution.py:210
  45.6 6.1 %collective-permute-start.13 = (bf16[32,2048]{1,0:T(8,128)(2,1)S(1)}, bf16[32,2048]{1,0:T(8,128)(2,1)S(1)}, u32[]{:S(2)}, u32[]{:S(2)}) collective-permute-start(bf16[32,2048]{1,0:T(8,128)(2,1)S(1)} %pad_maximum_fusion), channel_id=1, source_target_pairs={{0,4},{4,8},{8,12},{12,14},{14,10},{10,6},{6,2},{2,0},{1,5},{5,9},... | collective-permute-start | bytes 393224 | tf_op jit(solution)/shard_map/ppermute | solution.py:207
  47.2 5.9 %collective-permute-start.17 = (bf16[32,2048]{1,0:T(8,128)(2,1)S(1)}, bf16[32,2048]{1,0:T(8,128)(2,1)S(1)}, u32[]{:S(2)}, u32[]{:S(2)}) collective-permute-start(bf16[32,2048]{1,0:T(8,128)(2,1)S(1)} %pad_maximum_fusion.1), channel_id=1, source_target_pairs={{4,0},{8,4},{12,8},{14,12},{10,14},{6,10},{2,6},{0,2},{5,1},{9,5},... | collective-permute-start | bytes 393224 | tf_op jit(solution)/shard_map/ppermute | solution.py:210
  51.7 5.3 %collective-permute-start.14 = (bf16[32,2048]{1,0:T(8,128)(2,1)S(1)}, bf16[32,2048]{1,0:T(8,128)(2,1)S(1)}, u32[]{:S(2)}, u32[]{:S(2)}) collective-permute-start(bf16[32,2048]{1,0:T(8,128)(2,1)S(1)} %add_convert_fusion.4), channel_id=1, source_target_pairs={{0,4},{4,8},{8,12},{12,14},{14,10},{10,6},{6,2},{2,0},{1,5},{5,9},... | collective-permute-start | bytes 393224 | tf_op jit(solution)/shard_map/ppermute | solution.py:207
  53.1 5.1 %collective-permute-start.18 = (bf16[32,2048]{1,0:T(8,128)(2,1)S(1)}, bf16[32,2048]{1,0:T(8,128)(2,1)S(1)}, u32[]{:S(2)}, u32[]{:S(2)}) collective-permute-start(bf16[32,2048]{1,0:T(8,128)(2,1)S(1)} %add_convert_fusion.2), channel_id=1, source_target_pairs={{4,0},{8,4},{12,8},{14,12},{10,14},{6,10},{2,6},{0,2},{5,1},{9,5},... | collective-permute-start | bytes 393224 | tf_op jit(solution)/shard_map/ppermute | solution.py:210
  57.0 5.0 %collective-permute-start.15 = (bf16[32,2048]{1,0:T(8,128)(2,1)S(1)}, bf16[32,2048]{1,0:T(8,128)(2,1)S(1)}, u32[]{:S(2)}, u32[]{:S(2)}) collective-permute-start(bf16[32,2048]{1,0:T(8,128)(2,1)S(1)} %add_convert_fusion.3), channel_id=1, source_target_pairs={{0,4},{4,8},{8,12},{12,14},{14,10},{10,6},{6,2},{2,0},{1,5},{5,9},... | collective-permute-start | bytes 393224 | tf_op jit(solution)/shard_map/ppermute | solution.py:207
  58.3 5.0 %collective-permute-start.19 = (bf16[32,2048]{1,0:T(8,128)(2,1)S(1)}, bf16[32,2048]{1,0:T(8,128)(2,1)S(1)}, u32[]{:S(2)}, u32[]{:S(2)}) collective-permute-start(bf16[32,2048]{1,0:T(8,128)(2,1)S(1)} %add_convert_fusion.1), channel_id=1, source_target_pairs={{4,0},{8,4},{12,8},{14,12},{10,14},{6,10},{2,6},{0,2},{5,1},{9,5},... | collective-permute-start | bytes 393224 | tf_op jit(solution)/shard_map/ppermute | solution.py:210
  63.4 1.3 %collective-permute-start.20 = (bf16[32,1024]{1,0:T(8,128)(2,1)S(1)}, bf16[32,1024]{1,0:T(8,128)(2,1)S(1)}, u32[]{:S(2)}, u32[]{:S(2)}) collective-permute-start(bf16[32,1024]{1,0:T(8,128)(2,1)S(1)} %broadcast_select_fusion.2), channel_id=1, source_target_pairs={{0,1},{1,0},{2,3},{3,2},{4,5},{5,4},{6,7},{7,6},{8,9},{9,8},{10,11... | collective-permute-start | bytes 196616 | tf_op jit(solution)/shard_map/ppermute | solution.py:263

commit v3 on v1

--- a/solution.py
+++ b/solution.py
@@ -9,7 +9,9 @@
 
 LANES = 128
 PIECES = 3
-VMEM_LIMIT = 24 * 2**20
+VMEM_LIMIT = 16 * 2**20
+SMALL_LIMIT = 4 * 2**20
+MARK = (8, 128)
 
 
 def sparse_local(tokens, expert_ids, gate_scores, gate_proj, up_proj, down_proj):
@@ -63,50 +65,181 @@
     return mixed.astype(jnp.bfloat16)
 
 
-def expert_kernel(counts, select_ref, *refs):
+def in_vmem():
+    return pl.BlockSpec(memory_space=pltpu.VMEM)
+
+
+def in_hbm():
+    return pl.BlockSpec(memory_space=pltpu.HBM)
+
+
+def hbm(v):
+    return pltpu.with_memory_space_constraint(v, pltpu.HBM)
+
+
+def spread_kernel(n, head_ref, tokens_hbm, ids_hbm, scores_hbm, mine_ref, lanes_ref, ids, scores, sems):
+    part = mine_ref.shape[0]
+    head = head_ref[0]
+    copies = [
+        pltpu.make_async_copy(ids_hbm, ids, sems.at[0]),
+        pltpu.make_async_copy(scores_hbm, scores, sems.at[1]),
+        pltpu.make_async_copy(
+            tokens_hbm.at[pl.ds(pl.multiple_of(head * part, part), part)], mine_ref, sems.at[2]
+        ),
+    ]
+    for copy in copies:
+        copy.start()
+    copies[0].wait()
+    copies[1].wait()
+    names, values = ids[...], scores[...]
+    top, rows = names.shape
+    expert = lax.broadcasted_iota(jnp.int32, (n, rows), 0)
+    dense = jnp.zeros((n, rows), jnp.float32)
+    for k in range(top):
+        dense = dense + jnp.where(expert == names[k : k + 1], values[k : k + 1], 0.0)
+    pieces = []
+    for _ in range(PIECES):
+        piece = dense.astype(jnp.bfloat16).astype(jnp.float32)
+        pieces.append(piece)
+        dense = dense - piece
+    pieces.append(jnp.zeros((LANES - PIECES * n, rows), jnp.float32))
+    packed = jnp.concatenate(pieces, axis=0).T
+    lanes_ref[...] = jnp.where(head == 0, packed[:part], packed[part:]).astype(jnp.bfloat16)
+    copies[2].wait()
+
+
+def spread(head, tokens, expert_ids, gate_scores):
+    rows, half_width = tokens.shape
+    n = lax.axis_size("wide")
+    top = expert_ids.shape[1]
+    return pl.pallas_call(
+        functools.partial(spread_kernel, n),
+        out_shape=[
+            jax.ShapeDtypeStruct((rows // 2, half_width), jnp.bfloat16),
+            jax.ShapeDtypeStruct((rows // 2, LANES), jnp.bfloat16),
+        ],
+        in_specs=[pl.BlockSpec(memory_space=pltpu.SMEM)] + [in_hbm()] * 3,
+        out_specs=[in_vmem()] * 2,
+        scratch_shapes=[
+            pltpu.VMEM((top, rows), jnp.int32),
+            pltpu.VMEM((top, rows), jnp.float32),
+            pltpu.SemaphoreType.DMA((3,)),
+        ],
+        compiler_params=pltpu.CompilerParams(vmem_limit_bytes=SMALL_LIMIT),
+        cost_estimate=pl.CostEstimate(
+            flops=0, bytes_accessed=3 * rows * half_width, transcendentals=0
+        ),
+    )(head.reshape(1), hbm(tokens), hbm(expert_ids.T), hbm(gate_scores.T))
+
+
+def join_kernel(head_ref, mine_ref, got_ref, lanes_ref, out_ref):
+    part, half_width = mine_ref.shape
+    first = head_ref[0] == 0
+    mine = mine_ref[...]
+    out_ref[:, :half_width] = jnp.where(first, mine, got_ref[part:])
+    out_ref[:, half_width : 2 * half_width] = jnp.where(first, got_ref[:part], mine)
+    out_ref[:, 2 * half_width :] = lanes_ref[...]
+
+
+def join(head, mine, got, lanes):
+    part, half_width = mine.shape
+    return pl.pallas_call(
+        join_kernel,
+        out_shape=jax.ShapeDtypeStruct((part, 2 * half_width + LANES), jnp.bfloat16),
+        in_specs=[pl.BlockSpec(memory_space=pltpu.SMEM)] + [in_vmem()] * 3,
+        out_specs=in_vmem(),
+        compiler_params=pltpu.CompilerParams(vmem_limit_bytes=SMALL_LIMIT),
+        cost_estimate=pl.CostEstimate(
+            flops=0, bytes_accessed=8 * part * half_width, transcendentals=0
+        ),
+    )(head.reshape(1), mine, got, lanes)
+
+
+def gather_kernel(count, *refs):
+    kept, came = refs[:count], refs[count : 2 * count]
+    outs, mark, sems = refs[2 * count : 3 * count], refs[3 * count], refs[3 * count + 1]
+    copies = []
+    for i in range(count):
+        units = kept[i].shape[0]
+        cut = units // 2
+        for j, (source, target) in enumerate(
+            (
+                (kept[i].at[:cut], outs[i].at[:cut]),
+                (kept[i].at[cut:], outs[i].at[cut:units]),
+                (came[i], outs[i].at[units:]),
+            )
+        ):
+            copies.append(pltpu.make_async_copy(source, target, sems.at[i, j]))
+    for copy in copies:
+        copy.start()
+    mark[...] = jnp.zeros(mark.shape, mark.dtype)
+    for copy in copies:
+        copy.wait()
+
+
+def gather_weights(kept, came):
+    count = len(kept)
+    units, width = kept[0].shape
+    *whole, mark = pl.pallas_call(
+        functools.partial(gather_kernel, count),
+        out_shape=[jax.ShapeDtypeStruct((2 * units, width), jnp.bfloat16)] * count
+        + [jax.ShapeDtypeStruct(MARK, jnp.float32)],
+        in_specs=[in_hbm()] * count + [pl.BlockSpec(memory_space=pl.ANY)] * count,
+        out_specs=[in_vmem()] * (count + 1),
+        scratch_shapes=[pltpu.SemaphoreType.DMA((count, 3))],
+        compiler_params=pltpu.CompilerParams(vmem_limit_bytes=SMALL_LIMIT),
+        cost_estimate=pl.CostEstimate(
+            flops=0, bytes_accessed=4 * count * units * width, transcendentals=0
+        ),
+    )(*[hbm(w) for w in kept], *came)
+    return whole, mark
+
+
+def expert_kernel(counts, _, select_ref, *refs):
     blocks = refs[: len(counts)]
-    wg0, wg1, wu0, wu1, wd0, wd1 = refs[len(counts) : len(counts) + 6]
-    outs = refs[len(counts) + 6 :]
-    width = wg0.shape[1]
+    wg, wu, wd = refs[len(counts) : len(counts) + 3]
+    outs = refs[len(counts) + 3 : -1]
+    mark = refs[-1]
+    width = wg.shape[1]
     whole = [b[...] for b in blocks]
     rows = whole[0] if len(whole) == 1 else jnp.concatenate(whole, axis=0)
     x = rows[:, :width]
     scale = jnp.sum(rows[:, width:].astype(jnp.float32) * select_ref[...], axis=1, keepdims=True)
-    total = None
-    for wg, wu, wd in ((wg0, wu0, wd0), (wg1, wu1, wd1)):
-        gate = lax.dot_general(
-            x, wg[...], (((1,), (1,)), ((), ())), preferred_element_type=jnp.float32
-        )
-        up = lax.dot_general(
-            x, wu[...], (((1,), (1,)), ((), ())), preferred_element_type=jnp.float32
-        )
-        hidden = (gate / (1.0 + jnp.exp(-gate)) * up).astype(jnp.bfloat16)
-        term = jnp.dot(hidden, wd[...], preferred_element_type=jnp.float32)
-        total = term if total is None else total + term
+    contract = (((1,), (1,)), ((), ()))
+    gate = lax.dot_general(x, wg[...], contract, preferred_element_type=jnp.float32)
+    up = lax.dot_general(x, wu[...], contract, preferred_element_type=jnp.float32)
+    hidden = (gate / (1.0 + jnp.exp(-gate)) * up).astype(jnp.bfloat16)
+    total = jnp.dot(hidden, wd[...], preferred_element_type=jnp.float32)
     scaled = (total * scale).astype(jnp.bfloat16)
     start = 0
     for count, out in zip(counts, outs):
         out[...] = scaled[start : start + count]
         start += count
-
-
-def run_expert(blocks, select, weights):
+    mark[...] = jnp.zeros(mark.shape, mark.dtype)
+
+
+def run_expert(mark, blocks, select, weights):
     counts = tuple(b.shape[0] for b in blocks)
-    width = weights[0].shape[1]
-    units = sum(w.shape[0] for w in weights)
-    spec = pl.BlockSpec(memory_space=pltpu.VMEM)
-    return pl.pallas_call(
+    units, width = weights[0].shape
+    *outs, mark = pl.pallas_call(
         functools.partial(expert_kernel, counts),
-        out_shape=[jax.ShapeDtypeStruct((c, width), jnp.bfloat16) for c in counts],
-        in_specs=[spec] * (1 + len(blocks) + len(weights)),
-        out_specs=[spec] * len(blocks),
+        out_shape=[jax.ShapeDtypeStruct((c, width), jnp.bfloat16) for c in counts]
+        + [jax.ShapeDtypeStruct(MARK, jnp.float32)],
+        in_specs=[pl.BlockSpec(memory_space=pl.ANY)]
+        + [in_vmem()] * (1 + len(blocks) + len(weights)),
+        out_specs=[in_vmem()] * (len(blocks) + 1),
         compiler_params=pltpu.CompilerParams(vmem_limit_bytes=VMEM_LIMIT),
         cost_estimate=pl.CostEstimate(
-            flops=2 * sum(counts) * units * width,
-            bytes_accessed=2 * units * width,
-            transcendentals=sum(counts) * units // 3,
-        ),
-    )(select, *blocks, *weights)
+            flops=6 * sum(counts) * units * width,
+            bytes_accessed=6 * units * width,
+            transcendentals=sum(counts) * units,
+        ),
+    )(mark, select, *blocks, *weights)
+    return outs, mark
+
+
+def after(mark, *values):
+    return lax.optimization_barrier((mark, *values))
 
 
 def dense_local(tokens, expert_ids, gate_scores, gate_proj, up_proj, down_proj):
@@ -126,52 +259,44 @@
     def back(v):
         return lax.ppermute(v, "wide", behind)
 
-    mine = lax.dynamic_slice_in_dim(tokens, head * part, part, 0)
-    other = lax.dynamic_slice_in_dim(tokens, (1 - head) * part, part, 0)
-    got = lax.ppermute(other, "head", swap)
     first = head == 0
-    named = expert_ids[:, :, None] == jnp.arange(n, dtype=jnp.int32)[None, None, :]
-    scores = jnp.sum(jnp.where(named, gate_scores[:, :, None], 0.0), axis=1)
-    scores = lax.dynamic_slice_in_dim(scores, head * part, part, 0)
-    pieces = []
-    rest = scores
-    for _ in range(PIECES):
-        piece = rest.astype(jnp.bfloat16)
-        pieces.append(piece)
-        rest = rest - piece.astype(jnp.float32)
-    pad = jnp.zeros((part, LANES - PIECES * n), jnp.bfloat16)
-    own = jnp.concatenate(
-        [jnp.where(first, mine, got), jnp.where(first, got, mine)] + pieces + [pad], axis=1
-    )
+    got = lax.ppermute(tokens, "head", swap)
+    mine, lanes = spread(head, tokens, expert_ids, gate_scores)
+    kept = (gate_proj[0], up_proj[0], down_proj[0])
+    got, *kept = after(got, *kept)
+    came = [lax.ppermute(w, "head", swap) for w in kept]
+    own = join(head, mine, got, lanes)
     lane = jnp.arange(LANES, dtype=jnp.int32)
     select = jnp.where(lane % n == expert, 1.0, 0.0).astype(jnp.float32)[None, :]
 
-    weights = []
-    for w in (gate_proj[0], up_proj[0], down_proj[0]):
-        weights += [w, lax.ppermute(w, "head", swap)]
-
-    half_round = n // 2
+    reach = n // 2
     cut = part // 2
     near = {0: own}
-    f = b = own
-    sums = {}
-    todo = [0]
-    for k in range(1, half_round):
+    f, b = forth(own), back(own)
+    near[-1], near[1] = f, b
+    weights, mark = gather_weights(kept, came)
+    for k in range(2, reach):
         f, b = forth(f), back(b)
         near[-k], near[k] = f, b
-        done = run_expert([near[i] for i in todo], select, weights)
-        sums.update(zip(todo, done))
-        todo = [-k, k]
+        if k == 2:
+            mark, f, b = after(mark, f, b)
+    sums = {}
+    keys = sorted(i for i in near if abs(i) < reach - 1)
+    done, mark = run_expert(mark, [near[i] for i in keys], select, weights)
+    sums.update(zip(keys, done))
+    mark, f, b = after(mark, f, b)
     f, b = forth(f[:cut]), back(b[cut:])
-    done = run_expert([near[i] for i in todo], select, weights)
-    sums.update(zip(todo, done))
-    far = run_expert([f, b], select, weights)
+    keys = [1 - reach, reach - 1]
+    done, mark = run_expert(mark, [near[i] for i in keys], select, weights)
+    sums.update(zip(keys, done))
+    mark, f, b = after(mark, f, b)
+    far, _ = run_expert(mark, [f, b], select, weights)
 
     f, b = forth(far[0]), back(far[1])
-    for k in range(half_round - 1, 0, -1):
+    for k in range(reach - 1, 0, -1):
         up_sum = sums[k].astype(jnp.float32)
         down_sum = sums[-k].astype(jnp.float32)
-        if k == half_round - 1:
+        if k == reach - 1:
             up_sum = jnp.concatenate([up_sum[:cut] + f.astype(jnp.float32), up_sum[cut:]], axis=0)
             down_sum = jnp.concatenate(
                 [down_sum[:cut], down_sum[cut:] + b.astype(jnp.float32)], axis=0
@@ -185,9 +310,9 @@
     )
     left, right = mixed[:, :half_width], mixed[:, half_width:]
     keep = jnp.where(first, left, right)
-    came = lax.ppermute(jnp.where(first, right, left), "head", swap)
+    rest = lax.ppermute(jnp.where(first, right, left), "head", swap)
     return jnp.concatenate(
-        [jnp.where(first, keep, came), jnp.where(first, came, keep)], axis=0
+        [jnp.where(first, keep, rest), jnp.where(first, rest, keep)], axis=0
     )
 
 

time: 69.3 us -> 56.1 us (0.81)
  Pallas kernels: 18.8 us -> 12.3 us
  local copies, waits for them, and re-layouts: 5.87 us -> 0.02 us
  other arithmetic: 2.53 us -> 0.94 us
  waiting for transfers between devices: 22.7 us -> 23.8 us
    pallas_call x5 -> x3, Pallas kernels: 18.8 us -> 8.49 us  [run_expert(): pl.pallas_call(functools.partial(expert_kernel, counts), out_shape=[jax.S...]
    unnamed x17 -> x0, local copies, waits for them, and re-layouts: 4.83 us -> none
    pallas_call x0 -> x3, Pallas kernels: none -> 3.79 us  [the longest x1 2.87 us: gather_weights(): pl.pallas_call(functools.partial(gather_kernel, count), out_shape=[jax.Sh...]
    ppermute x8, waiting for transfers between devices: 3 us -> 6.11 us  [back(): return lax.ppermute(v, 'wide', behind)]
    ppermute x8, waiting for transfers between devices: 17.6 us -> 15.2 us  [forth(): return lax.ppermute(v, 'wide', ahead)]
    ppermute x8, starting transfers between devices: 15.1 us -> 13.9 us  [forth(): return lax.ppermute(v, 'wide', ahead)]
    dynamic_slice x2 -> x0, local copies, waits for them, and re-layouts: 0.92 us -> none  [the longest x1 0.84 us: dense_local(): other = lax.dynamic_slice_in_dim(tokens, (1 - head) * part, part, 0)]
    ppermute x8, starting transfers between devices: 2.56 us -> 3.46 us  [back(): return lax.ppermute(v, 'wide', behind)]
  transfers between devices with their start and end apart: 21 -> 21, of which waited for: 10 -> 12; matrix products, arithmetic and copies ran while one was open for 4% -> 0% of each run, Pallas kernels for 22% -> 17%
where the time goes in v3:
time: 56.1 us; the launch traced here: 55.9 us
  waiting for transfers between devices  23.8 us (42%)
  starting transfers between devices  18.7 us (33%)
  Pallas kernels  12.3 us (22%)
  other arithmetic  0.94 us (2%)
    ppermute x8, waiting for transfers between devices, forth(): return lax.ppermute(v, 'wide', ahead)  15.2 us
    ppermute x8, starting transfers between devices, forth(): return lax.ppermute(v, 'wide', ahead)  13.9 us
    pallas_call x3, Pallas kernels, run_expert(): pl.pallas_call(functools.partial(expert_kernel, counts), out_shape=[jax.S...  8.49 us
    ppermute x8, waiting for transfers between devices, back(): return lax.ppermute(v, 'wide', behind)  6.11 us
    ppermute x8, starting transfers between devices, back(): return lax.ppermute(v, 'wide', behind)  3.46 us
    pallas_call x1, Pallas kernels, gather_weights(): pl.pallas_call(functools.partial(gather_kernel, count), out_shape=[jax.Sh...  2.87 us
    ppermute x1, waiting for transfers between devices, dense_local(): rest = lax.ppermute(jnp.where(first, right, left), 'head', swap)  1.24 us
    ppermute x1, waiting for transfers between devices, dense_local(): got = lax.ppermute(tokens, 'head', swap)  1.2 us
  transfers between devices with their start and end apart: 21, of which 12 were waited for; matrix products, arithmetic and copies ran while one was open for 0% of the time, Pallas kernels for 17%

profile of v3, /device:TPU:0, one launch (start us, length us, event | category | flops | bytes accessed | tf_op | source)
XLA Modules:
  0.0 55.9 jit_solution(13103746294834963483)
XLA Ops:
  0.0 0.5 collective-permute-start
  0.5 1.2 %collective-permute-done.got_ref = bf16[64,1024]{1,0:T(8,128)(2,1)S(1)} collective-permute-done((bf16[64,1024]{1,0:T(8,128)(2,1)}, bf16[64,1024]{1,0:T(8,128)(2,1)S(1)}, u32[]{:S(2)}, u32[]{:S(2)}) %collective-permute-start) | collective-permute-done | bytes 131104 | tf_op jit(solution)/shard_map/ppermute | solution.py:263
  1.7 0.4 collective-permute-start.1
  2.0 0.1 collective-permute-start.2
  2.2 0.4 collective-permute-start.3
  2.5 0.9 %shard_map.65 = (bf16[32,1024]{1,0:T(8,128)(2,1)S(1)}, bf16[32,128]{1,0:T(8,128)(2,1)S(1)}) custom-call(s32[1]{0:T(128)} %bitcast.3.head_ref, bf16[64,1024]{1,0:T(8,128)(2,1)} %tokens_hbm.1, s32[8,64]{1,0:T(8,128)} %bitcast.12, f32[8,64]{1,0:T(8,128)} %bitcast.13), custom_call_target="tpu_custom_call" | custom-call | bytes 196608 | tf_op jit(solution)/shard_map/pallas_call | solution.py:115
  3.5 2.8 %collective-permute-start.4 = (bf16[32,2176]{1,0:T(8,128)(2,1)S(1)}, bf16[32,2176]{1,0:T(8,128)(2,1)S(1)}, u32[]{:S(2)}, u32[]{:S(2)}) collective-permute-start(bf16[32,2176]{1,0:T(8,128)(2,1)S(1)} %shard_map.66.refs_2_), channel_id=1, source_target_pairs={{0,4},{4,8},{8,12},{12,14},{14,10},{10,6},{6,2},{2,0},{1,5},{5,9},... | collective-permute-start | bytes 417800 | tf_op jit(solution)/shard_map/ppermute | solution.py:257
  6.2 0.0 collective-permute-start.6
  6.2 4.1 %collective-permute-done.4.refs_1_ = bf16[32,2176]{1,0:T(8,128)(2,1)S(1)} collective-permute-done((bf16[32,2176]{1,0:T(8,128)(2,1)S(1)}, bf16[32,2176]{1,0:T(8,128)(2,1)S(1)}, u32[]{:S(2)}, u32[]{:S(2)}) %collective-permute-start.4) | collective-permute-done | bytes 139296 | tf_op jit(solution)/shard_map/ppermute | solution.py:257
  10.3 1.8 %collective-permute-start.5 = (bf16[32,2176]{1,0:T(8,128)(2,1)S(1)}, bf16[32,2176]{1,0:T(8,128)(2,1)S(1)}, u32[]{:S(2)}, u32[]{:S(2)}) collective-permute-start(bf16[32,2176]{1,0:T(8,128)(2,1)S(1)} %collective-permute-done.4.refs_1_), channel_id=1, source_target_pairs={{0,4},{4,8},{8,12},{12,14},{14,10},{10,6},{6,2},{2,0},{1,5},{5,9},... | collective-permute-start | bytes 417800 | tf_op jit(solution)/shard_map/ppermute | solution.py:257
  12.2 0.0 collective-permute-done.6.refs_3_
  12.2 0.2 collective-permute-start.7
  12.4 0.0 collective-permute-done.1.refs_3_
  12.4 0.0 collective-permute-done.2.refs_4_
  12.4 0.0 collective-permute-done.3.refs_5_
  12.4 2.9 %shard_map.64 = (bf16[704,2048]{1,0:T(8,128)(2,1)S(1)}, bf16[704,2048]{1,0:T(8,128)(2,1)S(1)}, bf16[704,2048]{1,0:T(8,128)(2,1)S(1)}, f32[8,128]{1,0:T(8,128)S(1)}) custom-call(bf16[352,2048]{1,0:T(8,128)(2,1)} %bitcast.7, bf16[352,2048]{1,0:T(8,128)(2,1)} %bitcast.9, bf16[352,2048]{1,0:T(8,128)(2,1)} %bitcast.11, ...), custom_call_target="tpu_custom_call" | custom-call | bytes 8650752 | tf_op jit(solution)/shard_map/pallas_call | solution.py:183
  15.3 0.4 collective-permute-done.5.refs_0_
  15.7 1.6 %collective-permute-done.7.refs_4_ = bf16[32,2176]{1,0:T(8,128)(2,1)} collective-permute-done((bf16[32,2176]{1,0:T(8,128)(2,1)S(1)}, bf16[32,2176]{1,0:T(8,128)(2,1)}, u32[]{:S(2)}, u32[]{:S(2)}) %collective-permute-start.7) | collective-permute-done | bytes 139296 | tf_op jit(solution)/shard_map/ppermute | solution.py:260
  17.3 1.6 %collective-permute-start.8 = (bf16[32,2176]{1,0:T(8,128)(2,1)S(1)}, bf16[32,2176]{1,0:T(8,128)(2,1)S(1)}, u32[]{:S(2)}, u32[]{:S(2)}) collective-permute-start(bf16[32,2176]{1,0:T(8,128)(2,1)S(1)} %collective-permute-done.5.refs_0_), channel_id=1, source_target_pairs={{0,4},{4,8},{8,12},{12,14},{14,10},{10,6},{6,2},{2,0},{1,5},{5,9},... | collective-permute-start | bytes 417800 | tf_op jit(solution)/shard_map/ppermute | solution.py:257
  18.9 0.4 collective-permute-start.9
  19.4 3.4 %shard_map.67 = (bf16[32,2048]{1,0:T(8,128)(2,1)S(1)}, bf16[32,2048]{1,0:T(8,128)(2,1)S(1)}, bf16[32,2048]{1,0:T(8,128)(2,1)S(1)}, bf16[32,2048]{1,0:T(8,128)(2,...) custom-call(f32[8,128]{1,0:T(8,128)S(1)} %get-tuple-element.42._, ...), custom_call_target="tpu_custom_call" | custom-call | flops 1384120320 | bytes 8650752 | tf_op jit(solution)/shard_map/pallas_call | solution.py:224
  22.8 0.0 collective-permute-done.8.refs_0_
  22.8 1.4 %collective-permute-done.9.refs_1_ = bf16[32,2176]{1,0:T(8,128)(2,1)S(1)} collective-permute-done((bf16[32,2176]{1,0:T(8,128)(2,1)}, bf16[32,2176]{1,0:T(8,128)(2,1)S(1)}, u32[]{:S(2)}, u32[]{:S(2)}) %collective-permute-start.9) | collective-permute-done | bytes 139296 | tf_op jit(solution)/shard_map/ppermute | solution.py:260
  24.2 1.6 %collective-permute-start.10 = (bf16[16,2176]{1,0:T(8,128)(2,1)S(1)}, bf16[16,2176]{1,0:T(8,128)(2,1)S(1)}, u32[]{:S(2)}, u32[]{:S(2)}) collective-permute-start(bf16[16,2176]{1,0:T(8,128)(2,1)S(1)} %slice.34), channel_id=1, source_target_pairs={{0,4},{4,8},{8,12},{12,14},{14,10},{10,6},{6,2},{2,0},{1,5},{5,9},... | collective-permute-start | bytes 208904 | tf_op jit(solution)/shard_map/ppermute | solution.py:257
  25.8 0.4 collective-permute-start.11
  26.2 2.3 %shard_map.68 = (bf16[32,2048]{1,0:T(8,128)(2,1)S(1)}, bf16[32,2048]{1,0:T(8,128)(2,1)S(1)}, f32[8,128]{1,0:T(8,128)S(1)}) custom-call(f32[8,128]{1,0:T(8,128)S(1)} %get-tuple-element.52._, f32[1,128]{1,0:T(1,128)S(1)} %compare_select_fusion.select_ref, bf16[32,2176]{1,0:T(8,128)(2,1)S(1)} %collective-permute-done.8.refs_0_, ...), custom_call_target="tpu_custom_call" | custom-call | flops 553648128 | bytes 8650752 | tf_op jit(solution)/shard_map/pallas_call | solution.py:224
  28.6 0.0 collective-permute-done.10.refs_0_
  28.6 1.5 %collective-permute-done.11.refs_1_ = bf16[16,2176]{1,0:T(8,128)(2,1)S(1)} collective-permute-done((bf16[16,2176]{1,0:T(8,128)(2,1)S(1)}, bf16[16,2176]{1,0:T(8,128)(2,1)S(1)}, u32[]{:S(2)}, u32[]{:S(2)}) %collective-permute-start.11) | collective-permute-done | bytes 69664 | tf_op jit(solution)/shard_map/ppermute | solution.py:260
  30.1 2.7 %shard_map.69 = (bf16[16,2048]{1,0:T(8,128)(2,1)S(1)}, bf16[16,2048]{1,0:T(8,128)(2,1)S(1)}, f32[8,128]{1,0:T(8,128)}) custom-call(f32[8,128]{1,0:T(8,128)S(1)} %get-tuple-element.57._, f32[1,128]{1,0:T(1,128)S(1)} %compare_select_fusion.select_ref, bf16[16,2176]{1,0:T(8,128)(2,1)S(1)} %collective-permute-done.10.refs_0_, ...), custom_call_target="tpu_custom_call" | custom-call | flops 276824064 | bytes 8650752 | tf_op jit(solution)/shard_map/pallas_call | solution.py:224
  32.8 1.5 %collective-permute-start.12 = (bf16[16,2048]{1,0:T(8,128)(2,1)S(1)}, bf16[16,2048]{1,0:T(8,128)(2,1)S(1)}, u32[]{:S(2)}, u32[]{:S(2)}) collective-permute-start(bf16[16,2048]{1,0:T(8,128)(2,1)S(1)} %get-tuple-element.60), channel_id=1, source_target_pairs={{0,4},{4,8},{8,12},{12,14},{14,10},{10,6},{6,2},{2,0},{1,5},{5,9},... | collective-permute-start | bytes 196616 | tf_op jit(solution)/shard_map/ppermute | solution.py:257
  34.3 0.6 %collective-permute-start.16 = (bf16[16,2048]{1,0:T(8,128)(2,1)S(1)}, bf16[16,2048]{1,0:T(8,128)(2,1)S(1)}, u32[]{:S(2)}, u32[]{:S(2)}) collective-permute-start(bf16[16,2048]{1,0:T(8,128)(2,1)S(1)} %get-tuple-element.64), channel_id=1, source_target_pairs={{4,0},{8,4},{12,8},{14,12},{10,14},{6,10},{2,6},{0,2},{5,1},{9,5},... | collective-permute-start | bytes 196616 | tf_op jit(solution)/shard_map/ppermute | solution.py:260
  34.9 2.2 %collective-permute-done.12 = bf16[16,2048]{1,0:T(8,128)(2,1)S(1)} collective-permute-done((bf16[16,2048]{1,0:T(8,128)(2,1)S(1)}, bf16[16,2048]{1,0:T(8,128)(2,1)S(1)}, u32[]{:S(2)}, u32[]{:S(2)}) %collective-permute-start.12) | collective-permute-done | bytes 65568 | tf_op jit(solution)/shard_map/ppermute | solution.py:257
  37.1 1.5 %collective-permute-start.13 = (bf16[32,2048]{1,0:T(8,128)(2,1)S(1)}, bf16[32,2048]{1,0:T(8,128)(2,1)S(1)}, u32[]{:S(2)}, u32[]{:S(2)}) collective-permute-start(bf16[32,2048]{1,0:T(8,128)(2,1)S(1)} %pad_maximum_fusion), channel_id=1, source_target_pairs={{0,4},{4,8},{8,12},{12,14},{14,10},{10,6},{6,2},{2,0},{1,5},{5,9},... | collective-permute-start | bytes 393224 | tf_op jit(solution)/shard_map/ppermute | solution.py:257
  38.7 0.0 collective-permute-done.16
  38.7 0.6 %collective-permute-start.17 = (bf16[32,2048]{1,0:T(8,128)(2,1)S(1)}, bf16[32,2048]{1,0:T(8,128)(2,1)S(1)}, u32[]{:S(2)}, u32[]{:S(2)}) collective-permute-start(bf16[32,2048]{1,0:T(8,128)(2,1)S(1)} %pad_maximum_fusion.1), channel_id=1, source_target_pairs={{4,0},{8,4},{12,8},{14,12},{10,14},{6,10},{2,6},{0,2},{5,1},{9,5},... | collective-permute-start | bytes 393224 | tf_op jit(solution)/shard_map/ppermute | solution.py:260
  39.3 2.8 %collective-permute-done.13 = bf16[32,2048]{1,0:T(8,128)(2,1)S(1)} collective-permute-done((bf16[32,2048]{1,0:T(8,128)(2,1)S(1)}, bf16[32,2048]{1,0:T(8,128)(2,1)S(1)}, u32[]{:S(2)}, u32[]{:S(2)}) %collective-permute-start.13) | collective-permute-done | bytes 131104 | tf_op jit(solution)/shard_map/ppermute | solution.py:257
  42.2 1.5 %collective-permute-start.14 = (bf16[32,2048]{1,0:T(8,128)(2,1)S(1)}, bf16[32,2048]{1,0:T(8,128)(2,1)S(1)}, u32[]{:S(2)}, u32[]{:S(2)}) collective-permute-start(bf16[32,2048]{1,0:T(8,128)(2,1)S(1)} %add_convert_fusion.4), channel_id=1, source_target_pairs={{0,4},{4,8},{8,12},{12,14},{14,10},{10,6},{6,2},{2,0},{1,5},{5,9},... | collective-permute-start | bytes 393224 | tf_op jit(solution)/shard_map/ppermute | solution.py:257
  43.7 0.0 collective-permute-done.17
  43.8 0.6 %collective-permute-start.18 = (bf16[32,2048]{1,0:T(8,128)(2,1)S(1)}, bf16[32,2048]{1,0:T(8,128)(2,1)S(1)}, u32[]{:S(2)}, u32[]{:S(2)}) collective-permute-start(bf16[32,2048]{1,0:T(8,128)(2,1)S(1)} %add_convert_fusion.2), channel_id=1, source_target_pairs={{4,0},{8,4},{12,8},{14,12},{10,14},{6,10},{2,6},{0,2},{5,1},{9,5},... | collective-permute-start | bytes 393224 | tf_op jit(solution)/shard_map/ppermute | solution.py:260
  44.4 2.8 %collective-permute-done.14 = bf16[32,2048]{1,0:T(8,128)(2,1)S(1)} collective-permute-done((bf16[32,2048]{1,0:T(8,128)(2,1)S(1)}, bf16[32,2048]{1,0:T(8,128)(2,1)S(1)}, u32[]{:S(2)}, u32[]{:S(2)}) %collective-permute-start.14) | collective-permute-done | bytes 131104 | tf_op jit(solution)/shard_map/ppermute | solution.py:257
  47.2 1.5 %collective-permute-start.15 = (bf16[32,2048]{1,0:T(8,128)(2,1)S(1)}, bf16[32,2048]{1,0:T(8,128)(2,1)S(1)}, u32[]{:S(2)}, u32[]{:S(2)}) collective-permute-start(bf16[32,2048]{1,0:T(8,128)(2,1)S(1)} %add_convert_fusion.3), channel_id=1, source_target_pairs={{0,4},{4,8},{8,12},{12,14},{14,10},{10,6},{6,2},{2,0},{1,5},{5,9},... | collective-permute-start | bytes 393224 | tf_op jit(solution)/shard_map/ppermute | solution.py:257
  48.8 0.0 collective-permute-done.18
  48.8 0.6 %collective-permute-start.19 = (bf16[32,2048]{1,0:T(8,128)(2,1)S(1)}, bf16[32,2048]{1,0:T(8,128)(2,1)S(1)}, u32[]{:S(2)}, u32[]{:S(2)}) collective-permute-start(bf16[32,2048]{1,0:T(8,128)(2,1)S(1)} %add_convert_fusion.1), channel_id=1, source_target_pairs={{4,0},{8,4},{12,8},{14,12},{10,14},{6,10},{2,6},{0,2},{5,1},{9,5},... | collective-permute-start | bytes 393224 | tf_op jit(solution)/shard_map/ppermute | solution.py:260
  49.4 2.8 %collective-permute-done.15 = bf16[32,2048]{1,0:T(8,128)(2,1)S(1)} collective-permute-done((bf16[32,2048]{1,0:T(8,128)(2,1)S(1)}, bf16[32,2048]{1,0:T(8,128)(2,1)S(1)}, u32[]{:S(2)}, u32[]{:S(2)}) %collective-permute-start.15) | collective-permute-done | bytes 131104 | tf_op jit(solution)/shard_map/ppermute | solution.py:257
  52.3 1.6 %collective-permute-done.19 = bf16[32,2048]{1,0:T(8,128)(2,1)S(1)} collective-permute-done((bf16[32,2048]{1,0:T(8,128)(2,1)S(1)}, bf16[32,2048]{1,0:T(8,128)(2,1)S(1)}, u32[]{:S(2)}, u32[]{:S(2)}) %collective-permute-start.19) | collective-permute-done | bytes 131104 | tf_op jit(solution)/shard_map/ppermute | solution.py:260
  53.8 0.1 add_convert_fusion
  53.9 0.1 collective-permute-start.20
  54.0 1.2 %collective-permute-done.20 = bf16[32,1024]{1,0:T(8,128)(2,1)S(1)} collective-permute-done((bf16[32,1024]{1,0:T(8,128)(2,1)S(1)}, bf16[32,1024]{1,0:T(8,128)(2,1)S(1)}, u32[]{:S(2)}, u32[]{:S(2)}) %collective-permute-start.20) | collective-permute-done | bytes 65568 | tf_op jit(solution)/shard_map/ppermute | solution.py:313
  55.3 0.7 %pad_maximum_fusion.2 = bf16[64,1024]{1,0:T(8,128)(2,1)} fusion(bf16[32,1024]{1,0:T(8,128)(2,1)S(1)} %get-tuple-element.66, bf16[32,1024]{1,0:T(8,128)(2,1)S(1)} %get-tuple-element.65), kind=kLoop, calls=%fused_computation.7 | loop fusion | flops 262144 | bytes 262144 | tf_op jit(solution)/shard_map/concatenate | solution.py:314
  (16 shorter events, 0.3 us)
Async XLA Ops:
  0.0 1.6 %collective-permute-start = (bf16[64,1024]{1,0:T(8,128)(2,1)}, bf16[64,1024]{1,0:T(8,128)(2,1)S(1)}, u32[]{:S(2)}, u32[]{:S(2)}) collective-permute-start(bf16[64,1024]{1,0:T(8,128)(2,1)} %tokens_hbm.1), channel_id=1, source_target_pairs={{0,1},{1,0},{2,3},{3,2},{4,5},{5,4},{6,7},{7,6},{8,9},{9,8},{10,11... | collective-permute-start | bytes 393224 | tf_op jit(solution)/shard_map/ppermute | solution.py:263
  1.7 10.7 %collective-permute-start.1 = (bf16[352,2048]{1,0:T(8,128)(2,1)}, bf16[352,2048]{1,0:T(8,128)(2,1)S(1)}, u32[]{:S(2)}, u32[]{:S(2)}) collective-permute-start(bf16[352,2048]{1,0:T(8,128)(2,1)} %bitcast.6), channel_id=1, source_target_pairs={{0,1},{1,0},{2,3},{3,2},{4,5},{5,4},{6,7},{7,6},{8,9},{9,8},{10,11... | collective-permute-start | bytes 4325384 | tf_op jit(solution)/shard_map/ppermute | solution.py:267
  2.0 10.4 %collective-permute-start.2 = (bf16[352,2048]{1,0:T(8,128)(2,1)}, bf16[352,2048]{1,0:T(8,128)(2,1)S(1)}, u32[]{:S(2)}, u32[]{:S(2)}) collective-permute-start(bf16[352,2048]{1,0:T(8,128)(2,1)} %bitcast.8), channel_id=1, source_target_pairs={{0,1},{1,0},{2,3},{3,2},{4,5},{5,4},{6,7},{7,6},{8,9},{9,8},{10,11... | collective-permute-start | bytes 4325384 | tf_op jit(solution)/shard_map/ppermute | solution.py:267
  2.2 10.2 %collective-permute-start.3 = (bf16[352,2048]{1,0:T(8,128)(2,1)}, bf16[352,2048]{1,0:T(8,128)(2,1)}, u32[]{:S(2)}, u32[]{:S(2)}) collective-permute-start(bf16[352,2048]{1,0:T(8,128)(2,1)} %bitcast.10), channel_id=1, source_target_pairs={{0,1},{1,0},{2,3},{3,2},{4,5},{5,4},{6,7},{7,6},{8,9},{9,8},{10,11... | collective-permute-start | bytes 4325384 | tf_op jit(solution)/shard_map/ppermute | solution.py:267
  3.5 6.9 %collective-permute-start.4 = (bf16[32,2176]{1,0:T(8,128)(2,1)S(1)}, bf16[32,2176]{1,0:T(8,128)(2,1)S(1)}, u32[]{:S(2)}, u32[]{:S(2)}) collective-permute-start(bf16[32,2176]{1,0:T(8,128)(2,1)S(1)} %shard_map.66.refs_2_), channel_id=1, source_target_pairs={{0,4},{4,8},{8,12},{12,14},{14,10},{10,6},{6,2},{2,0},{1,5},{5,9},... | collective-permute-start | bytes 417800 | tf_op jit(solution)/shard_map/ppermute | solution.py:257
  6.2 5.9 %collective-permute-start.6 = (bf16[32,2176]{1,0:T(8,128)(2,1)S(1)}, bf16[32,2176]{1,0:T(8,128)(2,1)S(1)}, u32[]{:S(2)}, u32[]{:S(2)}) collective-permute-start(bf16[32,2176]{1,0:T(8,128)(2,1)S(1)} %shard_map.66.refs_2_), channel_id=1, source_target_pairs={{4,0},{8,4},{12,8},{14,12},{10,14},{6,10},{2,6},{0,2},{5,1},{9,5},... | collective-permute-start | bytes 417800 | tf_op jit(solution)/shard_map/ppermute | solution.py:260
  10.3 5.4 %collective-permute-start.5 = (bf16[32,2176]{1,0:T(8,128)(2,1)S(1)}, bf16[32,2176]{1,0:T(8,128)(2,1)S(1)}, u32[]{:S(2)}, u32[]{:S(2)}) collective-permute-start(bf16[32,2176]{1,0:T(8,128)(2,1)S(1)} %collective-permute-done.4.refs_1_), channel_id=1, source_target_pairs={{0,4},{4,8},{8,12},{12,14},{14,10},{10,6},{6,2},{2,0},{1,5},{5,9},... | collective-permute-start | bytes 417800 | tf_op jit(solution)/shard_map/ppermute | solution.py:257
  12.2 5.2 %collective-permute-start.7 = (bf16[32,2176]{1,0:T(8,128)(2,1)S(1)}, bf16[32,2176]{1,0:T(8,128)(2,1)}, u32[]{:S(2)}, u32[]{:S(2)}) collective-permute-start(bf16[32,2176]{1,0:T(8,128)(2,1)S(1)} %collective-permute-done.6.refs_3_), channel_id=1, source_target_pairs={{4,0},{8,4},{12,8},{14,12},{10,14},{6,10},{2,6},{0,2},{5,1},{9,5},... | collective-permute-start | bytes 417800 | tf_op jit(solution)/shard_map/ppermute | solution.py:260
  17.3 5.5 %collective-permute-start.8 = (bf16[32,2176]{1,0:T(8,128)(2,1)S(1)}, bf16[32,2176]{1,0:T(8,128)(2,1)S(1)}, u32[]{:S(2)}, u32[]{:S(2)}) collective-permute-start(bf16[32,2176]{1,0:T(8,128)(2,1)S(1)} %collective-permute-done.5.refs_0_), channel_id=1, source_target_pairs={{0,4},{4,8},{8,12},{12,14},{14,10},{10,6},{6,2},{2,0},{1,5},{5,9},... | collective-permute-start | bytes 417800 | tf_op jit(solution)/shard_map/ppermute | solution.py:257
  18.9 5.3 %collective-permute-start.9 = (bf16[32,2176]{1,0:T(8,128)(2,1)}, bf16[32,2176]{1,0:T(8,128)(2,1)S(1)}, u32[]{:S(2)}, u32[]{:S(2)}) collective-permute-start(bf16[32,2176]{1,0:T(8,128)(2,1)} %collective-permute-done.7.refs_4_), channel_id=1, source_target_pairs={{4,0},{8,4},{12,8},{14,12},{10,14},{6,10},{2,6},{0,2},{5,1},{9,5},... | collective-permute-start | bytes 417800 | tf_op jit(solution)/shard_map/ppermute | solution.py:260
  24.2 4.4 %collective-permute-start.10 = (bf16[16,2176]{1,0:T(8,128)(2,1)S(1)}, bf16[16,2176]{1,0:T(8,128)(2,1)S(1)}, u32[]{:S(2)}, u32[]{:S(2)}) collective-permute-start(bf16[16,2176]{1,0:T(8,128)(2,1)S(1)} %slice.34), channel_id=1, source_target_pairs={{0,4},{4,8},{8,12},{12,14},{14,10},{10,6},{6,2},{2,0},{1,5},{5,9},... | collective-permute-start | bytes 208904 | tf_op jit(solution)/shard_map/ppermute | solution.py:257
  25.8 4.3 %collective-permute-start.11 = (bf16[16,2176]{1,0:T(8,128)(2,1)S(1)}, bf16[16,2176]{1,0:T(8,128)(2,1)S(1)}, u32[]{:S(2)}, u32[]{:S(2)}) collective-permute-start(bf16[16,2176]{1,0:T(8,128)(2,1)S(1)} %slice.35), channel_id=1, source_target_pairs={{4,0},{8,4},{12,8},{14,12},{10,14},{6,10},{2,6},{0,2},{5,1},{9,5},... | collective-permute-start | bytes 208904 | tf_op jit(solution)/shard_map/ppermute | solution.py:260
  32.8 4.3 %collective-permute-start.12 = (bf16[16,2048]{1,0:T(8,128)(2,1)S(1)}, bf16[16,2048]{1,0:T(8,128)(2,1)S(1)}, u32[]{:S(2)}, u32[]{:S(2)}) collective-permute-start(bf16[16,2048]{1,0:T(8,128)(2,1)S(1)} %get-tuple-element.60), channel_id=1, source_target_pairs={{0,4},{4,8},{8,12},{12,14},{14,10},{10,6},{6,2},{2,0},{1,5},{5,9},... | collective-permute-start | bytes 196616 | tf_op jit(solution)/shard_map/ppermute | solution.py:257
  34.3 4.3 %collective-permute-start.16 = (bf16[16,2048]{1,0:T(8,128)(2,1)S(1)}, bf16[16,2048]{1,0:T(8,128)(2,1)S(1)}, u32[]{:S(2)}, u32[]{:S(2)}) collective-permute-start(bf16[16,2048]{1,0:T(8,128)(2,1)S(1)} %get-tuple-element.64), channel_id=1, source_target_pairs={{4,0},{8,4},{12,8},{14,12},{10,14},{6,10},{2,6},{0,2},{5,1},{9,5},... | collective-permute-start | bytes 196616 | tf_op jit(solution)/shard_map/ppermute | solution.py:260
  37.1 5.0 %collective-permute-start.13 = (bf16[32,2048]{1,0:T(8,128)(2,1)S(1)}, bf16[32,2048]{1,0:T(8,128)(2,1)S(1)}, u32[]{:S(2)}, u32[]{:S(2)}) collective-permute-start(bf16[32,2048]{1,0:T(8,128)(2,1)S(1)} %pad_maximum_fusion), channel_id=1, source_target_pairs={{0,4},{4,8},{8,12},{12,14},{14,10},{10,6},{6,2},{2,0},{1,5},{5,9},... | collective-permute-start | bytes 393224 | tf_op jit(solution)/shard_map/ppermute | solution.py:257
  38.7 5.0 %collective-permute-start.17 = (bf16[32,2048]{1,0:T(8,128)(2,1)S(1)}, bf16[32,2048]{1,0:T(8,128)(2,1)S(1)}, u32[]{:S(2)}, u32[]{:S(2)}) collective-permute-start(bf16[32,2048]{1,0:T(8,128)(2,1)S(1)} %pad_maximum_fusion.1), channel_id=1, source_target_pairs={{4,0},{8,4},{12,8},{14,12},{10,14},{6,10},{2,6},{0,2},{5,1},{9,5},... | collective-permute-start | bytes 393224 | tf_op jit(solution)/shard_map/ppermute | solution.py:260
  42.2 5.0 %collective-permute-start.14 = (bf16[32,2048]{1,0:T(8,128)(2,1)S(1)}, bf16[32,2048]{1,0:T(8,128)(2,1)S(1)}, u32[]{:S(2)}, u32[]{:S(2)}) collective-permute-start(bf16[32,2048]{1,0:T(8,128)(2,1)S(1)} %add_convert_fusion.4), channel_id=1, source_target_pairs={{0,4},{4,8},{8,12},{12,14},{14,10},{10,6},{6,2},{2,0},{1,5},{5,9},... | collective-permute-start | bytes 393224 | tf_op jit(solution)/shard_map/ppermute | solution.py:257
  43.8 5.0 %collective-permute-start.18 = (bf16[32,2048]{1,0:T(8,128)(2,1)S(1)}, bf16[32,2048]{1,0:T(8,128)(2,1)S(1)}, u32[]{:S(2)}, u32[]{:S(2)}) collective-permute-start(bf16[32,2048]{1,0:T(8,128)(2,1)S(1)} %add_convert_fusion.2), channel_id=1, source_target_pairs={{4,0},{8,4},{12,8},{14,12},{10,14},{6,10},{2,6},{0,2},{5,1},{9,5},... | collective-permute-start | bytes 393224 | tf_op jit(solution)/shard_map/ppermute | solution.py:260
  47.2 5.0 %collective-permute-start.15 = (bf16[32,2048]{1,0:T(8,128)(2,1)S(1)}, bf16[32,2048]{1,0:T(8,128)(2,1)S(1)}, u32[]{:S(2)}, u32[]{:S(2)}) collective-permute-start(bf16[32,2048]{1,0:T(8,128)(2,1)S(1)} %add_convert_fusion.3), channel_id=1, source_target_pairs={{0,4},{4,8},{8,12},{12,14},{14,10},{10,6},{6,2},{2,0},{1,5},{5,9},... | collective-permute-start | bytes 393224 | tf_op jit(solution)/shard_map/ppermute | solution.py:257
  48.8 5.0 %collective-permute-start.19 = (bf16[32,2048]{1,0:T(8,128)(2,1)S(1)}, bf16[32,2048]{1,0:T(8,128)(2,1)S(1)}, u32[]{:S(2)}, u32[]{:S(2)}) collective-permute-start(bf16[32,2048]{1,0:T(8,128)(2,1)S(1)} %add_convert_fusion.1), channel_id=1, source_target_pairs={{4,0},{8,4},{12,8},{14,12},{10,14},{6,10},{2,6},{0,2},{5,1},{9,5},... | collective-permute-start | bytes 393224 | tf_op jit(solution)/shard_map/ppermute | solution.py:260
  53.9 1.3 %collective-permute-start.20 = (bf16[32,1024]{1,0:T(8,128)(2,1)S(1)}, bf16[32,1024]{1,0:T(8,128)(2,1)S(1)}, u32[]{:S(2)}, u32[]{:S(2)}) collective-permute-start(bf16[32,1024]{1,0:T(8,128)(2,1)S(1)} %broadcast_select_fusion.2), channel_id=1, source_target_pairs={{0,1},{1,0},{2,3},{3,2},{4,5},{5,4},{6,7},{7,6},{8,9},{9,8},{10,11... | collective-permute-start | bytes 196616 | tf_op jit(solution)/shard_map/ppermute | solution.py:313

commit v4 on v3

--- a/solution.py
+++ b/solution.py
@@ -10,8 +10,19 @@
 LANES = 128
 PIECES = 3
 VMEM_LIMIT = 16 * 2**20
-SMALL_LIMIT = 4 * 2**20
+SMALL_LIMIT = 1 * 2**20
 MARK = (8, 128)
+
+
+def cost(size):
+    return pl.CostEstimate(flops=0, bytes_accessed=size, transcendentals=0)
+
+
+NO_COST = cost(1)
+GATHER_COST = 1
+TOUCH_COST = 1
+EXPERT_COST = 1
+ADD_COST = 1
 
 
 def sparse_local(tokens, expert_ids, gate_scores, gate_proj, up_proj, down_proj):
@@ -126,9 +137,7 @@
             pltpu.SemaphoreType.DMA((3,)),
         ],
         compiler_params=pltpu.CompilerParams(vmem_limit_bytes=SMALL_LIMIT),
-        cost_estimate=pl.CostEstimate(
-            flops=0, bytes_accessed=3 * rows * half_width, transcendentals=0
-        ),
+        cost_estimate=NO_COST,
     )(head.reshape(1), hbm(tokens), hbm(expert_ids.T), hbm(gate_scores.T))
 
 
@@ -149,13 +158,11 @@
         in_specs=[pl.BlockSpec(memory_space=pltpu.SMEM)] + [in_vmem()] * 3,
         out_specs=in_vmem(),
         compiler_params=pltpu.CompilerParams(vmem_limit_bytes=SMALL_LIMIT),
-        cost_estimate=pl.CostEstimate(
-            flops=0, bytes_accessed=8 * part * half_width, transcendentals=0
-        ),
+        cost_estimate=NO_COST,
     )(head.reshape(1), mine, got, lanes)
 
 
-def gather_kernel(count, *refs):
+def gather_kernel(count, _, *refs):
     kept, came = refs[:count], refs[count : 2 * count]
     outs, mark, sems = refs[2 * count : 3 * count], refs[3 * count], refs[3 * count + 1]
     copies = []
@@ -177,28 +184,43 @@
         copy.wait()
 
 
-def gather_weights(kept, came):
+def gather_weights(mark, kept, came):
     count = len(kept)
     units, width = kept[0].shape
     *whole, mark = pl.pallas_call(
         functools.partial(gather_kernel, count),
         out_shape=[jax.ShapeDtypeStruct((2 * units, width), jnp.bfloat16)] * count
         + [jax.ShapeDtypeStruct(MARK, jnp.float32)],
-        in_specs=[in_hbm()] * count + [pl.BlockSpec(memory_space=pl.ANY)] * count,
+        in_specs=[pl.BlockSpec(memory_space=pl.ANY)]
+        + [in_hbm()] * count
+        + [pl.BlockSpec(memory_space=pl.ANY)] * count,
         out_specs=[in_vmem()] * (count + 1),
         scratch_shapes=[pltpu.SemaphoreType.DMA((count, 3))],
         compiler_params=pltpu.CompilerParams(vmem_limit_bytes=SMALL_LIMIT),
-        cost_estimate=pl.CostEstimate(
-            flops=0, bytes_accessed=4 * count * units * width, transcendentals=0
-        ),
-    )(*[hbm(w) for w in kept], *came)
+        cost_estimate=cost(GATHER_COST),
+    )(mark, *[hbm(w) for w in kept], *came)
     return whole, mark
 
 
-def expert_kernel(counts, _, select_ref, *refs):
-    blocks = refs[: len(counts)]
-    wg, wu, wd = refs[len(counts) : len(counts) + 3]
-    outs = refs[len(counts) + 3 : -1]
+def touch_kernel(*refs):
+    refs[-1][...] = jnp.zeros(refs[-1].shape, refs[-1].dtype)
+
+
+def touch(*values):
+    return pl.pallas_call(
+        touch_kernel,
+        out_shape=jax.ShapeDtypeStruct(MARK, jnp.float32),
+        in_specs=[pl.BlockSpec(memory_space=pl.ANY)] * len(values),
+        out_specs=in_vmem(),
+        compiler_params=pltpu.CompilerParams(vmem_limit_bytes=SMALL_LIMIT),
+        cost_estimate=cost(TOUCH_COST),
+    )(*values)
+
+
+def expert_kernel(count, _, select_ref, *refs):
+    blocks = refs[:count]
+    wg, wu, wd = refs[count : count + 3]
+    outs = refs[count + 3 : -1]
     mark = refs[-1]
     width = wg.shape[1]
     whole = [b[...] for b in blocks]
@@ -212,30 +234,48 @@
     total = jnp.dot(hidden, wd[...], preferred_element_type=jnp.float32)
     scaled = (total * scale).astype(jnp.bfloat16)
     start = 0
-    for count, out in zip(counts, outs):
-        out[...] = scaled[start : start + count]
-        start += count
+    for out in outs:
+        out[...] = scaled[start : start + out.shape[0]]
+        start += out.shape[0]
     mark[...] = jnp.zeros(mark.shape, mark.dtype)
 
 
-def run_expert(mark, blocks, select, weights):
-    counts = tuple(b.shape[0] for b in blocks)
+def run_expert(mark, groups, select, weights):
+    blocks = [b for group in groups for b in group]
+    counts = [sum(b.shape[0] for b in group) for group in groups]
     units, width = weights[0].shape
     *outs, mark = pl.pallas_call(
-        functools.partial(expert_kernel, counts),
+        functools.partial(expert_kernel, len(blocks)),
         out_shape=[jax.ShapeDtypeStruct((c, width), jnp.bfloat16) for c in counts]
         + [jax.ShapeDtypeStruct(MARK, jnp.float32)],
         in_specs=[pl.BlockSpec(memory_space=pl.ANY)]
         + [in_vmem()] * (1 + len(blocks) + len(weights)),
-        out_specs=[in_vmem()] * (len(blocks) + 1),
+        out_specs=[in_vmem()] * (len(groups) + 1),
         compiler_params=pltpu.CompilerParams(vmem_limit_bytes=VMEM_LIMIT),
-        cost_estimate=pl.CostEstimate(
-            flops=6 * sum(counts) * units * width,
-            bytes_accessed=6 * units * width,
-            transcendentals=sum(counts) * units,
-        ),
+        cost_estimate=cost(EXPERT_COST),
     )(mark, select, *blocks, *weights)
     return outs, mark
+
+
+def add_kernel(_, a_ref, b_ref, out_ref, mark):
+    out_ref[...] = (a_ref[...].astype(jnp.float32) + b_ref[...].astype(jnp.float32)).astype(
+        jnp.bfloat16
+    )
+    mark[...] = jnp.zeros(mark.shape, mark.dtype)
+
+
+def add_rows(mark, a, b):
+    return pl.pallas_call(
+        add_kernel,
+        out_shape=[
+            jax.ShapeDtypeStruct(a.shape, jnp.bfloat16),
+            jax.ShapeDtypeStruct(MARK, jnp.float32),
+        ],
+        in_specs=[pl.BlockSpec(memory_space=pl.ANY)] + [in_vmem()] * 2,
+        out_specs=[in_vmem()] * 2,
+        compiler_params=pltpu.CompilerParams(vmem_limit_bytes=SMALL_LIMIT),
+        cost_estimate=cost(ADD_COST),
+    )(mark, a, b)
 
 
 def after(mark, *values):
@@ -249,65 +289,59 @@
     tok_rows, half_width = tokens.shape
     part = tok_rows // 2
     swap = ((0, 1), (1, 0))
-    order = list(range(0, n, 2)) + list(range(n - 1, 0, -2))
-    ahead = [(order[i], order[(i + 1) % n]) for i in range(n)]
-    behind = [(b, a) for a, b in ahead]
-
-    def forth(v):
-        return lax.ppermute(v, "wide", ahead)
-
-    def back(v):
-        return lax.ppermute(v, "wide", behind)
+
+    def pair(v):
+        return lax.ppermute(v, "wide", [(w, w ^ 1) for w in range(n)])
+
+    def column(v, k):
+        return lax.ppermute(v, "wide", [(w, w ^ (2 * k)) for w in range(n)])
+
+    def add(*terms):
+        return sum(t.astype(jnp.float32) for t in terms).astype(jnp.bfloat16)
 
     first = head == 0
     got = lax.ppermute(tokens, "head", swap)
     mine, lanes = spread(head, tokens, expert_ids, gate_scores)
     kept = (gate_proj[0], up_proj[0], down_proj[0])
-    got, *kept = after(got, *kept)
-    came = [lax.ppermute(w, "head", swap) for w in kept]
+    lanes, got = after(lanes, got)
     own = join(head, mine, got, lanes)
     lane = jnp.arange(LANES, dtype=jnp.int32)
     select = jnp.where(lane % n == expert, 1.0, 0.0).astype(jnp.float32)[None, :]
 
-    reach = n // 2
-    cut = part // 2
-    near = {0: own}
-    f, b = forth(own), back(own)
-    near[-1], near[1] = f, b
-    weights, mark = gather_weights(kept, came)
-    for k in range(2, reach):
-        f, b = forth(f), back(b)
-        near[-k], near[k] = f, b
-        if k == 2:
-            mark, f, b = after(mark, f, b)
-    sums = {}
-    keys = sorted(i for i in near if abs(i) < reach - 1)
-    done, mark = run_expert(mark, [near[i] for i in keys], select, weights)
-    sums.update(zip(keys, done))
-    mark, f, b = after(mark, f, b)
-    f, b = forth(f[:cut]), back(b[cut:])
-    keys = [1 - reach, reach - 1]
-    done, mark = run_expert(mark, [near[i] for i in keys], select, weights)
-    sums.update(zip(keys, done))
-    mark, f, b = after(mark, f, b)
-    far, _ = run_expert(mark, [f, b], select, weights)
-
-    f, b = forth(far[0]), back(far[1])
-    for k in range(reach - 1, 0, -1):
-        up_sum = sums[k].astype(jnp.float32)
-        down_sum = sums[-k].astype(jnp.float32)
-        if k == reach - 1:
-            up_sum = jnp.concatenate([up_sum[:cut] + f.astype(jnp.float32), up_sum[cut:]], axis=0)
-            down_sum = jnp.concatenate(
-                [down_sum[:cut], down_sum[cut:] + b.astype(jnp.float32)], axis=0
-            )
-        else:
-            up_sum = up_sum + f.astype(jnp.float32)
-            down_sum = down_sum + b.astype(jnp.float32)
-        f, b = forth(up_sum.astype(jnp.bfloat16)), back(down_sum.astype(jnp.bfloat16))
-    mixed = (sums[0].astype(jnp.float32) + f.astype(jnp.float32) + b.astype(jnp.float32)).astype(
-        jnp.bfloat16
-    )
+    last = 2
+    mid = list(range(3, n // 2))
+    got, *held = after(got, *kept)
+    came = [lax.ppermute(w, "head", swap) for w in held]
+    block = {0: own}
+    block.update({k: column(own, k) for k in mid + [1]})
+    over = {0: pair(own), 1: pair(block[1])}
+    block[1], own_again = after(block[1], own)
+    block[last] = column(own_again, last)
+    mark = touch(block[1], *came[:2])
+    for k in mid:
+        mark, block[k] = after(mark, block[k])
+        over[k] = pair(block[k])
+    weights, mark = gather_weights(mark, kept, came)
+    mark, block[last] = after(mark, block[last])
+    over[last] = pair(block[last])
+
+    groups = [[block[0]], [block[1]]] + [[v[k]] for k in mid for v in (block, over)]
+    done, mark = run_expert(mark, groups + [[over[0], over[1]]], select, weights)
+    here = {0: done[0], 1: done[1]}
+    there = {}
+    for i, k in enumerate(mid):
+        here[k] = done[2 + 2 * i]
+        there[k] = pair(done[3 + 2 * i])
+    first_two = pair(done[-1])
+    there[0], there[1] = first_two[:part], first_two[part:]
+    done, mark = run_expert(mark, [[block[last]], [over[last]]], select, weights)
+    here[last] = done[0]
+    there[last] = pair(done[1])
+    returned = []
+    for k in mid + [1, last]:
+        total, mark = add_rows(mark, here[k], there[k])
+        returned.append(column(total, k))
+    mixed = add(here[0], there[0], *returned)
     left, right = mixed[:, :half_width], mixed[:, half_width:]
     keep = jnp.where(first, left, right)
     rest = lax.ppermute(jnp.where(first, right, left), "head", swap)
@@ -318,8 +352,9 @@
 
 def local(tokens, expert_ids, gate_scores, gate_proj, up_proj, down_proj):
     n = lax.axis_size("wide")
-    dense = expert_ids.shape[1] == n and lax.axis_size("head") == 2 and n % 2 == 0
-    if dense and tokens.shape[0] % 64 == 0 and PIECES * n <= LANES:
+    named = expert_ids.shape[1]
+    dense = named == n and n >= 4 and n & (n - 1) == 0 and PIECES * n <= LANES
+    if dense and lax.axis_size("head") == 2 and tokens.shape[0] % 32 == 0:
         return dense_local(tokens, expert_ids, gate_scores, gate_proj, up_proj, down_proj)
     return sparse_local(tokens, expert_ids, gate_scores, gate_proj, up_proj, down_proj)
 

time: 56.1 us -> 51.6 us (0.920)
  waiting for transfers between devices: 23.8 us -> 17 us
  starting transfers between devices: 18.7 us -> 23.1 us
  Pallas kernels: 12.3 us -> 10.4 us
    ppermute x19 -> x16, waiting for transfers between devices: 21.4 us -> 15.5 us  [the longest x6 9.15 us: column(): return lax.ppermute(v, 'wide', [(w, w ^ 2 * k) for w in range(n)])]
    ppermute x19 -> x16, starting transfers between devices: 18.2 us -> 22.6 us  [the longest x6 13 us: column(): return lax.ppermute(v, 'wide', [(w, w ^ 2 * k) for w in range(n)])]
    pallas_call x3 -> x6, Pallas kernels: 8.49 us -> 6.59 us  [the longest x2 5.91 us: run_expert(): pl.pallas_call(functools.partial(expert_kernel, len(blocks)), out_shape=[...]
    ppermute x1, waiting for transfers between devices: 1.2 us -> 0.29 us  [dense_local(): got = lax.ppermute(tokens, 'head', swap)]
  transfers between devices with their start and end apart: 21 -> 18, of which waited for: 12 -> 9; matrix products, arithmetic and copies ran while one was open for 0% -> 0% of each run, Pallas kernels for 17% -> 20%
where the time goes in v4:
time: 51.6 us; the launch traced here: 51.4 us
  starting transfers between devices  23.1 us (45%)
  waiting for transfers between devices  17 us (33%)
  Pallas kernels  10.4 us (20%)
  other arithmetic  0.78 us (2%)
    ppermute x6, starting transfers between devices, column(): return lax.ppermute(v, 'wide', [(w, w ^ 2 * k) for w in range(n)])  13 us
    ppermute x6, waiting for transfers between devices, column(): return lax.ppermute(v, 'wide', [(w, w ^ 2 * k) for w in range(n)])  9.15 us
    ppermute x7, starting transfers between devices, pair(): return lax.ppermute(v, 'wide', [(w, w ^ 1) for w in range(n)])  8.66 us
    ppermute x7, waiting for transfers between devices, pair(): return lax.ppermute(v, 'wide', [(w, w ^ 1) for w in range(n)])  6.35 us
    pallas_call x2, Pallas kernels, run_expert(): pl.pallas_call(functools.partial(expert_kernel, len(blocks)), out_shape=[...  5.91 us
    pallas_call x1, Pallas kernels, gather_weights(): pl.pallas_call(functools.partial(gather_kernel, count), out_shape=[jax.Sh...  2.86 us
    ppermute x1, waiting for transfers between devices, dense_local(): rest = lax.ppermute(jnp.where(first, right, left), 'head', swap)  1.24 us
  transfers between devices with their start and end apart: 18, of which 9 were waited for; matrix products, arithmetic and copies ran while one was open for 0% of the time, Pallas kernels for 20%

profile of v4, /device:TPU:0, one launch (start us, length us, event | category | flops | bytes accessed | tf_op | source)
XLA Modules:
  0.0 51.4 jit_solution(8248531193409680746)
XLA Ops:
  0.0 0.5 collective-permute-start
  0.5 0.9 %shard_map.64 = (bf16[32,1024]{1,0:T(8,128)(2,1)S(1)}, bf16[32,128]{1,0:T(8,128)(2,1)S(1)}) custom-call(s32[1]{0:T(128)} %bitcast.head_ref, bf16[64,1024]{1,0:T(8,128)(2,1)} %tokens_hbm.1, s32[8,64]{1,0:T(8,128)} %bitcast.12, f32[8,64]{1,0:T(8,128)} %bitcast.13), custom_call_target="tpu_custom_call" | custom-call | bytes 1 | tf_op jit(solution)/shard_map/pallas_call | solution.py:126
  1.4 0.3 collective-permute-done.got_ref
  1.7 0.4 collective-permute-start.2
  2.0 0.1 collective-permute-start.3
  2.2 0.4 collective-permute-start.5
  2.5 2.8 %collective-permute-start.1 = (bf16[32,2176]{1,0:T(8,128)(2,1)S(1)}, bf16[32,2176]{1,0:T(8,128)(2,1)S(1)}, u32[]{:S(2)}, u32[]{:S(2)}) collective-permute-start(bf16[32,2176]{1,0:T(8,128)(2,1)S(1)} %shard_map.65.refs_0_), channel_id=1, source_target_pairs={{0,4},{2,6},{4,0},{6,2},{8,12},{10,14},{12,8},{14,10},{1,5},{3,7},... | collective-permute-start | bytes 417800 | tf_op jit(solution)/shard_map/ppermute | solution.py:297
  5.3 2.5 %collective-permute-start.4 = (bf16[32,2176]{1,0:T(8,128)(2,1)S(1)}, bf16[32,2176]{1,0:T(8,128)(2,1)S(1)}, u32[]{:S(2)}, u32[]{:S(2)}) collective-permute-start(bf16[32,2176]{1,0:T(8,128)(2,1)S(1)} %shard_map.65.refs_0_), channel_id=1, source_target_pairs={{0,12},{2,14},{4,8},{6,10},{8,4},{10,6},{12,0},{14,2},{1,13},{3,15... | collective-permute-start | bytes 417800 | tf_op jit(solution)/shard_map/ppermute | solution.py:297
  7.8 1.7 %collective-permute-done.1.refs_0_.refs_1_ = bf16[32,2176]{1,0:T(8,128)(2,1)S(1)} collective-permute-done((bf16[32,2176]{1,0:T(8,128)(2,1)S(1)}, bf16[32,2176]{1,0:T(8,128)(2,1)S(1)}, u32[]{:S(2)}, u32[]{:S(2)}) %collective-permute-start.1) | collective-permute-done | bytes 139296 | tf_op jit(solution)/shard_map/ppermute | solution.py:297
  9.5 3.3 %collective-permute-start.6 = (bf16[32,2176]{1,0:T(8,128)(2,1)S(1)}, bf16[32,2176]{1,0:T(8,128)(2,1)S(1)}, u32[]{:S(2)}, u32[]{:S(2)}) collective-permute-start(bf16[32,2176]{1,0:T(8,128)(2,1)S(1)} %shard_map.65.refs_0_), channel_id=1, source_target_pairs={{0,8},{2,10},{4,12},{6,14},{8,0},{10,2},{12,4},{14,6},{1,9},{3,11}... | collective-permute-start | bytes 417800 | tf_op jit(solution)/shard_map/ppermute | solution.py:297
  12.8 0.0 collective-permute-done.2.refs_1_.refs_3_
  12.8 1.5 %collective-permute-start.8 = (bf16[32,2176]{1,0:T(8,128)(2,1)S(1)}, bf16[32,2176]{1,0:T(8,128)(2,1)}, u32[]{:S(2)}, u32[]{:S(2)}) collective-permute-start(bf16[32,2176]{1,0:T(8,128)(2,1)S(1)} %shard_map.65.refs_0_), channel_id=1, source_target_pairs={{0,2},{2,0},{4,6},{6,4},{8,10},{10,8},{12,14},{14,12},{1,3},{3,1},... | collective-permute-start | bytes 417800 | tf_op jit(solution)/shard_map/ppermute | solution.py:294
  14.3 0.0 collective-permute-done.3.refs_2_.refs_4_
  14.3 0.5 %collective-permute-start.9 = (bf16[32,2176]{1,0:T(8,128)(2,1)S(1)}, bf16[32,2176]{1,0:T(8,128)(2,1)}, u32[]{:S(2)}, u32[]{:S(2)}) collective-permute-start(bf16[32,2176]{1,0:T(8,128)(2,1)S(1)} %collective-permute-done.1.refs_0_.refs_1_), channel_id=1, source_target_pairs={{0,2},{2,0},{4,6},{6,4},{8,10},{10,8},{12,14},{14,12},{1,3},{3,1},... | collective-permute-start | bytes 417800 | tf_op jit(solution)/shard_map/ppermute | solution.py:294
  14.9 0.5 collective-permute-done.4.refs_2_
  15.4 1.5 %collective-permute-start.7 = (bf16[32,2176]{1,0:T(8,128)(2,1)S(1)}, bf16[32,2176]{1,0:T(8,128)(2,1)}, u32[]{:S(2)}, u32[]{:S(2)}) collective-permute-start(bf16[32,2176]{1,0:T(8,128)(2,1)S(1)} %collective-permute-done.4.refs_2_), channel_id=1, source_target_pairs={{0,2},{2,0},{4,6},{6,4},{8,10},{10,8},{12,14},{14,12},{1,3},{3,1},... | collective-permute-start | bytes 417800 | tf_op jit(solution)/shard_map/ppermute | solution.py:294
  16.9 0.0 collective-permute-done.5.refs_5_
  16.9 2.9 %shard_map.67 = (bf16[704,2048]{1,0:T(8,128)(2,1)S(1)}, bf16[704,2048]{1,0:T(8,128)(2,1)S(1)}, bf16[704,2048]{1,0:T(8,128)(2,1)S(1)}, f32[8,128]{1,0:T(8,128)S(1)}) custom-call(f32[8,128]{1,0:T(8,128)S(1)} %shard_map.66._, bf16[352,2048]{1,0:T(8,128)(2,1)} %bitcast.7, bf16[352,2048]{1,0:T(8,128)(2,1)} %bitcast.9, bf16[352,2048]{1,0:T(8,128)(2,1)} %bitcast.11, ...), custom_call_target="tpu_custom_call" | custom-call | bytes 1 | tf_op jit(solution)/shard_map/pallas_call | solution.py:190
  19.7 1.0 %collective-permute-done.6.refs_0_ = bf16[32,2176]{1,0:T(8,128)(2,1)S(1)} collective-permute-done((bf16[32,2176]{1,0:T(8,128)(2,1)S(1)}, bf16[32,2176]{1,0:T(8,128)(2,1)S(1)}, u32[]{:S(2)}, u32[]{:S(2)}) %collective-permute-start.6) | collective-permute-done | bytes 139296 | tf_op jit(solution)/shard_map/ppermute | solution.py:297
  20.7 1.5 %collective-permute-start.11 = (bf16[32,2176]{1,0:T(8,128)(2,1)S(1)}, bf16[32,2176]{1,0:T(8,128)(2,1)S(1)}, u32[]{:S(2)}, u32[]{:S(2)}) collective-permute-start(bf16[32,2176]{1,0:T(8,128)(2,1)S(1)} %collective-permute-done.6.refs_0_), channel_id=1, source_target_pairs={{0,2},{2,0},{4,6},{6,4},{8,10},{10,8},{12,14},{14,12},{1,3},{3,1},... | collective-permute-start | bytes 417800 | tf_op jit(solution)/shard_map/ppermute | solution.py:294
  22.2 0.0 collective-permute-done.8.refs_4_
  22.2 0.0 collective-permute-done.9.refs_5_
  22.2 1.0 %collective-permute-done.7.refs_3_ = bf16[32,2176]{1,0:T(8,128)(2,1)} collective-permute-done((bf16[32,2176]{1,0:T(8,128)(2,1)S(1)}, bf16[32,2176]{1,0:T(8,128)(2,1)}, u32[]{:S(2)}, u32[]{:S(2)}) %collective-permute-start.7) | collective-permute-done | bytes 139296 | tf_op jit(solution)/shard_map/ppermute | solution.py:294
  23.2 3.6 %shard_map.68 = (bf16[32,2048]{1,0:T(8,128)(2,1)S(1)}, bf16[32,2048]{1,0:T(8,128)(2,1)S(1)}, bf16[32,2048]{1,0:T(8,128)(2,1)S(1)}, bf16[32,2048]{1,0:T(8,128)(2,...) custom-call(f32[8,128]{1,0:T(8,128)S(1)} %get-tuple-element.47._, ...), custom_call_target="tpu_custom_call" | custom-call | bytes 1 | tf_op jit(solution)/shard_map/pallas_call | solution.py:247
  26.8 1.6 %collective-permute-start.10 = (bf16[64,2048]{1,0:T(8,128)(2,1)S(1)}, bf16[64,2048]{1,0:T(8,128)(2,1)S(1)}, u32[]{:S(2)}, u32[]{:S(2)}) collective-permute-start(bf16[64,2048]{1,0:T(8,128)(2,1)S(1)} %get-tuple-element.53), channel_id=1, source_target_pairs={{0,2},{2,0},{4,6},{6,4},{8,10},{10,8},{12,14},{14,12},{1,3},{3,1},... | collective-permute-start | bytes 786440 | tf_op jit(solution)/shard_map/ppermute | solution.py:294
  28.3 0.5 %collective-permute-start.12 = (bf16[32,2048]{1,0:T(8,128)(2,1)S(1)}, bf16[32,2048]{1,0:T(8,128)(2,1)S(1)}, u32[]{:S(2)}, u32[]{:S(2)}) collective-permute-start(bf16[32,2048]{1,0:T(8,128)(2,1)S(1)} %get-tuple-element.58), channel_id=1, source_target_pairs={{0,2},{2,0},{4,6},{6,4},{8,10},{10,8},{12,14},{14,12},{1,3},{3,1},... | collective-permute-start | bytes 393224 | tf_op jit(solution)/shard_map/ppermute | solution.py:294
  28.9 0.0 collective-permute-done.11.refs_1_
  28.9 2.3 %shard_map.69 = (bf16[32,2048]{1,0:T(8,128)(2,1)S(1)}, bf16[32,2048]{1,0:T(8,128)(2,1)S(1)}, f32[8,128]{1,0:T(8,128)S(1)}) custom-call(f32[8,128]{1,0:T(8,128)S(1)} %get-tuple-element.54._, f32[1,128]{1,0:T(1,128)S(1)} %compare_select_fusion.select_ref, bf16[32,2176]{1,0:T(8,128)(2,1)S(1)} %collective-permute-done.6.refs_0_, ...), custom_call_target="tpu_custom_call" | custom-call | bytes 1 | tf_op jit(solution)/shard_map/pallas_call | solution.py:247
  31.2 1.6 %collective-permute-start.15 = (bf16[32,2048]{1,0:T(8,128)(2,1)S(1)}, bf16[32,2048]{1,0:T(8,128)(2,1)S(1)}, u32[]{:S(2)}, u32[]{:S(2)}) collective-permute-start(bf16[32,2048]{1,0:T(8,128)(2,1)S(1)} %get-tuple-element.65), channel_id=1, source_target_pairs={{0,2},{2,0},{4,6},{6,4},{8,10},{10,8},{12,14},{14,12},{1,3},{3,1},... | collective-permute-start | bytes 393224 | tf_op jit(solution)/shard_map/ppermute | solution.py:294
  32.8 5.4 %collective-permute-done.12.b_ref = bf16[32,2048]{1,0:T(8,128)(2,1)S(1)} collective-permute-done((bf16[32,2048]{1,0:T(8,128)(2,1)S(1)}, bf16[32,2048]{1,0:T(8,128)(2,1)S(1)}, u32[]{:S(2)}, u32[]{:S(2)}) %collective-permute-start.12) | collective-permute-done | bytes 131104 | tf_op jit(solution)/shard_map/ppermute | solution.py:294
  38.2 1.9 %collective-permute-start.13 = (bf16[32,2048]{1,0:T(8,128)(2,1)S(1)}, bf16[32,2048]{1,0:T(8,128)(2,1)S(1)}, u32[]{:S(2)}, u32[]{:S(2)}) collective-permute-start(bf16[32,2048]{1,0:T(8,128)(2,1)S(1)} %get-tuple-element.59), channel_id=1, source_target_pairs={{0,12},{2,14},{4,8},{6,10},{8,4},{10,6},{12,0},{14,2},{1,13},{3,15... | collective-permute-start | bytes 393224 | tf_op jit(solution)/shard_map/ppermute | solution.py:297
  40.1 0.0 collective-permute-done.10
  40.1 0.0 collective-permute-done.15.b_ref
  40.1 0.6 %shard_map.72 = (bf16[32,2048]{1,0:T(8,128)(2,1)S(1)}, f32[8,128]{1,0:T(8,128)}) custom-call(f32[8,128]{1,0:T(8,128)S(1)} %get-tuple-element.63._, bf16[32,2048]{1,0:T(8,128)(2,1)S(1)} %get-tuple-element.64.a_ref, bf16[32,2048]{1,0:T(8,128)(2,1)S(1)} %collective-permute-done.15.b_ref), custom_call_target="tpu_custom_call" | custom-call | bytes 1 | tf_op jit(solution)/shard_map/pallas_call | solution.py:268
  40.7 0.8 %collective-permute-start.16 = (bf16[32,2048]{1,0:T(8,128)(2,1)S(1)}, bf16[32,2048]{1,0:T(8,128)(2,1)S(1)}, u32[]{:S(2)}, u32[]{:S(2)}) collective-permute-start(bf16[32,2048]{1,0:T(8,128)(2,1)S(1)} %get-tuple-element.66), channel_id=1, source_target_pairs={{0,8},{2,10},{4,12},{6,14},{8,0},{10,2},{12,4},{14,6},{1,9},{3,11}... | collective-permute-start | bytes 393224 | tf_op jit(solution)/shard_map/ppermute | solution.py:297
  41.5 1.8 %collective-permute-start.14 = (bf16[32,2048]{1,0:T(8,128)(2,1)S(1)}, bf16[32,2048]{1,0:T(8,128)(2,1)S(1)}, u32[]{:S(2)}, u32[]{:S(2)}) collective-permute-start(bf16[32,2048]{1,0:T(8,128)(2,1)S(1)} %get-tuple-element.62), channel_id=1, source_target_pairs={{0,4},{2,6},{4,0},{6,2},{8,12},{10,14},{12,8},{14,10},{1,5},{3,7},... | collective-permute-start | bytes 393224 | tf_op jit(solution)/shard_map/ppermute | solution.py:297
  43.3 2.4 %collective-permute-done.13 = bf16[32,2048]{1,0:T(8,128)(2,1)S(1)} collective-permute-done((bf16[32,2048]{1,0:T(8,128)(2,1)S(1)}, bf16[32,2048]{1,0:T(8,128)(2,1)S(1)}, u32[]{:S(2)}, u32[]{:S(2)}) %collective-permute-start.13) | collective-permute-done | bytes 131104 | tf_op jit(solution)/shard_map/ppermute | solution.py:297
  45.7 3.6 %collective-permute-done.16 = bf16[32,2048]{1,0:T(8,128)(2,1)S(1)} collective-permute-done((bf16[32,2048]{1,0:T(8,128)(2,1)S(1)}, bf16[32,2048]{1,0:T(8,128)(2,1)S(1)}, u32[]{:S(2)}, u32[]{:S(2)}) %collective-permute-start.16) | collective-permute-done | bytes 131104 | tf_op jit(solution)/shard_map/ppermute | solution.py:297
  49.3 0.0 collective-permute-done.14
  49.3 0.1 add_convert_fusion
  49.4 0.1 collective-permute-start.17
  49.5 1.2 %collective-permute-done.17 = bf16[32,1024]{1,0:T(8,128)(2,1)S(1)} collective-permute-done((bf16[32,1024]{1,0:T(8,128)(2,1)S(1)}, bf16[32,1024]{1,0:T(8,128)(2,1)S(1)}, u32[]{:S(2)}, u32[]{:S(2)}) %collective-permute-start.17) | collective-permute-done | bytes 65568 | tf_op jit(solution)/shard_map/ppermute | solution.py:347
  50.7 0.7 %pad_maximum_fusion = bf16[64,1024]{1,0:T(8,128)(2,1)} fusion(bf16[32,1024]{1,0:T(8,128)(2,1)S(1)} %get-tuple-element.68, bf16[32,1024]{1,0:T(8,128)(2,1)S(1)} %get-tuple-element.67), kind=kLoop, calls=%fused_computation.1 | loop fusion | flops 262144 | bytes 262144 | tf_op jit(solution)/shard_map/concatenate | solution.py:348
  (8 shorter events, 0.1 us)
Async XLA Ops:
  0.0 1.6 %collective-permute-start = (bf16[64,1024]{1,0:T(8,128)(2,1)}, bf16[64,1024]{1,0:T(8,128)(2,1)S(1)}, u32[]{:S(2)}, u32[]{:S(2)}) collective-permute-start(bf16[64,1024]{1,0:T(8,128)(2,1)} %tokens_hbm.1), channel_id=1, source_target_pairs={{0,1},{1,0},{2,3},{3,2},{4,5},{5,4},{6,7},{7,6},{8,9},{9,8},{10,11... | collective-permute-start | bytes 393224 | tf_op jit(solution)/shard_map/ppermute | solution.py:303
  1.7 11.2 %collective-permute-start.2 = (bf16[352,2048]{1,0:T(8,128)(2,1)}, bf16[352,2048]{1,0:T(8,128)(2,1)S(1)}, u32[]{:S(2)}, u32[]{:S(2)}) collective-permute-start(bf16[352,2048]{1,0:T(8,128)(2,1)} %bitcast.6), channel_id=1, source_target_pairs={{0,1},{1,0},{2,3},{3,2},{4,5},{5,4},{6,7},{7,6},{8,9},{9,8},{10,11... | collective-permute-start | bytes 4325384 | tf_op jit(solution)/shard_map/ppermute | solution.py:314
  2.0 12.3 %collective-permute-start.3 = (bf16[352,2048]{1,0:T(8,128)(2,1)}, bf16[352,2048]{1,0:T(8,128)(2,1)S(1)}, u32[]{:S(2)}, u32[]{:S(2)}) collective-permute-start(bf16[352,2048]{1,0:T(8,128)(2,1)} %bitcast.8), channel_id=1, source_target_pairs={{0,1},{1,0},{2,3},{3,2},{4,5},{5,4},{6,7},{7,6},{8,9},{9,8},{10,11... | collective-permute-start | bytes 4325384 | tf_op jit(solution)/shard_map/ppermute | solution.py:314
  2.2 14.7 %collective-permute-start.5 = (bf16[352,2048]{1,0:T(8,128)(2,1)}, bf16[352,2048]{1,0:T(8,128)(2,1)}, u32[]{:S(2)}, u32[]{:S(2)}) collective-permute-start(bf16[352,2048]{1,0:T(8,128)(2,1)} %bitcast.10), channel_id=1, source_target_pairs={{0,1},{1,0},{2,3},{3,2},{4,5},{5,4},{6,7},{7,6},{8,9},{9,8},{10,11... | collective-permute-start | bytes 4325384 | tf_op jit(solution)/shard_map/ppermute | solution.py:314
  2.5 7.0 %collective-permute-start.1 = (bf16[32,2176]{1,0:T(8,128)(2,1)S(1)}, bf16[32,2176]{1,0:T(8,128)(2,1)S(1)}, u32[]{:S(2)}, u32[]{:S(2)}) collective-permute-start(bf16[32,2176]{1,0:T(8,128)(2,1)S(1)} %shard_map.65.refs_0_), channel_id=1, source_target_pairs={{0,4},{2,6},{4,0},{6,2},{8,12},{10,14},{12,8},{14,10},{1,5},{3,7},... | collective-permute-start | bytes 417800 | tf_op jit(solution)/shard_map/ppermute | solution.py:297
  5.3 10.0 %collective-permute-start.4 = (bf16[32,2176]{1,0:T(8,128)(2,1)S(1)}, bf16[32,2176]{1,0:T(8,128)(2,1)S(1)}, u32[]{:S(2)}, u32[]{:S(2)}) collective-permute-start(bf16[32,2176]{1,0:T(8,128)(2,1)S(1)} %shard_map.65.refs_0_), channel_id=1, source_target_pairs={{0,12},{2,14},{4,8},{6,10},{8,4},{10,6},{12,0},{14,2},{1,13},{3,15... | collective-permute-start | bytes 417800 | tf_op jit(solution)/shard_map/ppermute | solution.py:297
  9.5 11.2 %collective-permute-start.6 = (bf16[32,2176]{1,0:T(8,128)(2,1)S(1)}, bf16[32,2176]{1,0:T(8,128)(2,1)S(1)}, u32[]{:S(2)}, u32[]{:S(2)}) collective-permute-start(bf16[32,2176]{1,0:T(8,128)(2,1)S(1)} %shard_map.65.refs_0_), channel_id=1, source_target_pairs={{0,8},{2,10},{4,12},{6,14},{8,0},{10,2},{12,4},{14,6},{1,9},{3,11}... | collective-permute-start | bytes 417800 | tf_op jit(solution)/shard_map/ppermute | solution.py:297
  12.8 9.4 %collective-permute-start.8 = (bf16[32,2176]{1,0:T(8,128)(2,1)S(1)}, bf16[32,2176]{1,0:T(8,128)(2,1)}, u32[]{:S(2)}, u32[]{:S(2)}) collective-permute-start(bf16[32,2176]{1,0:T(8,128)(2,1)S(1)} %shard_map.65.refs_0_), channel_id=1, source_target_pairs={{0,2},{2,0},{4,6},{6,4},{8,10},{10,8},{12,14},{14,12},{1,3},{3,1},... | collective-permute-start | bytes 417800 | tf_op jit(solution)/shard_map/ppermute | solution.py:294
  14.3 7.9 %collective-permute-start.9 = (bf16[32,2176]{1,0:T(8,128)(2,1)S(1)}, bf16[32,2176]{1,0:T(8,128)(2,1)}, u32[]{:S(2)}, u32[]{:S(2)}) collective-permute-start(bf16[32,2176]{1,0:T(8,128)(2,1)S(1)} %collective-permute-done.1.refs_0_.refs_1_), channel_id=1, source_target_pairs={{0,2},{2,0},{4,6},{6,4},{8,10},{10,8},{12,14},{14,12},{1,3},{3,1},... | collective-permute-start | bytes 417800 | tf_op jit(solution)/shard_map/ppermute | solution.py:294
  15.4 7.8 %collective-permute-start.7 = (bf16[32,2176]{1,0:T(8,128)(2,1)S(1)}, bf16[32,2176]{1,0:T(8,128)(2,1)}, u32[]{:S(2)}, u32[]{:S(2)}) collective-permute-start(bf16[32,2176]{1,0:T(8,128)(2,1)S(1)} %collective-permute-done.4.refs_2_), channel_id=1, source_target_pairs={{0,2},{2,0},{4,6},{6,4},{8,10},{10,8},{12,14},{14,12},{1,3},{3,1},... | collective-permute-start | bytes 417800 | tf_op jit(solution)/shard_map/ppermute | solution.py:294
  20.7 8.1 %collective-permute-start.11 = (bf16[32,2176]{1,0:T(8,128)(2,1)S(1)}, bf16[32,2176]{1,0:T(8,128)(2,1)S(1)}, u32[]{:S(2)}, u32[]{:S(2)}) collective-permute-start(bf16[32,2176]{1,0:T(8,128)(2,1)S(1)} %collective-permute-done.6.refs_0_), channel_id=1, source_target_pairs={{0,2},{2,0},{4,6},{6,4},{8,10},{10,8},{12,14},{14,12},{1,3},{3,1},... | collective-permute-start | bytes 417800 | tf_op jit(solution)/shard_map/ppermute | solution.py:294
  26.8 13.3 %collective-permute-start.10 = (bf16[64,2048]{1,0:T(8,128)(2,1)S(1)}, bf16[64,2048]{1,0:T(8,128)(2,1)S(1)}, u32[]{:S(2)}, u32[]{:S(2)}) collective-permute-start(bf16[64,2048]{1,0:T(8,128)(2,1)S(1)} %get-tuple-element.53), channel_id=1, source_target_pairs={{0,2},{2,0},{4,6},{6,4},{8,10},{10,8},{12,14},{14,12},{1,3},{3,1},... | collective-permute-start | bytes 786440 | tf_op jit(solution)/shard_map/ppermute | solution.py:294
  28.3 9.8 %collective-permute-start.12 = (bf16[32,2048]{1,0:T(8,128)(2,1)S(1)}, bf16[32,2048]{1,0:T(8,128)(2,1)S(1)}, u32[]{:S(2)}, u32[]{:S(2)}) collective-permute-start(bf16[32,2048]{1,0:T(8,128)(2,1)S(1)} %get-tuple-element.58), channel_id=1, source_target_pairs={{0,2},{2,0},{4,6},{6,4},{8,10},{10,8},{12,14},{14,12},{1,3},{3,1},... | collective-permute-start | bytes 393224 | tf_op jit(solution)/shard_map/ppermute | solution.py:294
  31.2 8.9 %collective-permute-start.15 = (bf16[32,2048]{1,0:T(8,128)(2,1)S(1)}, bf16[32,2048]{1,0:T(8,128)(2,1)S(1)}, u32[]{:S(2)}, u32[]{:S(2)}) collective-permute-start(bf16[32,2048]{1,0:T(8,128)(2,1)S(1)} %get-tuple-element.65), channel_id=1, source_target_pairs={{0,2},{2,0},{4,6},{6,4},{8,10},{10,8},{12,14},{14,12},{1,3},{3,1},... | collective-permute-start | bytes 393224 | tf_op jit(solution)/shard_map/ppermute | solution.py:294
  38.2 7.5 %collective-permute-start.13 = (bf16[32,2048]{1,0:T(8,128)(2,1)S(1)}, bf16[32,2048]{1,0:T(8,128)(2,1)S(1)}, u32[]{:S(2)}, u32[]{:S(2)}) collective-permute-start(bf16[32,2048]{1,0:T(8,128)(2,1)S(1)} %get-tuple-element.59), channel_id=1, source_target_pairs={{0,12},{2,14},{4,8},{6,10},{8,4},{10,6},{12,0},{14,2},{1,13},{3,15... | collective-permute-start | bytes 393224 | tf_op jit(solution)/shard_map/ppermute | solution.py:297
  40.7 8.5 %collective-permute-start.16 = (bf16[32,2048]{1,0:T(8,128)(2,1)S(1)}, bf16[32,2048]{1,0:T(8,128)(2,1)S(1)}, u32[]{:S(2)}, u32[]{:S(2)}) collective-permute-start(bf16[32,2048]{1,0:T(8,128)(2,1)S(1)} %get-tuple-element.66), channel_id=1, source_target_pairs={{0,8},{2,10},{4,12},{6,14},{8,0},{10,2},{12,4},{14,6},{1,9},{3,11}... | collective-permute-start | bytes 393224 | tf_op jit(solution)/shard_map/ppermute | solution.py:297
  41.5 7.8 %collective-permute-start.14 = (bf16[32,2048]{1,0:T(8,128)(2,1)S(1)}, bf16[32,2048]{1,0:T(8,128)(2,1)S(1)}, u32[]{:S(2)}, u32[]{:S(2)}) collective-permute-start(bf16[32,2048]{1,0:T(8,128)(2,1)S(1)} %get-tuple-element.62), channel_id=1, source_target_pairs={{0,4},{2,6},{4,0},{6,2},{8,12},{10,14},{12,8},{14,10},{1,5},{3,7},... | collective-permute-start | bytes 393224 | tf_op jit(solution)/shard_map/ppermute | solution.py:297
  49.4 1.3 %collective-permute-start.17 = (bf16[32,1024]{1,0:T(8,128)(2,1)S(1)}, bf16[32,1024]{1,0:T(8,128)(2,1)S(1)}, u32[]{:S(2)}, u32[]{:S(2)}) collective-permute-start(bf16[32,1024]{1,0:T(8,128)(2,1)S(1)} %broadcast_select_fusion.2), channel_id=1, source_target_pairs={{0,1},{1,0},{2,3},{3,2},{4,5},{5,4},{6,7},{7,6},{8,9},{9,8},{10,11... | collective-permute-start | bytes 196616 | tf_op jit(solution)/shard_map/ppermute | solution.py:347

commit v5 on v4

--- a/solution.py
+++ b/solution.py
@@ -10,7 +10,7 @@
 LANES = 128
 PIECES = 3
 VMEM_LIMIT = 16 * 2**20
-SMALL_LIMIT = 1 * 2**20
+SMALL_LIMIT = 2 * 2**20
 MARK = (8, 128)
 
 
@@ -20,9 +20,9 @@
 
 NO_COST = cost(1)
 GATHER_COST = 1
-TOUCH_COST = 1
+TOUCH_COST = 1000000
 EXPERT_COST = 1
-ADD_COST = 1
+ADD_COST = 1000000
 
 
 def sparse_local(tokens, expert_ids, gate_scores, gate_proj, up_proj, down_proj):
@@ -88,7 +88,9 @@
     return pltpu.with_memory_space_constraint(v, pltpu.HBM)
 
 
-def spread_kernel(n, head_ref, tokens_hbm, ids_hbm, scores_hbm, mine_ref, lanes_ref, ids, scores, sems):
+def spread_kernel(
+    n, head_ref, expert_ref, tokens_hbm, ids_hbm, scores_hbm, mine_ref, lanes_ref, select_ref, ids, scores, sems
+):
     part = mine_ref.shape[0]
     head = head_ref[0]
     copies = [
@@ -116,10 +118,12 @@
     pieces.append(jnp.zeros((LANES - PIECES * n, rows), jnp.float32))
     packed = jnp.concatenate(pieces, axis=0).T
     lanes_ref[...] = jnp.where(head == 0, packed[:part], packed[part:]).astype(jnp.bfloat16)
+    lane = lax.broadcasted_iota(jnp.int32, select_ref.shape, 1)
+    select_ref[...] = jnp.where(lane % n == expert_ref[0], 1.0, 0.0)
     copies[2].wait()
 
 
-def spread(head, tokens, expert_ids, gate_scores):
+def spread(head, expert, tokens, expert_ids, gate_scores):
     rows, half_width = tokens.shape
     n = lax.axis_size("wide")
     top = expert_ids.shape[1]
@@ -128,9 +132,10 @@
         out_shape=[
             jax.ShapeDtypeStruct((rows // 2, half_width), jnp.bfloat16),
             jax.ShapeDtypeStruct((rows // 2, LANES), jnp.bfloat16),
+            jax.ShapeDtypeStruct((1, LANES), jnp.float32),
         ],
-        in_specs=[pl.BlockSpec(memory_space=pltpu.SMEM)] + [in_hbm()] * 3,
-        out_specs=[in_vmem()] * 2,
+        in_specs=[pl.BlockSpec(memory_space=pltpu.SMEM)] * 2 + [in_hbm()] * 3,
+        out_specs=[in_vmem()] * 3,
         scratch_shapes=[
             pltpu.VMEM((top, rows), jnp.int32),
             pltpu.VMEM((top, rows), jnp.float32),
@@ -138,7 +143,7 @@
         ],
         compiler_params=pltpu.CompilerParams(vmem_limit_bytes=SMALL_LIMIT),
         cost_estimate=NO_COST,
-    )(head.reshape(1), hbm(tokens), hbm(expert_ids.T), hbm(gate_scores.T))
+    )(head, expert, hbm(tokens), hbm(expert_ids.T), hbm(gate_scores.T))
 
 
 def join_kernel(head_ref, mine_ref, got_ref, lanes_ref, out_ref):
@@ -159,7 +164,7 @@
         out_specs=in_vmem(),
         compiler_params=pltpu.CompilerParams(vmem_limit_bytes=SMALL_LIMIT),
         cost_estimate=NO_COST,
-    )(head.reshape(1), mine, got, lanes)
+    )(head, mine, got, lanes)
 
 
 def gather_kernel(count, _, *refs):
@@ -278,14 +283,76 @@
     )(mark, a, b)
 
 
+def grow_kernel(count, _, *refs):
+    terms, total_ref, mark = refs[:count], refs[count], refs[count + 1]
+    total_ref[...] = sum(t[...].astype(jnp.float32) for t in terms)
+    mark[...] = jnp.zeros(mark.shape, mark.dtype)
+
+
+def grow(mark, terms):
+    return pl.pallas_call(
+        functools.partial(grow_kernel, len(terms)),
+        out_shape=[
+            jax.ShapeDtypeStruct(terms[0].shape, jnp.float32),
+            jax.ShapeDtypeStruct(MARK, jnp.float32),
+        ],
+        in_specs=[pl.BlockSpec(memory_space=pl.ANY)] + [in_vmem()] * len(terms),
+        out_specs=[in_vmem()] * 2,
+        compiler_params=pltpu.CompilerParams(vmem_limit_bytes=SMALL_LIMIT),
+        cost_estimate=cost(ADD_COST),
+    )(mark, *terms)
+
+
+def collect_kernel(count, head_ref, *refs):
+    terms, keep_ref, send_ref = refs[:count], refs[count], refs[count + 1]
+    half = keep_ref.shape[1]
+    first = head_ref[0] == 0
+    total = sum(t[...].astype(jnp.float32) for t in terms).astype(jnp.bfloat16)
+    left, right = total[:, :half], total[:, half:]
+    keep_ref[...] = jnp.where(first, left, right)
+    send_ref[...] = jnp.where(first, right, left)
+
+
+def collect(head, terms):
+    part, width = terms[0].shape
+    return pl.pallas_call(
+        functools.partial(collect_kernel, len(terms)),
+        out_shape=[jax.ShapeDtypeStruct((part, width // 2), jnp.bfloat16)] * 2,
+        in_specs=[pl.BlockSpec(memory_space=pltpu.SMEM)] + [in_vmem()] * len(terms),
+        out_specs=[in_vmem()] * 2,
+        compiler_params=pltpu.CompilerParams(vmem_limit_bytes=SMALL_LIMIT),
+        cost_estimate=NO_COST,
+    )(head, *terms)
+
+
+def place_kernel(head_ref, keep_ref, rest_ref, out_ref):
+    part = keep_ref.shape[0]
+    first = head_ref[0] == 0
+    keep, rest = keep_ref[...], rest_ref[...]
+    out_ref[:part] = jnp.where(first, keep, rest)
+    out_ref[part:] = jnp.where(first, rest, keep)
+
+
+def place(head, keep, rest):
+    part, half_width = keep.shape
+    return pl.pallas_call(
+        place_kernel,
+        out_shape=jax.ShapeDtypeStruct((2 * part, half_width), jnp.bfloat16),
+        in_specs=[pl.BlockSpec(memory_space=pltpu.SMEM)] + [in_vmem()] * 2,
+        out_specs=in_vmem(),
+        compiler_params=pltpu.CompilerParams(vmem_limit_bytes=SMALL_LIMIT),
+        cost_estimate=NO_COST,
+    )(head, keep, rest)
+
+
 def after(mark, *values):
     return lax.optimization_barrier((mark, *values))
 
 
 def dense_local(tokens, expert_ids, gate_scores, gate_proj, up_proj, down_proj):
     n = lax.axis_size("wide")
-    head = lax.axis_index("head")
-    expert = lax.axis_index("wide")
+    head = lax.axis_index("head").reshape(1)
+    expert = lax.axis_index("wide").reshape(1)
     tok_rows, half_width = tokens.shape
     part = tok_rows // 2
     swap = ((0, 1), (1, 0))
@@ -299,14 +366,11 @@
     def add(*terms):
         return sum(t.astype(jnp.float32) for t in terms).astype(jnp.bfloat16)
 
-    first = head == 0
     got = lax.ppermute(tokens, "head", swap)
-    mine, lanes = spread(head, tokens, expert_ids, gate_scores)
+    mine, lanes, select = spread(head, expert, tokens, expert_ids, gate_scores)
     kept = (gate_proj[0], up_proj[0], down_proj[0])
     lanes, got = after(lanes, got)
     own = join(head, mine, got, lanes)
-    lane = jnp.arange(LANES, dtype=jnp.int32)
-    select = jnp.where(lane % n == expert, 1.0, 0.0).astype(jnp.float32)[None, :]
 
     last = 2
     mid = list(range(3, n // 2))
@@ -314,10 +378,11 @@
     came = [lax.ppermute(w, "head", swap) for w in held]
     block = {0: own}
     block.update({k: column(own, k) for k in mid + [1]})
-    over = {0: pair(own), 1: pair(block[1])}
+    over = {1: pair(block[1])}
     block[1], own_again = after(block[1], own)
     block[last] = column(own_again, last)
     mark = touch(block[1], *came[:2])
+    over[0] = pair(own)
     for k in mid:
         mark, block[k] = after(mark, block[k])
         over[k] = pair(block[k])
@@ -325,35 +390,40 @@
     mark, block[last] = after(mark, block[last])
     over[last] = pair(block[last])
 
-    groups = [[block[0]], [block[1]]] + [[v[k]] for k in mid for v in (block, over)]
-    done, mark = run_expert(mark, groups + [[over[0], over[1]]], select, weights)
-    here = {0: done[0], 1: done[1]}
-    there = {}
-    for i, k in enumerate(mid):
-        here[k] = done[2 + 2 * i]
-        there[k] = pair(done[3 + 2 * i])
-    first_two = pair(done[-1])
-    there[0], there[1] = first_two[:part], first_two[part:]
-    done, mark = run_expert(mark, [[block[last]], [over[last]]], select, weights)
-    here[last] = done[0]
-    there[last] = pair(done[1])
-    returned = []
+    here, there = {}, {}
+    keys = [0] + [1] + mid
+    groups = [[v[k]] for v in (block, over) for k in keys]
+    done, mark = run_expert(mark, groups, select, weights)
+    here.update(zip(keys, done))
+    for j, k in enumerate(keys):
+        there[k] = pair(done[len(keys) + j])
+    keys = [last]
+    groups = [[v[k]] for v in (block, over) for k in keys]
+    done, mark = run_expert(mark, groups, select, weights)
+    here.update(zip(keys, done))
+    for j, k in enumerate(keys):
+        there[k] = pair(done[len(keys) + j])
+    returned = {}
     for k in mid + [1, last]:
-        total, mark = add_rows(mark, here[k], there[k])
-        returned.append(column(total, k))
-    mixed = add(here[0], there[0], *returned)
-    left, right = mixed[:, :half_width], mixed[:, half_width:]
-    keep = jnp.where(first, left, right)
-    rest = lax.ppermute(jnp.where(first, right, left), "head", swap)
-    return jnp.concatenate(
-        [jnp.where(first, keep, rest), jnp.where(first, rest, keep)], axis=0
-    )
+        if k in mid + [1]:
+            total, mark = add_rows(mark, here[k], there[k])
+        else:
+            total = add(here[k], there[k])
+        returned[k] = column(total, k)
+    terms = [here[0], there[0]]
+    for k in mid + [1]:
+        total, mark = grow(mark, terms + [returned[k]])
+        terms = [total]
+    terms.append(returned[last])
+    keep, send = collect(head, terms)
+    rest = lax.ppermute(send, "head", swap)
+    return place(head, keep, rest)
 
 
 def local(tokens, expert_ids, gate_scores, gate_proj, up_proj, down_proj):
     n = lax.axis_size("wide")
     named = expert_ids.shape[1]
-    dense = named == n and n >= 4 and n & (n - 1) == 0 and PIECES * n <= LANES
+    dense = named == n and n >= 8 and n & (n - 1) == 0 and PIECES * n <= LANES
     if dense and lax.axis_size("head") == 2 and tokens.shape[0] % 32 == 0:
         return dense_local(tokens, expert_ids, gate_scores, gate_proj, up_proj, down_proj)
     return sparse_local(tokens, expert_ids, gate_scores, gate_proj, up_proj, down_proj)

time: 51.6 us -> 48 us (0.930)
  waiting for transfers between devices: 17 us -> 13.6 us
  starting transfers between devices: 23.1 us -> 24.4 us
  Pallas kernels: 10.4 us -> 9.63 us
  other arithmetic: 0.78 us -> 0.03 us
    ppermute x7 -> x8, waiting for transfers between devices: 6.35 us -> 2 us  [pair(): return lax.ppermute(v, 'wide', [(w, w ^ 1) for w in range(n)])]
    pallas_call x0 -> x4, Pallas kernels: none -> 1.39 us  [the longest x2 0.68 us: grow(): pl.pallas_call(functools.partial(grow_kernel, len(terms)), out_shape=[jax...]
    pallas_call x2, Pallas kernels: 5.91 us -> 4.87 us  [run_expert(): pl.pallas_call(functools.partial(expert_kernel, len(blocks)), out_shape=[...]
    ppermute x6, waiting for transfers between devices: 9.15 us -> 10.1 us  [column(): return lax.ppermute(v, 'wide', [(w, w ^ 2 * k) for w in range(n)])]
    ppermute x6, starting transfers between devices: 13 us -> 13.8 us  [column(): return lax.ppermute(v, 'wide', [(w, w ^ 2 * k) for w in range(n)])]
    concatenate x1 -> x0, other arithmetic: 0.67 us -> none  [dense_local(): jnp.concatenate([jnp.where(first, keep, rest), jnp.where(first, rest, kee...]
    pallas_call x3 -> x2, Pallas kernels: 0.68 us -> 0.07 us  [add_rows(): pl.pallas_call(add_kernel, out_shape=[jax.ShapeDtypeStruct(a.shape, jnp.b...]
    ppermute x7 -> x8, starting transfers between devices: 8.66 us -> 9.19 us  [pair(): return lax.ppermute(v, 'wide', [(w, w ^ 1) for w in range(n)])]
  transfers between devices with their start and end apart: 18 -> 19, of which waited for: 9 -> 11; matrix products, arithmetic and copies ran while one was open for 0% -> 0% of each run, Pallas kernels for 20% -> 19%
where the time goes in v5:
time: 48 us; the launch traced here: 47.8 us
  starting transfers between devices  24.4 us (51%)
  waiting for transfers between devices  13.6 us (28%)
  Pallas kernels  9.63 us (20%)
    ppermute x6, starting transfers between devices, column(): return lax.ppermute(v, 'wide', [(w, w ^ 2 * k) for w in range(n)])  13.8 us
    ppermute x6, waiting for transfers between devices, column(): return lax.ppermute(v, 'wide', [(w, w ^ 2 * k) for w in range(n)])  10.1 us
    ppermute x8, starting transfers between devices, pair(): return lax.ppermute(v, 'wide', [(w, w ^ 1) for w in range(n)])  9.19 us
    pallas_call x2, Pallas kernels, run_expert(): pl.pallas_call(functools.partial(expert_kernel, len(blocks)), out_shape=[...  4.87 us
    pallas_call x1, Pallas kernels, gather_weights(): pl.pallas_call(functools.partial(gather_kernel, count), out_shape=[jax.Sh...  2.39 us
    ppermute x8, waiting for transfers between devices, pair(): return lax.ppermute(v, 'wide', [(w, w ^ 1) for w in range(n)])  2 us
    ppermute x1, waiting for transfers between devices, dense_local(): rest = lax.ppermute(send, 'head', swap)  1.24 us
  transfers between devices with their start and end apart: 19, of which 11 were waited for; matrix products, arithmetic and copies ran while one was open for 0% of the time, Pallas kernels for 19%

profile of v5, /device:TPU:0, one launch (start us, length us, event | category | flops | bytes accessed | tf_op | source)
XLA Modules:
  0.0 47.8 jit_solution(1666504583513892851)
XLA Ops:
  0.0 0.5 collective-permute-start
  0.5 0.9 %shard_map.64 = (bf16[32,1024]{1,0:T(8,128)(2,1)S(1)}, bf16[32,128]{1,0:T(8,128)(2,1)S(1)}, f32[1,128]{1,0:T(1,128)S(1)}) custom-call(s32[1]{0:T(128)} %bitcast.head_ref, s32[1]{0:T(128)} %bitcast.1.expert_ref, bf16[64,1024]{1,0:T(8,128)(2,1)} %tokens_hbm.1, s32[8,64]{1,0:T(8,128)} %bitcast.13, f32[8,64]{1,0:T(8,128)} %bitcast.14), custom_call_target="tpu_custom_call" | custom-call | bytes 1 | tf_op jit(solution)/shard_map/pallas_call | solution.py:130
  1.4 0.3 collective-permute-done.got_ref
  1.7 0.4 collective-permute-start.2
  2.0 0.1 collective-permute-start.3
  2.2 0.4 collective-permute-start.5
  2.5 2.8 %collective-permute-start.1 = (bf16[32,2176]{1,0:T(8,128)(2,1)S(1)}, bf16[32,2176]{1,0:T(8,128)(2,1)S(1)}, u32[]{:S(2)}, u32[]{:S(2)}) collective-permute-start(bf16[32,2176]{1,0:T(8,128)(2,1)S(1)} %shard_map.65.refs_0_), channel_id=1, source_target_pairs={{0,4},{2,6},{4,0},{6,2},{8,12},{10,14},{12,8},{14,10},{1,5},{3,7},... | collective-permute-start | bytes 417800 | tf_op jit(solution)/shard_map/ppermute | solution.py:364
  5.3 2.5 %collective-permute-start.4 = (bf16[32,2176]{1,0:T(8,128)(2,1)S(1)}, bf16[32,2176]{1,0:T(8,128)(2,1)S(1)}, u32[]{:S(2)}, u32[]{:S(2)}) collective-permute-start(bf16[32,2176]{1,0:T(8,128)(2,1)S(1)} %shard_map.65.refs_0_), channel_id=1, source_target_pairs={{0,12},{2,14},{4,8},{6,10},{8,4},{10,6},{12,0},{14,2},{1,13},{3,15... | collective-permute-start | bytes 417800 | tf_op jit(solution)/shard_map/ppermute | solution.py:364
  7.8 1.7 %collective-permute-done.1.refs_0_.refs_1_ = bf16[32,2176]{1,0:T(8,128)(2,1)S(1)} collective-permute-done((bf16[32,2176]{1,0:T(8,128)(2,1)S(1)}, bf16[32,2176]{1,0:T(8,128)(2,1)S(1)}, u32[]{:S(2)}, u32[]{:S(2)}) %collective-permute-start.1) | collective-permute-done | bytes 139296 | tf_op jit(solution)/shard_map/ppermute | solution.py:364
  9.5 3.3 %collective-permute-start.6 = (bf16[32,2176]{1,0:T(8,128)(2,1)S(1)}, bf16[32,2176]{1,0:T(8,128)(2,1)S(1)}, u32[]{:S(2)}, u32[]{:S(2)}) collective-permute-start(bf16[32,2176]{1,0:T(8,128)(2,1)S(1)} %shard_map.65.refs_0_), channel_id=1, source_target_pairs={{0,8},{2,10},{4,12},{6,14},{8,0},{10,2},{12,4},{14,6},{1,9},{3,11}... | collective-permute-start | bytes 417800 | tf_op jit(solution)/shard_map/ppermute | solution.py:364
  12.8 0.0 collective-permute-done.2.refs_1_.refs_3_
  12.8 1.5 %collective-permute-start.7 = (bf16[32,2176]{1,0:T(8,128)(2,1)S(1)}, bf16[32,2176]{1,0:T(8,128)(2,1)S(1)}, u32[]{:S(2)}, u32[]{:S(2)}) collective-permute-start(bf16[32,2176]{1,0:T(8,128)(2,1)S(1)} %shard_map.65.refs_0_), channel_id=1, source_target_pairs={{0,2},{2,0},{4,6},{6,4},{8,10},{10,8},{12,14},{14,12},{1,3},{3,1},... | collective-permute-start | bytes 417800 | tf_op jit(solution)/shard_map/ppermute | solution.py:361
  14.3 0.0 collective-permute-done.3.refs_2_.refs_4_
  14.3 0.5 %collective-permute-start.8 = (bf16[32,2176]{1,0:T(8,128)(2,1)S(1)}, bf16[32,2176]{1,0:T(8,128)(2,1)S(1)}, u32[]{:S(2)}, u32[]{:S(2)}) collective-permute-start(bf16[32,2176]{1,0:T(8,128)(2,1)S(1)} %collective-permute-done.1.refs_0_.refs_1_), channel_id=1, source_target_pairs={{0,2},{2,0},{4,6},{6,4},{8,10},{10,8},{12,14},{14,12},{1,3},{3,1},... | collective-permute-start | bytes 417800 | tf_op jit(solution)/shard_map/ppermute | solution.py:361
  14.9 0.5 %collective-permute-done.4.refs_2_ = bf16[32,2176]{1,0:T(8,128)(2,1)S(1)} collective-permute-done((bf16[32,2176]{1,0:T(8,128)(2,1)S(1)}, bf16[32,2176]{1,0:T(8,128)(2,1)S(1)}, u32[]{:S(2)}, u32[]{:S(2)}) %collective-permute-start.4) | collective-permute-done | bytes 139296 | tf_op jit(solution)/shard_map/ppermute | solution.py:364
  15.4 1.5 %collective-permute-start.9 = (bf16[32,2176]{1,0:T(8,128)(2,1)S(1)}, bf16[32,2176]{1,0:T(8,128)(2,1)S(1)}, u32[]{:S(2)}, u32[]{:S(2)}) collective-permute-start(bf16[32,2176]{1,0:T(8,128)(2,1)S(1)} %collective-permute-done.4.refs_2_), channel_id=1, source_target_pairs={{0,2},{2,0},{4,6},{6,4},{8,10},{10,8},{12,14},{14,12},{1,3},{3,1},... | collective-permute-start | bytes 417800 | tf_op jit(solution)/shard_map/ppermute | solution.py:361
  16.9 0.0 collective-permute-done.5.refs_5_
  16.9 2.4 %shard_map.67 = (bf16[704,2048]{1,0:T(8,128)(2,1)S(1)}, bf16[704,2048]{1,0:T(8,128)(2,1)S(1)}, bf16[704,2048]{1,0:T(8,128)(2,1)S(1)}, f32[8,128]{1,0:T(8,128)S(1)}) custom-call(f32[8,128]{1,0:T(8,128)S(1)} %shard_map.66._, bf16[352,2048]{1,0:T(8,128)(2,1)} %bitcast.8, bf16[352,2048]{1,0:T(8,128)(2,1)} %bitcast.10, bf16[352,2048]{1,0:T(8,128)(2,1)} %bitcast.12, ...), custom_call_target="tpu_custom_call" | custom-call | bytes 1 | tf_op jit(solution)/shard_map/pallas_call | solution.py:195
  19.3 1.5 %collective-permute-done.6.refs_0_ = bf16[32,2176]{1,0:T(8,128)(2,1)S(1)} collective-permute-done((bf16[32,2176]{1,0:T(8,128)(2,1)S(1)}, bf16[32,2176]{1,0:T(8,128)(2,1)S(1)}, u32[]{:S(2)}, u32[]{:S(2)}) %collective-permute-start.6) | collective-permute-done | bytes 139296 | tf_op jit(solution)/shard_map/ppermute | solution.py:364
  20.7 1.5 %collective-permute-start.10 = (bf16[32,2176]{1,0:T(8,128)(2,1)S(1)}, bf16[32,2176]{1,0:T(8,128)(2,1)S(1)}, u32[]{:S(2)}, u32[]{:S(2)}) collective-permute-start(bf16[32,2176]{1,0:T(8,128)(2,1)S(1)} %collective-permute-done.6.refs_0_), channel_id=1, source_target_pairs={{0,2},{2,0},{4,6},{6,4},{8,10},{10,8},{12,14},{14,12},{1,3},{3,1},... | collective-permute-start | bytes 417800 | tf_op jit(solution)/shard_map/ppermute | solution.py:361
  22.2 0.0 collective-permute-done.7.refs_3_
  22.2 0.0 collective-permute-done.8.refs_4_
  22.2 0.9 %collective-permute-done.9.refs_5_ = bf16[32,2176]{1,0:T(8,128)(2,1)S(1)} collective-permute-done((bf16[32,2176]{1,0:T(8,128)(2,1)S(1)}, bf16[32,2176]{1,0:T(8,128)(2,1)S(1)}, u32[]{:S(2)}, u32[]{:S(2)}) %collective-permute-start.9) | collective-permute-done | bytes 139296 | tf_op jit(solution)/shard_map/ppermute | solution.py:361
  23.1 2.5 %shard_map.68 = (bf16[32,2048]{1,0:T(8,128)(2,1)S(1)}, bf16[32,2048]{1,0:T(8,128)(2,1)S(1)}, bf16[32,2048]{1,0:T(8,128)(2,1)S(1)}, bf16[32,2048]{1,0:T(8,128)(2,...) custom-call(f32[8,128]{1,0:T(8,128)S(1)} %get-tuple-element.53._, ...), custom_call_target="tpu_custom_call" | custom-call | bytes 1 | tf_op jit(solution)/shard_map/pallas_call | solution.py:252
  25.6 1.6 %collective-permute-start.11 = (bf16[32,2048]{1,0:T(8,128)(2,1)S(1)}, bf16[32,2048]{1,0:T(8,128)(2,1)S(1)}, u32[]{:S(2)}, u32[]{:S(2)}) collective-permute-start(bf16[32,2048]{1,0:T(8,128)(2,1)S(1)} %get-tuple-element.63), channel_id=1, source_target_pairs={{0,2},{2,0},{4,6},{6,4},{8,10},{10,8},{12,14},{14,12},{1,3},{3,1},... | collective-permute-start | bytes 393224 | tf_op jit(solution)/shard_map/ppermute | solution.py:361
  27.2 0.5 %collective-permute-start.12 = (bf16[32,2048]{1,0:T(8,128)(2,1)S(1)}, bf16[32,2048]{1,0:T(8,128)(2,1)S(1)}, u32[]{:S(2)}, u32[]{:S(2)}) collective-permute-start(bf16[32,2048]{1,0:T(8,128)(2,1)S(1)} %get-tuple-element.66), channel_id=1, source_target_pairs={{0,2},{2,0},{4,6},{6,4},{8,10},{10,8},{12,14},{14,12},{1,3},{3,1},... | collective-permute-start | bytes 393224 | tf_op jit(solution)/shard_map/ppermute | solution.py:361
  27.7 0.0 collective-permute-done.10.refs_1_
  27.7 2.3 %shard_map.69 = (bf16[32,2048]{1,0:T(8,128)(2,1)S(1)}, bf16[32,2048]{1,0:T(8,128)(2,1)S(1)}, f32[8,128]{1,0:T(8,128)S(1)}) custom-call(f32[8,128]{1,0:T(8,128)S(1)} %get-tuple-element.59._, f32[1,128]{1,0:T(1,128)S(1)} %get-tuple-element.54.select_ref, bf16[32,2176]{1,0:T(8,128)(2,1)S(1)} %collective-permute-done.6.refs_0_, ...), custom_call_target="tpu_custom_call" | custom-call | bytes 1 | tf_op jit(solution)/shard_map/pallas_call | solution.py:252
  30.1 1.6 %collective-permute-start.16 = (bf16[32,2048]{1,0:T(8,128)(2,1)S(1)}, bf16[32,2048]{1,0:T(8,128)(2,1)S(1)}, u32[]{:S(2)}, u32[]{:S(2)}) collective-permute-start(bf16[32,2048]{1,0:T(8,128)(2,1)S(1)} %get-tuple-element.76), channel_id=1, source_target_pairs={{0,2},{2,0},{4,6},{6,4},{8,10},{10,8},{12,14},{14,12},{1,3},{3,1},... | collective-permute-start | bytes 393224 | tf_op jit(solution)/shard_map/ppermute | solution.py:361
  31.6 0.5 %collective-permute-start.13 = (bf16[32,2048]{1,0:T(8,128)(2,1)S(1)}, bf16[32,2048]{1,0:T(8,128)(2,1)S(1)}, u32[]{:S(2)}, u32[]{:S(2)}) collective-permute-start(bf16[32,2048]{1,0:T(8,128)(2,1)S(1)} %get-tuple-element.69), channel_id=1, source_target_pairs={{0,2},{2,0},{4,6},{6,4},{8,10},{10,8},{12,14},{14,12},{1,3},{3,1},... | collective-permute-start | bytes 393224 | tf_op jit(solution)/shard_map/ppermute | solution.py:361
  32.2 0.0 collective-permute-done.11.b_ref
  32.2 1.9 %collective-permute-start.14 = (bf16[32,2048]{1,0:T(8,128)(2,1)S(1)}, bf16[32,2048]{1,0:T(8,128)(2,1)S(1)}, u32[]{:S(2)}, u32[]{:S(2)}) collective-permute-start(bf16[32,2048]{1,0:T(8,128)(2,1)S(1)} %get-tuple-element.70), channel_id=1, source_target_pairs={{0,12},{2,14},{4,8},{6,10},{8,4},{10,6},{12,0},{14,2},{1,13},{3,15... | collective-permute-start | bytes 393224 | tf_op jit(solution)/shard_map/ppermute | solution.py:364
  34.1 0.5 collective-permute-done.12.b_ref
  34.6 1.8 %collective-permute-start.15 = (bf16[32,2048]{1,0:T(8,128)(2,1)S(1)}, bf16[32,2048]{1,0:T(8,128)(2,1)S(1)}, u32[]{:S(2)}, u32[]{:S(2)}) collective-permute-start(bf16[32,2048]{1,0:T(8,128)(2,1)S(1)} %get-tuple-element.73), channel_id=1, source_target_pairs={{0,4},{2,6},{4,0},{6,2},{8,12},{10,14},{12,8},{14,10},{1,5},{3,7},... | collective-permute-start | bytes 393224 | tf_op jit(solution)/shard_map/ppermute | solution.py:364
  36.5 0.7 %collective-permute-done.16 = bf16[32,2048]{1,0:T(8,128)(2,1)S(1)} collective-permute-done((bf16[32,2048]{1,0:T(8,128)(2,1)S(1)}, bf16[32,2048]{1,0:T(8,128)(2,1)S(1)}, u32[]{:S(2)}, u32[]{:S(2)}) %collective-permute-start.16) | collective-permute-done | bytes 131104 | tf_op jit(solution)/shard_map/ppermute | solution.py:361
  37.2 1.5 %collective-permute-start.17 = (bf16[32,2048]{1,0:T(8,128)(2,1)S(1)}, bf16[32,2048]{1,0:T(8,128)(2,1)S(1)}, u32[]{:S(2)}, u32[]{:S(2)}) collective-permute-start(bf16[32,2048]{1,0:T(8,128)(2,1)S(1)} %add_convert_fusion), channel_id=1, source_target_pairs={{0,8},{2,10},{4,12},{6,14},{8,0},{10,2},{12,4},{14,6},{1,9},{3,11}... | collective-permute-start | bytes 393224 | tf_op jit(solution)/shard_map/ppermute | solution.py:364
  38.7 0.0 collective-permute-done.13.refs_1_
  38.7 1.6 %collective-permute-done.14.refs_2_ = bf16[32,2048]{1,0:T(8,128)(2,1)S(1)} collective-permute-done((bf16[32,2048]{1,0:T(8,128)(2,1)S(1)}, bf16[32,2048]{1,0:T(8,128)(2,1)S(1)}, u32[]{:S(2)}, u32[]{:S(2)}) %collective-permute-start.14) | collective-permute-done | bytes 131104 | tf_op jit(solution)/shard_map/ppermute | solution.py:364
  40.3 0.1 shard_map.72
  40.4 1.1 %collective-permute-done.15.refs_1_ = bf16[32,2048]{1,0:T(8,128)(2,1)S(1)} collective-permute-done((bf16[32,2048]{1,0:T(8,128)(2,1)S(1)}, bf16[32,2048]{1,0:T(8,128)(2,1)S(1)}, u32[]{:S(2)}, u32[]{:S(2)}) %collective-permute-start.15) | collective-permute-done | bytes 131104 | tf_op jit(solution)/shard_map/ppermute | solution.py:364
  41.5 0.6 %shard_map.73 = (f32[32,2048]{1,0:T(8,128)S(1)}, f32[8,128]{1,0:T(8,128)}) custom-call(f32[8,128]{1,0:T(8,128)S(1)} %get-tuple-element.71._, f32[32,2048]{1,0:T(8,128)S(1)} %get-tuple-element.72.refs_0_, bf16[32,2048]{1,0:T(8,128)(2,1)S(1)} %collective-permute-done.15.refs_1_), custom_call_target="tpu_custom_call" | custom-call | bytes 1000000 | tf_op jit(solution)/shard_map/pallas_call | solution.py:293
  42.1 3.7 %collective-permute-done.17.refs_1_ = bf16[32,2048]{1,0:T(8,128)(2,1)S(1)} collective-permute-done((bf16[32,2048]{1,0:T(8,128)(2,1)S(1)}, bf16[32,2048]{1,0:T(8,128)(2,1)S(1)}, u32[]{:S(2)}, u32[]{:S(2)}) %collective-permute-start.17) | collective-permute-done | bytes 131104 | tf_op jit(solution)/shard_map/ppermute | solution.py:364
  45.8 0.1 collective-permute-start.18
  45.9 1.2 %collective-permute-done.18.rest_ref = bf16[32,1024]{1,0:T(8,128)(2,1)S(1)} collective-permute-done((bf16[32,1024]{1,0:T(8,128)(2,1)S(1)}, bf16[32,1024]{1,0:T(8,128)(2,1)S(1)}, u32[]{:S(2)}, u32[]{:S(2)}) %collective-permute-start.18) | collective-permute-done | bytes 65568 | tf_op jit(solution)/shard_map/ppermute | solution.py:419
  47.1 0.7 %shard_map.75 = bf16[64,1024]{1,0:T(8,128)(2,1)} custom-call(s32[1]{0:T(128)} %bitcast.head_ref, bf16[32,1024]{1,0:T(8,128)(2,1)S(1)} %get-tuple-element.77.keep_ref, bf16[32,1024]{1,0:T(8,128)(2,1)S(1)} %collective-permute-done.18.rest_ref), custom_call_target="tpu_custom_call" | custom-call | bytes 1 | tf_op jit(solution)/shard_map/pallas_call | solution.py:338
  (6 shorter events, 0.2 us)
Async XLA Ops:
  0.0 1.6 %collective-permute-start = (bf16[64,1024]{1,0:T(8,128)(2,1)}, bf16[64,1024]{1,0:T(8,128)(2,1)S(1)}, u32[]{:S(2)}, u32[]{:S(2)}) collective-permute-start(bf16[64,1024]{1,0:T(8,128)(2,1)} %tokens_hbm.1), channel_id=1, source_target_pairs={{0,1},{1,0},{2,3},{3,2},{4,5},{5,4},{6,7},{7,6},{8,9},{9,8},{10,11... | collective-permute-start | bytes 393224 | tf_op jit(solution)/shard_map/ppermute | solution.py:369
  1.7 11.2 %collective-permute-start.2 = (bf16[352,2048]{1,0:T(8,128)(2,1)}, bf16[352,2048]{1,0:T(8,128)(2,1)S(1)}, u32[]{:S(2)}, u32[]{:S(2)}) collective-permute-start(bf16[352,2048]{1,0:T(8,128)(2,1)} %bitcast.7), channel_id=1, source_target_pairs={{0,1},{1,0},{2,3},{3,2},{4,5},{5,4},{6,7},{7,6},{8,9},{9,8},{10,11... | collective-permute-start | bytes 4325384 | tf_op jit(solution)/shard_map/ppermute | solution.py:378
  2.0 12.3 %collective-permute-start.3 = (bf16[352,2048]{1,0:T(8,128)(2,1)}, bf16[352,2048]{1,0:T(8,128)(2,1)S(1)}, u32[]{:S(2)}, u32[]{:S(2)}) collective-permute-start(bf16[352,2048]{1,0:T(8,128)(2,1)} %bitcast.9), channel_id=1, source_target_pairs={{0,1},{1,0},{2,3},{3,2},{4,5},{5,4},{6,7},{7,6},{8,9},{9,8},{10,11... | collective-permute-start | bytes 4325384 | tf_op jit(solution)/shard_map/ppermute | solution.py:378
  2.2 14.7 %collective-permute-start.5 = (bf16[352,2048]{1,0:T(8,128)(2,1)}, bf16[352,2048]{1,0:T(8,128)(2,1)S(1)}, u32[]{:S(2)}, u32[]{:S(2)}) collective-permute-start(bf16[352,2048]{1,0:T(8,128)(2,1)} %bitcast.11), channel_id=1, source_target_pairs={{0,1},{1,0},{2,3},{3,2},{4,5},{5,4},{6,7},{7,6},{8,9},{9,8},{10,11... | collective-permute-start | bytes 4325384 | tf_op jit(solution)/shard_map/ppermute | solution.py:378
  2.5 7.0 %collective-permute-start.1 = (bf16[32,2176]{1,0:T(8,128)(2,1)S(1)}, bf16[32,2176]{1,0:T(8,128)(2,1)S(1)}, u32[]{:S(2)}, u32[]{:S(2)}) collective-permute-start(bf16[32,2176]{1,0:T(8,128)(2,1)S(1)} %shard_map.65.refs_0_), channel_id=1, source_target_pairs={{0,4},{2,6},{4,0},{6,2},{8,12},{10,14},{12,8},{14,10},{1,5},{3,7},... | collective-permute-start | bytes 417800 | tf_op jit(solution)/shard_map/ppermute | solution.py:364
  5.3 10.0 %collective-permute-start.4 = (bf16[32,2176]{1,0:T(8,128)(2,1)S(1)}, bf16[32,2176]{1,0:T(8,128)(2,1)S(1)}, u32[]{:S(2)}, u32[]{:S(2)}) collective-permute-start(bf16[32,2176]{1,0:T(8,128)(2,1)S(1)} %shard_map.65.refs_0_), channel_id=1, source_target_pairs={{0,12},{2,14},{4,8},{6,10},{8,4},{10,6},{12,0},{14,2},{1,13},{3,15... | collective-permute-start | bytes 417800 | tf_op jit(solution)/shard_map/ppermute | solution.py:364
  9.5 11.2 %collective-permute-start.6 = (bf16[32,2176]{1,0:T(8,128)(2,1)S(1)}, bf16[32,2176]{1,0:T(8,128)(2,1)S(1)}, u32[]{:S(2)}, u32[]{:S(2)}) collective-permute-start(bf16[32,2176]{1,0:T(8,128)(2,1)S(1)} %shard_map.65.refs_0_), channel_id=1, source_target_pairs={{0,8},{2,10},{4,12},{6,14},{8,0},{10,2},{12,4},{14,6},{1,9},{3,11}... | collective-permute-start | bytes 417800 | tf_op jit(solution)/shard_map/ppermute | solution.py:364
  12.8 9.4 %collective-permute-start.7 = (bf16[32,2176]{1,0:T(8,128)(2,1)S(1)}, bf16[32,2176]{1,0:T(8,128)(2,1)S(1)}, u32[]{:S(2)}, u32[]{:S(2)}) collective-permute-start(bf16[32,2176]{1,0:T(8,128)(2,1)S(1)} %shard_map.65.refs_0_), channel_id=1, source_target_pairs={{0,2},{2,0},{4,6},{6,4},{8,10},{10,8},{12,14},{14,12},{1,3},{3,1},... | collective-permute-start | bytes 417800 | tf_op jit(solution)/shard_map/ppermute | solution.py:361
  14.3 7.9 %collective-permute-start.8 = (bf16[32,2176]{1,0:T(8,128)(2,1)S(1)}, bf16[32,2176]{1,0:T(8,128)(2,1)S(1)}, u32[]{:S(2)}, u32[]{:S(2)}) collective-permute-start(bf16[32,2176]{1,0:T(8,128)(2,1)S(1)} %collective-permute-done.1.refs_0_.refs_1_), channel_id=1, source_target_pairs={{0,2},{2,0},{4,6},{6,4},{8,10},{10,8},{12,14},{14,12},{1,3},{3,1},... | collective-permute-start | bytes 417800 | tf_op jit(solution)/shard_map/ppermute | solution.py:361
  15.4 7.7 %collective-permute-start.9 = (bf16[32,2176]{1,0:T(8,128)(2,1)S(1)}, bf16[32,2176]{1,0:T(8,128)(2,1)S(1)}, u32[]{:S(2)}, u32[]{:S(2)}) collective-permute-start(bf16[32,2176]{1,0:T(8,128)(2,1)S(1)} %collective-permute-done.4.refs_2_), channel_id=1, source_target_pairs={{0,2},{2,0},{4,6},{6,4},{8,10},{10,8},{12,14},{14,12},{1,3},{3,1},... | collective-permute-start | bytes 417800 | tf_op jit(solution)/shard_map/ppermute | solution.py:361
  20.7 7.0 %collective-permute-start.10 = (bf16[32,2176]{1,0:T(8,128)(2,1)S(1)}, bf16[32,2176]{1,0:T(8,128)(2,1)S(1)}, u32[]{:S(2)}, u32[]{:S(2)}) collective-permute-start(bf16[32,2176]{1,0:T(8,128)(2,1)S(1)} %collective-permute-done.6.refs_0_), channel_id=1, source_target_pairs={{0,2},{2,0},{4,6},{6,4},{8,10},{10,8},{12,14},{14,12},{1,3},{3,1},... | collective-permute-start | bytes 417800 | tf_op jit(solution)/shard_map/ppermute | solution.py:361
  25.6 6.5 %collective-permute-start.11 = (bf16[32,2048]{1,0:T(8,128)(2,1)S(1)}, bf16[32,2048]{1,0:T(8,128)(2,1)S(1)}, u32[]{:S(2)}, u32[]{:S(2)}) collective-permute-start(bf16[32,2048]{1,0:T(8,128)(2,1)S(1)} %get-tuple-element.63), channel_id=1, source_target_pairs={{0,2},{2,0},{4,6},{6,4},{8,10},{10,8},{12,14},{14,12},{1,3},{3,1},... | collective-permute-start | bytes 393224 | tf_op jit(solution)/shard_map/ppermute | solution.py:361
  27.2 7.4 %collective-permute-start.12 = (bf16[32,2048]{1,0:T(8,128)(2,1)S(1)}, bf16[32,2048]{1,0:T(8,128)(2,1)S(1)}, u32[]{:S(2)}, u32[]{:S(2)}) collective-permute-start(bf16[32,2048]{1,0:T(8,128)(2,1)S(1)} %get-tuple-element.66), channel_id=1, source_target_pairs={{0,2},{2,0},{4,6},{6,4},{8,10},{10,8},{12,14},{14,12},{1,3},{3,1},... | collective-permute-start | bytes 393224 | tf_op jit(solution)/shard_map/ppermute | solution.py:361
  30.1 7.0 %collective-permute-start.16 = (bf16[32,2048]{1,0:T(8,128)(2,1)S(1)}, bf16[32,2048]{1,0:T(8,128)(2,1)S(1)}, u32[]{:S(2)}, u32[]{:S(2)}) collective-permute-start(bf16[32,2048]{1,0:T(8,128)(2,1)S(1)} %get-tuple-element.76), channel_id=1, source_target_pairs={{0,2},{2,0},{4,6},{6,4},{8,10},{10,8},{12,14},{14,12},{1,3},{3,1},... | collective-permute-start | bytes 393224 | tf_op jit(solution)/shard_map/ppermute | solution.py:361
  31.6 7.0 %collective-permute-start.13 = (bf16[32,2048]{1,0:T(8,128)(2,1)S(1)}, bf16[32,2048]{1,0:T(8,128)(2,1)S(1)}, u32[]{:S(2)}, u32[]{:S(2)}) collective-permute-start(bf16[32,2048]{1,0:T(8,128)(2,1)S(1)} %get-tuple-element.69), channel_id=1, source_target_pairs={{0,2},{2,0},{4,6},{6,4},{8,10},{10,8},{12,14},{14,12},{1,3},{3,1},... | collective-permute-start | bytes 393224 | tf_op jit(solution)/shard_map/ppermute | solution.py:361
  32.2 8.1 %collective-permute-start.14 = (bf16[32,2048]{1,0:T(8,128)(2,1)S(1)}, bf16[32,2048]{1,0:T(8,128)(2,1)S(1)}, u32[]{:S(2)}, u32[]{:S(2)}) collective-permute-start(bf16[32,2048]{1,0:T(8,128)(2,1)S(1)} %get-tuple-element.70), channel_id=1, source_target_pairs={{0,12},{2,14},{4,8},{6,10},{8,4},{10,6},{12,0},{14,2},{1,13},{3,15... | collective-permute-start | bytes 393224 | tf_op jit(solution)/shard_map/ppermute | solution.py:364
  34.6 6.8 %collective-permute-start.15 = (bf16[32,2048]{1,0:T(8,128)(2,1)S(1)}, bf16[32,2048]{1,0:T(8,128)(2,1)S(1)}, u32[]{:S(2)}, u32[]{:S(2)}) collective-permute-start(bf16[32,2048]{1,0:T(8,128)(2,1)S(1)} %get-tuple-element.73), channel_id=1, source_target_pairs={{0,4},{2,6},{4,0},{6,2},{8,12},{10,14},{12,8},{14,10},{1,5},{3,7},... | collective-permute-start | bytes 393224 | tf_op jit(solution)/shard_map/ppermute | solution.py:364
  37.2 8.6 %collective-permute-start.17 = (bf16[32,2048]{1,0:T(8,128)(2,1)S(1)}, bf16[32,2048]{1,0:T(8,128)(2,1)S(1)}, u32[]{:S(2)}, u32[]{:S(2)}) collective-permute-start(bf16[32,2048]{1,0:T(8,128)(2,1)S(1)} %add_convert_fusion), channel_id=1, source_target_pairs={{0,8},{2,10},{4,12},{6,14},{8,0},{10,2},{12,4},{14,6},{1,9},{3,11}... | collective-permute-start | bytes 393224 | tf_op jit(solution)/shard_map/ppermute | solution.py:364
  45.8 1.3 %collective-permute-start.18 = (bf16[32,1024]{1,0:T(8,128)(2,1)S(1)}, bf16[32,1024]{1,0:T(8,128)(2,1)S(1)}, u32[]{:S(2)}, u32[]{:S(2)}) collective-permute-start(bf16[32,1024]{1,0:T(8,128)(2,1)S(1)} %get-tuple-element.78), channel_id=1, source_target_pairs={{0,1},{1,0},{2,3},{3,2},{4,5},{5,4},{6,7},{7,6},{8,9},{9,8},{10,11... | collective-permute-start | bytes 196616 | tf_op jit(solution)/shard_map/ppermute | solution.py:419

commit v6 on v5

--- a/solution.py
+++ b/solution.py
@@ -378,7 +378,8 @@
     came = [lax.ppermute(w, "head", swap) for w in held]
     block = {0: own}
     block.update({k: column(own, k) for k in mid + [1]})
-    over = {1: pair(block[1])}
+    over = {}
+    over[1] = pair(block[1])
     block[1], own_again = after(block[1], own)
     block[last] = column(own_again, last)
     mark = touch(block[1], *came[:2])
@@ -396,25 +397,31 @@
     done, mark = run_expert(mark, groups, select, weights)
     here.update(zip(keys, done))
     for j, k in enumerate(keys):
-        there[k] = pair(done[len(keys) + j])
+        there[k] = done[len(keys) + j]
+        if k >= 2:
+            there[k] = pair(there[k])
     keys = [last]
     groups = [[v[k]] for v in (block, over) for k in keys]
     done, mark = run_expert(mark, groups, select, weights)
     here.update(zip(keys, done))
     for j, k in enumerate(keys):
-        there[k] = pair(done[len(keys) + j])
+        there[k] = done[len(keys) + j]
+        if k >= 2:
+            there[k] = pair(there[k])
     returned = {}
-    for k in mid + [1, last]:
-        if k in mid + [1]:
-            total, mark = add_rows(mark, here[k], there[k])
-        else:
-            total = add(here[k], there[k])
+    for k in mid:
+        total, mark = add_rows(mark, here[k], there[k])
         returned[k] = column(total, k)
-    terms = [here[0], there[0]]
-    for k in mid + [1]:
-        total, mark = grow(mark, terms + [returned[k]])
-        terms = [total]
-    terms.append(returned[last])
+        for j in (1, 0):
+            mark, there[j] = after(mark, there[j])
+            there[j] = pair(there[j])
+    total = add(here[last], there[last])
+    returned[last] = column(total, last)
+    total, mark = grow(mark, [here[0]] + [returned[k] for k in mid])
+    first, mark = add_rows(mark, here[1], there[1])
+    returned[1] = column(first, 1)
+    total, mark = grow(mark, [total, there[0]])
+    terms = [total, returned[1], returned[last]]
     keep, send = collect(head, terms)
     rest = lax.ppermute(send, "head", swap)
     return place(head, keep, rest)

time: 48 us -> 46.7 us (0.973)
  waiting for transfers between devices: 13.6 us -> 10.4 us
  starting transfers between devices: 24.4 us -> 26.4 us
    ppermute x6, waiting for transfers between devices: 10.1 us -> 3.81 us  [column(): return lax.ppermute(v, 'wide', [(w, w ^ 2 * k) for w in range(n)])]
    ppermute x8, waiting for transfers between devices: 2 us -> 5.06 us  [pair(): return lax.ppermute(v, 'wide', [(w, w ^ 1) for w in range(n)])]
    ppermute x6, starting transfers between devices: 13.8 us -> 16.6 us  [column(): return lax.ppermute(v, 'wide', [(w, w ^ 2 * k) for w in range(n)])]
    ppermute x8, starting transfers between devices: 9.19 us -> 8.46 us  [pair(): return lax.ppermute(v, 'wide', [(w, w ^ 1) for w in range(n)])]
  transfers between devices with their start and end apart: 19 -> 19, of which waited for: 11 -> 10; matrix products, arithmetic and copies ran while one was open for 0% -> 0% of each run, Pallas kernels for 19% -> 19%
where the time goes in v6:
time: 46.7 us; the launch traced here: 46.6 us
  starting transfers between devices  26.4 us (57%)
  waiting for transfers between devices  10.4 us (22%)
  Pallas kernels  9.61 us (21%)
    ppermute x6, starting transfers between devices, column(): return lax.ppermute(v, 'wide', [(w, w ^ 2 * k) for w in range(n)])  16.6 us
    ppermute x8, starting transfers between devices, pair(): return lax.ppermute(v, 'wide', [(w, w ^ 1) for w in range(n)])  8.46 us
    ppermute x8, waiting for transfers between devices, pair(): return lax.ppermute(v, 'wide', [(w, w ^ 1) for w in range(n)])  5.06 us
    pallas_call x2, Pallas kernels, run_expert(): pl.pallas_call(functools.partial(expert_kernel, len(blocks)), out_shape=[...  4.88 us
    ppermute x6, waiting for transfers between devices, column(): return lax.ppermute(v, 'wide', [(w, w ^ 2 * k) for w in range(n)])  3.81 us
    pallas_call x1, Pallas kernels, gather_weights(): pl.pallas_call(functools.partial(gather_kernel, count), out_shape=[jax.Sh...  2.39 us
    ppermute x1, waiting for transfers between devices, dense_local(): rest = lax.ppermute(send, 'head', swap)  1.24 us
  transfers between devices with their start and end apart: 19, of which 10 were waited for; matrix products, arithmetic and copies ran while one was open for 0% of the time, Pallas kernels for 19%

profile of v6, /device:TPU:0, one launch (start us, length us, event | category | flops | bytes accessed | tf_op | source)
XLA Modules:
  0.0 46.6 jit_solution(6368512432809606591)
XLA Ops:
  0.0 0.5 collective-permute-start
  0.5 0.9 %shard_map.64 = (bf16[32,1024]{1,0:T(8,128)(2,1)S(1)}, bf16[32,128]{1,0:T(8,128)(2,1)S(1)}, f32[1,128]{1,0:T(1,128)S(1)}) custom-call(s32[1]{0:T(128)} %bitcast.head_ref, s32[1]{0:T(128)} %bitcast.1.expert_ref, bf16[64,1024]{1,0:T(8,128)(2,1)} %tokens_hbm.1, s32[8,64]{1,0:T(8,128)} %bitcast.13, f32[8,64]{1,0:T(8,128)} %bitcast.14), custom_call_target="tpu_custom_call" | custom-call | bytes 1 | tf_op jit(solution)/shard_map/pallas_call | solution.py:130
  1.4 0.3 collective-permute-done.got_ref
  1.7 0.4 collective-permute-start.2
  2.0 0.1 collective-permute-start.3
  2.2 0.4 collective-permute-start.5
  2.5 2.8 %collective-permute-start.1 = (bf16[32,2176]{1,0:T(8,128)(2,1)S(1)}, bf16[32,2176]{1,0:T(8,128)(2,1)S(1)}, u32[]{:S(2)}, u32[]{:S(2)}) collective-permute-start(bf16[32,2176]{1,0:T(8,128)(2,1)S(1)} %shard_map.65.refs_0_), channel_id=1, source_target_pairs={{0,4},{2,6},{4,0},{6,2},{8,12},{10,14},{12,8},{14,10},{1,5},{3,7},... | collective-permute-start | bytes 417800 | tf_op jit(solution)/shard_map/ppermute | solution.py:364
  5.3 2.5 %collective-permute-start.4 = (bf16[32,2176]{1,0:T(8,128)(2,1)S(1)}, bf16[32,2176]{1,0:T(8,128)(2,1)S(1)}, u32[]{:S(2)}, u32[]{:S(2)}) collective-permute-start(bf16[32,2176]{1,0:T(8,128)(2,1)S(1)} %shard_map.65.refs_0_), channel_id=1, source_target_pairs={{0,12},{2,14},{4,8},{6,10},{8,4},{10,6},{12,0},{14,2},{1,13},{3,15... | collective-permute-start | bytes 417800 | tf_op jit(solution)/shard_map/ppermute | solution.py:364
  7.8 1.7 %collective-permute-done.1.refs_0_.refs_1_ = bf16[32,2176]{1,0:T(8,128)(2,1)S(1)} collective-permute-done((bf16[32,2176]{1,0:T(8,128)(2,1)S(1)}, bf16[32,2176]{1,0:T(8,128)(2,1)S(1)}, u32[]{:S(2)}, u32[]{:S(2)}) %collective-permute-start.1) | collective-permute-done | bytes 139296 | tf_op jit(solution)/shard_map/ppermute | solution.py:364
  9.5 3.3 %collective-permute-start.6 = (bf16[32,2176]{1,0:T(8,128)(2,1)S(1)}, bf16[32,2176]{1,0:T(8,128)(2,1)S(1)}, u32[]{:S(2)}, u32[]{:S(2)}) collective-permute-start(bf16[32,2176]{1,0:T(8,128)(2,1)S(1)} %shard_map.65.refs_0_), channel_id=1, source_target_pairs={{0,8},{2,10},{4,12},{6,14},{8,0},{10,2},{12,4},{14,6},{1,9},{3,11}... | collective-permute-start | bytes 417800 | tf_op jit(solution)/shard_map/ppermute | solution.py:364
  12.8 0.0 collective-permute-done.2.refs_1_.refs_3_
  12.8 1.5 %collective-permute-start.7 = (bf16[32,2176]{1,0:T(8,128)(2,1)S(1)}, bf16[32,2176]{1,0:T(8,128)(2,1)S(1)}, u32[]{:S(2)}, u32[]{:S(2)}) collective-permute-start(bf16[32,2176]{1,0:T(8,128)(2,1)S(1)} %shard_map.65.refs_0_), channel_id=1, source_target_pairs={{0,2},{2,0},{4,6},{6,4},{8,10},{10,8},{12,14},{14,12},{1,3},{3,1},... | collective-permute-start | bytes 417800 | tf_op jit(solution)/shard_map/ppermute | solution.py:361
  14.3 0.0 collective-permute-done.3.refs_2_.refs_4_
  14.3 0.5 %collective-permute-start.8 = (bf16[32,2176]{1,0:T(8,128)(2,1)S(1)}, bf16[32,2176]{1,0:T(8,128)(2,1)S(1)}, u32[]{:S(2)}, u32[]{:S(2)}) collective-permute-start(bf16[32,2176]{1,0:T(8,128)(2,1)S(1)} %collective-permute-done.1.refs_0_.refs_1_), channel_id=1, source_target_pairs={{0,2},{2,0},{4,6},{6,4},{8,10},{10,8},{12,14},{14,12},{1,3},{3,1},... | collective-permute-start | bytes 417800 | tf_op jit(solution)/shard_map/ppermute | solution.py:361
  14.9 0.5 %collective-permute-done.4.refs_2_ = bf16[32,2176]{1,0:T(8,128)(2,1)S(1)} collective-permute-done((bf16[32,2176]{1,0:T(8,128)(2,1)S(1)}, bf16[32,2176]{1,0:T(8,128)(2,1)S(1)}, u32[]{:S(2)}, u32[]{:S(2)}) %collective-permute-start.4) | collective-permute-done | bytes 139296 | tf_op jit(solution)/shard_map/ppermute | solution.py:364
  15.4 1.5 %collective-permute-start.9 = (bf16[32,2176]{1,0:T(8,128)(2,1)S(1)}, bf16[32,2176]{1,0:T(8,128)(2,1)S(1)}, u32[]{:S(2)}, u32[]{:S(2)}) collective-permute-start(bf16[32,2176]{1,0:T(8,128)(2,1)S(1)} %collective-permute-done.4.refs_2_), channel_id=1, source_target_pairs={{0,2},{2,0},{4,6},{6,4},{8,10},{10,8},{12,14},{14,12},{1,3},{3,1},... | collective-permute-start | bytes 417800 | tf_op jit(solution)/shard_map/ppermute | solution.py:361
  16.9 0.0 collective-permute-done.5.refs_5_
  16.9 2.4 %shard_map.67 = (bf16[704,2048]{1,0:T(8,128)(2,1)S(1)}, bf16[704,2048]{1,0:T(8,128)(2,1)S(1)}, bf16[704,2048]{1,0:T(8,128)(2,1)S(1)}, f32[8,128]{1,0:T(8,128)S(1)}) custom-call(f32[8,128]{1,0:T(8,128)S(1)} %shard_map.66._, bf16[352,2048]{1,0:T(8,128)(2,1)} %bitcast.8, bf16[352,2048]{1,0:T(8,128)(2,1)} %bitcast.10, bf16[352,2048]{1,0:T(8,128)(2,1)} %bitcast.12, ...), custom_call_target="tpu_custom_call" | custom-call | bytes 1 | tf_op jit(solution)/shard_map/pallas_call | solution.py:195
  19.3 1.5 %collective-permute-done.6.refs_0_ = bf16[32,2176]{1,0:T(8,128)(2,1)S(1)} collective-permute-done((bf16[32,2176]{1,0:T(8,128)(2,1)S(1)}, bf16[32,2176]{1,0:T(8,128)(2,1)S(1)}, u32[]{:S(2)}, u32[]{:S(2)}) %collective-permute-start.6) | collective-permute-done | bytes 139296 | tf_op jit(solution)/shard_map/ppermute | solution.py:364
  20.7 1.5 %collective-permute-start.10 = (bf16[32,2176]{1,0:T(8,128)(2,1)S(1)}, bf16[32,2176]{1,0:T(8,128)(2,1)S(1)}, u32[]{:S(2)}, u32[]{:S(2)}) collective-permute-start(bf16[32,2176]{1,0:T(8,128)(2,1)S(1)} %collective-permute-done.6.refs_0_), channel_id=1, source_target_pairs={{0,2},{2,0},{4,6},{6,4},{8,10},{10,8},{12,14},{14,12},{1,3},{3,1},... | collective-permute-start | bytes 417800 | tf_op jit(solution)/shard_map/ppermute | solution.py:361
  22.2 0.0 collective-permute-done.7.refs_3_
  22.2 0.0 collective-permute-done.8.refs_4_
  22.2 0.9 %collective-permute-done.9.refs_5_ = bf16[32,2176]{1,0:T(8,128)(2,1)S(1)} collective-permute-done((bf16[32,2176]{1,0:T(8,128)(2,1)S(1)}, bf16[32,2176]{1,0:T(8,128)(2,1)S(1)}, u32[]{:S(2)}, u32[]{:S(2)}) %collective-permute-start.9) | collective-permute-done | bytes 139296 | tf_op jit(solution)/shard_map/ppermute | solution.py:361
  23.1 2.5 %shard_map.68 = (bf16[32,2048]{1,0:T(8,128)(2,1)S(1)}, bf16[32,2048]{1,0:T(8,128)(2,1)S(1)}, bf16[32,2048]{1,0:T(8,128)(2,1)S(1)}, bf16[32,2048]{1,0:T(8,128)(2,...) custom-call(f32[8,128]{1,0:T(8,128)S(1)} %get-tuple-element.57._, ...), custom_call_target="tpu_custom_call" | custom-call | bytes 1 | tf_op jit(solution)/shard_map/pallas_call | solution.py:252
  25.6 1.6 %collective-permute-start.11 = (bf16[32,2048]{1,0:T(8,128)(2,1)S(1)}, bf16[32,2048]{1,0:T(8,128)(2,1)S(1)}, u32[]{:S(2)}, u32[]{:S(2)}) collective-permute-start(bf16[32,2048]{1,0:T(8,128)(2,1)S(1)} %get-tuple-element.67), channel_id=1, source_target_pairs={{0,2},{2,0},{4,6},{6,4},{8,10},{10,8},{12,14},{14,12},{1,3},{3,1},... | collective-permute-start | bytes 393224 | tf_op jit(solution)/shard_map/ppermute | solution.py:361
  27.2 0.0 collective-permute-done.10.refs_1_
  27.2 2.3 %shard_map.69 = (bf16[32,2048]{1,0:T(8,128)(2,1)S(1)}, bf16[32,2048]{1,0:T(8,128)(2,1)S(1)}, f32[8,128]{1,0:T(8,128)S(1)}) custom-call(f32[8,128]{1,0:T(8,128)S(1)} %get-tuple-element.63._, f32[1,128]{1,0:T(1,128)S(1)} %get-tuple-element.58.select_ref, bf16[32,2176]{1,0:T(8,128)(2,1)S(1)} %collective-permute-done.6.refs_0_, ...), custom_call_target="tpu_custom_call" | custom-call | bytes 1 | tf_op jit(solution)/shard_map/pallas_call | solution.py:252
  29.5 0.8 %collective-permute-start.16 = (bf16[32,2048]{1,0:T(8,128)(2,1)S(1)}, bf16[32,2048]{1,0:T(8,128)(2,1)S(1)}, u32[]{:S(2)}, u32[]{:S(2)}) collective-permute-start(bf16[32,2048]{1,0:T(8,128)(2,1)S(1)} %get-tuple-element.84), channel_id=1, source_target_pairs={{0,2},{2,0},{4,6},{6,4},{8,10},{10,8},{12,14},{14,12},{1,3},{3,1},... | collective-permute-start | bytes 393224 | tf_op jit(solution)/shard_map/ppermute | solution.py:361
  30.4 0.3 collective-permute-done.11.b_ref
  30.7 2.7 %collective-permute-start.12 = (bf16[32,2048]{1,0:T(8,128)(2,1)S(1)}, bf16[32,2048]{1,0:T(8,128)(2,1)S(1)}, u32[]{:S(2)}, u32[]{:S(2)}) collective-permute-start(bf16[32,2048]{1,0:T(8,128)(2,1)S(1)} %get-tuple-element.74), channel_id=1, source_target_pairs={{0,12},{2,14},{4,8},{6,10},{8,4},{10,6},{12,0},{14,2},{1,13},{3,15... | collective-permute-start | bytes 393224 | tf_op jit(solution)/shard_map/ppermute | solution.py:364
  33.4 0.8 %collective-permute-start.13 = (bf16[32,2048]{1,0:T(8,128)(2,1)S(1)}, bf16[32,2048]{1,0:T(8,128)(2,1)S(1)}, u32[]{:S(2)}, u32[]{:S(2)}) collective-permute-start(bf16[32,2048]{1,0:T(8,128)(2,1)S(1)} %get-tuple-element.77), channel_id=1, source_target_pairs={{0,2},{2,0},{4,6},{6,4},{8,10},{10,8},{12,14},{14,12},{1,3},{3,1},... | collective-permute-start | bytes 393224 | tf_op jit(solution)/shard_map/ppermute | solution.py:361
  34.2 1.7 %collective-permute-done.16 = bf16[32,2048]{1,0:T(8,128)(2,1)S(1)} collective-permute-done((bf16[32,2048]{1,0:T(8,128)(2,1)S(1)}, bf16[32,2048]{1,0:T(8,128)(2,1)S(1)}, u32[]{:S(2)}, u32[]{:S(2)}) %collective-permute-start.16) | collective-permute-done | bytes 131104 | tf_op jit(solution)/shard_map/ppermute | solution.py:361
  35.9 2.9 %collective-permute-start.17 = (bf16[32,2048]{1,0:T(8,128)(2,1)S(1)}, bf16[32,2048]{1,0:T(8,128)(2,1)S(1)}, u32[]{:S(2)}, u32[]{:S(2)}) collective-permute-start(bf16[32,2048]{1,0:T(8,128)(2,1)S(1)} %add_convert_fusion), channel_id=1, source_target_pairs={{0,8},{2,10},{4,12},{6,14},{8,0},{10,2},{12,4},{14,6},{1,9},{3,11}... | collective-permute-start | bytes 393224 | tf_op jit(solution)/shard_map/ppermute | solution.py:364
  38.8 0.3 collective-permute-start.14
  39.1 0.0 collective-permute-done.12.refs_1_
  39.1 0.0 collective-permute-done.13.b_ref
  39.2 2.4 %collective-permute-start.15 = (bf16[32,2048]{1,0:T(8,128)(2,1)S(1)}, bf16[32,2048]{1,0:T(8,128)(2,1)S(1)}, u32[]{:S(2)}, u32[]{:S(2)}) collective-permute-start(bf16[32,2048]{1,0:T(8,128)(2,1)S(1)} %get-tuple-element.82), channel_id=1, source_target_pairs={{0,4},{2,6},{4,0},{6,2},{8,12},{10,14},{12,8},{14,10},{1,5},{3,7},... | collective-permute-start | bytes 393224 | tf_op jit(solution)/shard_map/ppermute | solution.py:364
  41.6 2.2 %collective-permute-done.14.refs_1_ = bf16[32,2048]{1,0:T(8,128)(2,1)S(1)} collective-permute-done((bf16[32,2048]{1,0:T(8,128)(2,1)S(1)}, bf16[32,2048]{1,0:T(8,128)(2,1)S(1)}, u32[]{:S(2)}, u32[]{:S(2)}) %collective-permute-start.14) | collective-permute-done | bytes 131104 | tf_op jit(solution)/shard_map/ppermute | solution.py:361
  43.8 0.6 %shard_map.73 = (f32[32,2048]{1,0:T(8,128)S(1)}, f32[8,128]{1,0:T(8,128)}) custom-call(f32[8,128]{1,0:T(8,128)S(1)} %get-tuple-element.78._, f32[32,2048]{1,0:T(8,128)S(1)} %get-tuple-element.79.refs_0_, bf16[32,2048]{1,0:T(8,128)(2,1)S(1)} %collective-permute-done.14.refs_1_), custom_call_target="tpu_custom_call" | custom-call | bytes 1000000 | tf_op jit(solution)/shard_map/pallas_call | solution.py:293
  44.4 0.0 collective-permute-done.17.refs_2_
  44.4 0.1 collective-permute-done.15.refs_1_
  44.5 0.1 shard_map.74
  44.6 0.1 collective-permute-start.18
  44.7 1.2 %collective-permute-done.18.rest_ref = bf16[32,1024]{1,0:T(8,128)(2,1)S(1)} collective-permute-done((bf16[32,1024]{1,0:T(8,128)(2,1)S(1)}, bf16[32,1024]{1,0:T(8,128)(2,1)S(1)}, u32[]{:S(2)}, u32[]{:S(2)}) %collective-permute-start.18) | collective-permute-done | bytes 65568 | tf_op jit(solution)/shard_map/ppermute | solution.py:426
  45.9 0.7 %shard_map.75 = bf16[64,1024]{1,0:T(8,128)(2,1)} custom-call(s32[1]{0:T(128)} %bitcast.head_ref, bf16[32,1024]{1,0:T(8,128)(2,1)S(1)} %get-tuple-element.85.keep_ref, bf16[32,1024]{1,0:T(8,128)(2,1)S(1)} %collective-permute-done.18.rest_ref), custom_call_target="tpu_custom_call" | custom-call | bytes 1 | tf_op jit(solution)/shard_map/pallas_call | solution.py:338
  (6 shorter events, 0.1 us)
Async XLA Ops:
  0.0 1.6 %collective-permute-start = (bf16[64,1024]{1,0:T(8,128)(2,1)}, bf16[64,1024]{1,0:T(8,128)(2,1)S(1)}, u32[]{:S(2)}, u32[]{:S(2)}) collective-permute-start(bf16[64,1024]{1,0:T(8,128)(2,1)} %tokens_hbm.1), channel_id=1, source_target_pairs={{0,1},{1,0},{2,3},{3,2},{4,5},{5,4},{6,7},{7,6},{8,9},{9,8},{10,11... | collective-permute-start | bytes 393224 | tf_op jit(solution)/shard_map/ppermute | solution.py:369
  1.7 11.2 %collective-permute-start.2 = (bf16[352,2048]{1,0:T(8,128)(2,1)}, bf16[352,2048]{1,0:T(8,128)(2,1)S(1)}, u32[]{:S(2)}, u32[]{:S(2)}) collective-permute-start(bf16[352,2048]{1,0:T(8,128)(2,1)} %bitcast.7), channel_id=1, source_target_pairs={{0,1},{1,0},{2,3},{3,2},{4,5},{5,4},{6,7},{7,6},{8,9},{9,8},{10,11... | collective-permute-start | bytes 4325384 | tf_op jit(solution)/shard_map/ppermute | solution.py:378
  2.0 12.3 %collective-permute-start.3 = (bf16[352,2048]{1,0:T(8,128)(2,1)}, bf16[352,2048]{1,0:T(8,128)(2,1)S(1)}, u32[]{:S(2)}, u32[]{:S(2)}) collective-permute-start(bf16[352,2048]{1,0:T(8,128)(2,1)} %bitcast.9), channel_id=1, source_target_pairs={{0,1},{1,0},{2,3},{3,2},{4,5},{5,4},{6,7},{7,6},{8,9},{9,8},{10,11... | collective-permute-start | bytes 4325384 | tf_op jit(solution)/shard_map/ppermute | solution.py:378
  2.2 14.7 %collective-permute-start.5 = (bf16[352,2048]{1,0:T(8,128)(2,1)}, bf16[352,2048]{1,0:T(8,128)(2,1)S(1)}, u32[]{:S(2)}, u32[]{:S(2)}) collective-permute-start(bf16[352,2048]{1,0:T(8,128)(2,1)} %bitcast.11), channel_id=1, source_target_pairs={{0,1},{1,0},{2,3},{3,2},{4,5},{5,4},{6,7},{7,6},{8,9},{9,8},{10,11... | collective-permute-start | bytes 4325384 | tf_op jit(solution)/shard_map/ppermute | solution.py:378
  2.5 7.0 %collective-permute-start.1 = (bf16[32,2176]{1,0:T(8,128)(2,1)S(1)}, bf16[32,2176]{1,0:T(8,128)(2,1)S(1)}, u32[]{:S(2)}, u32[]{:S(2)}) collective-permute-start(bf16[32,2176]{1,0:T(8,128)(2,1)S(1)} %shard_map.65.refs_0_), channel_id=1, source_target_pairs={{0,4},{2,6},{4,0},{6,2},{8,12},{10,14},{12,8},{14,10},{1,5},{3,7},... | collective-permute-start | bytes 417800 | tf_op jit(solution)/shard_map/ppermute | solution.py:364
  5.3 10.0 %collective-permute-start.4 = (bf16[32,2176]{1,0:T(8,128)(2,1)S(1)}, bf16[32,2176]{1,0:T(8,128)(2,1)S(1)}, u32[]{:S(2)}, u32[]{:S(2)}) collective-permute-start(bf16[32,2176]{1,0:T(8,128)(2,1)S(1)} %shard_map.65.refs_0_), channel_id=1, source_target_pairs={{0,12},{2,14},{4,8},{6,10},{8,4},{10,6},{12,0},{14,2},{1,13},{3,15... | collective-permute-start | bytes 417800 | tf_op jit(solution)/shard_map/ppermute | solution.py:364
  9.5 11.2 %collective-permute-start.6 = (bf16[32,2176]{1,0:T(8,128)(2,1)S(1)}, bf16[32,2176]{1,0:T(8,128)(2,1)S(1)}, u32[]{:S(2)}, u32[]{:S(2)}) collective-permute-start(bf16[32,2176]{1,0:T(8,128)(2,1)S(1)} %shard_map.65.refs_0_), channel_id=1, source_target_pairs={{0,8},{2,10},{4,12},{6,14},{8,0},{10,2},{12,4},{14,6},{1,9},{3,11}... | collective-permute-start | bytes 417800 | tf_op jit(solution)/shard_map/ppermute | solution.py:364
  12.8 9.4 %collective-permute-start.7 = (bf16[32,2176]{1,0:T(8,128)(2,1)S(1)}, bf16[32,2176]{1,0:T(8,128)(2,1)S(1)}, u32[]{:S(2)}, u32[]{:S(2)}) collective-permute-start(bf16[32,2176]{1,0:T(8,128)(2,1)S(1)} %shard_map.65.refs_0_), channel_id=1, source_target_pairs={{0,2},{2,0},{4,6},{6,4},{8,10},{10,8},{12,14},{14,12},{1,3},{3,1},... | collective-permute-start | bytes 417800 | tf_op jit(solution)/shard_map/ppermute | solution.py:361
  14.3 7.9 %collective-permute-start.8 = (bf16[32,2176]{1,0:T(8,128)(2,1)S(1)}, bf16[32,2176]{1,0:T(8,128)(2,1)S(1)}, u32[]{:S(2)}, u32[]{:S(2)}) collective-permute-start(bf16[32,2176]{1,0:T(8,128)(2,1)S(1)} %collective-permute-done.1.refs_0_.refs_1_), channel_id=1, source_target_pairs={{0,2},{2,0},{4,6},{6,4},{8,10},{10,8},{12,14},{14,12},{1,3},{3,1},... | collective-permute-start | bytes 417800 | tf_op jit(solution)/shard_map/ppermute | solution.py:361
  15.4 7.7 %collective-permute-start.9 = (bf16[32,2176]{1,0:T(8,128)(2,1)S(1)}, bf16[32,2176]{1,0:T(8,128)(2,1)S(1)}, u32[]{:S(2)}, u32[]{:S(2)}) collective-permute-start(bf16[32,2176]{1,0:T(8,128)(2,1)S(1)} %collective-permute-done.4.refs_2_), channel_id=1, source_target_pairs={{0,2},{2,0},{4,6},{6,4},{8,10},{10,8},{12,14},{14,12},{1,3},{3,1},... | collective-permute-start | bytes 417800 | tf_op jit(solution)/shard_map/ppermute | solution.py:361
  20.7 6.5 %collective-permute-start.10 = (bf16[32,2176]{1,0:T(8,128)(2,1)S(1)}, bf16[32,2176]{1,0:T(8,128)(2,1)S(1)}, u32[]{:S(2)}, u32[]{:S(2)}) collective-permute-start(bf16[32,2176]{1,0:T(8,128)(2,1)S(1)} %collective-permute-done.6.refs_0_), channel_id=1, source_target_pairs={{0,2},{2,0},{4,6},{6,4},{8,10},{10,8},{12,14},{14,12},{1,3},{3,1},... | collective-permute-start | bytes 417800 | tf_op jit(solution)/shard_map/ppermute | solution.py:361
  25.6 5.0 %collective-permute-start.11 = (bf16[32,2048]{1,0:T(8,128)(2,1)S(1)}, bf16[32,2048]{1,0:T(8,128)(2,1)S(1)}, u32[]{:S(2)}, u32[]{:S(2)}) collective-permute-start(bf16[32,2048]{1,0:T(8,128)(2,1)S(1)} %get-tuple-element.67), channel_id=1, source_target_pairs={{0,2},{2,0},{4,6},{6,4},{8,10},{10,8},{12,14},{14,12},{1,3},{3,1},... | collective-permute-start | bytes 393224 | tf_op jit(solution)/shard_map/ppermute | solution.py:361
  29.5 6.3 %collective-permute-start.16 = (bf16[32,2048]{1,0:T(8,128)(2,1)S(1)}, bf16[32,2048]{1,0:T(8,128)(2,1)S(1)}, u32[]{:S(2)}, u32[]{:S(2)}) collective-permute-start(bf16[32,2048]{1,0:T(8,128)(2,1)S(1)} %get-tuple-element.84), channel_id=1, source_target_pairs={{0,2},{2,0},{4,6},{6,4},{8,10},{10,8},{12,14},{14,12},{1,3},{3,1},... | collective-permute-start | bytes 393224 | tf_op jit(solution)/shard_map/ppermute | solution.py:361
  30.7 8.4 %collective-permute-start.12 = (bf16[32,2048]{1,0:T(8,128)(2,1)S(1)}, bf16[32,2048]{1,0:T(8,128)(2,1)S(1)}, u32[]{:S(2)}, u32[]{:S(2)}) collective-permute-start(bf16[32,2048]{1,0:T(8,128)(2,1)S(1)} %get-tuple-element.74), channel_id=1, source_target_pairs={{0,12},{2,14},{4,8},{6,10},{8,4},{10,6},{12,0},{14,2},{1,13},{3,15... | collective-permute-start | bytes 393224 | tf_op jit(solution)/shard_map/ppermute | solution.py:364
  33.4 5.7 %collective-permute-start.13 = (bf16[32,2048]{1,0:T(8,128)(2,1)S(1)}, bf16[32,2048]{1,0:T(8,128)(2,1)S(1)}, u32[]{:S(2)}, u32[]{:S(2)}) collective-permute-start(bf16[32,2048]{1,0:T(8,128)(2,1)S(1)} %get-tuple-element.77), channel_id=1, source_target_pairs={{0,2},{2,0},{4,6},{6,4},{8,10},{10,8},{12,14},{14,12},{1,3},{3,1},... | collective-permute-start | bytes 393224 | tf_op jit(solution)/shard_map/ppermute | solution.py:361
  35.9 8.5 %collective-permute-start.17 = (bf16[32,2048]{1,0:T(8,128)(2,1)S(1)}, bf16[32,2048]{1,0:T(8,128)(2,1)S(1)}, u32[]{:S(2)}, u32[]{:S(2)}) collective-permute-start(bf16[32,2048]{1,0:T(8,128)(2,1)S(1)} %add_convert_fusion), channel_id=1, source_target_pairs={{0,8},{2,10},{4,12},{6,14},{8,0},{10,2},{12,4},{14,6},{1,9},{3,11}... | collective-permute-start | bytes 393224 | tf_op jit(solution)/shard_map/ppermute | solution.py:364
  38.8 5.0 %collective-permute-start.14 = (bf16[32,2048]{1,0:T(8,128)(2,1)S(1)}, bf16[32,2048]{1,0:T(8,128)(2,1)S(1)}, u32[]{:S(2)}, u32[]{:S(2)}) collective-permute-start(bf16[32,2048]{1,0:T(8,128)(2,1)S(1)} %get-tuple-element.80), channel_id=1, source_target_pairs={{0,2},{2,0},{4,6},{6,4},{8,10},{10,8},{12,14},{14,12},{1,3},{3,1},... | collective-permute-start | bytes 393224 | tf_op jit(solution)/shard_map/ppermute | solution.py:361
  39.2 5.3 %collective-permute-start.15 = (bf16[32,2048]{1,0:T(8,128)(2,1)S(1)}, bf16[32,2048]{1,0:T(8,128)(2,1)S(1)}, u32[]{:S(2)}, u32[]{:S(2)}) collective-permute-start(bf16[32,2048]{1,0:T(8,128)(2,1)S(1)} %get-tuple-element.82), channel_id=1, source_target_pairs={{0,4},{2,6},{4,0},{6,2},{8,12},{10,14},{12,8},{14,10},{1,5},{3,7},... | collective-permute-start | bytes 393224 | tf_op jit(solution)/shard_map/ppermute | solution.py:364
  44.6 1.3 %collective-permute-start.18 = (bf16[32,1024]{1,0:T(8,128)(2,1)S(1)}, bf16[32,1024]{1,0:T(8,128)(2,1)S(1)}, u32[]{:S(2)}, u32[]{:S(2)}) collective-permute-start(bf16[32,1024]{1,0:T(8,128)(2,1)S(1)} %get-tuple-element.86), channel_id=1, source_target_pairs={{0,1},{1,0},{2,3},{3,2},{4,5},{5,4},{6,7},{7,6},{8,9},{9,8},{10,11... | collective-permute-start | bytes 196616 | tf_op jit(solution)/shard_map/ppermute | solution.py:426

commit v7 on v6

--- a/solution.py
+++ b/solution.py
@@ -22,7 +22,6 @@
 GATHER_COST = 1
 TOUCH_COST = 1000000
 EXPERT_COST = 1
-ADD_COST = 1000000
 
 
 def sparse_local(tokens, expert_ids, gate_scores, gate_proj, up_proj, down_proj):
@@ -262,48 +261,7 @@
     return outs, mark
 
 
-def add_kernel(_, a_ref, b_ref, out_ref, mark):
-    out_ref[...] = (a_ref[...].astype(jnp.float32) + b_ref[...].astype(jnp.float32)).astype(
-        jnp.bfloat16
-    )
-    mark[...] = jnp.zeros(mark.shape, mark.dtype)
-
-
-def add_rows(mark, a, b):
-    return pl.pallas_call(
-        add_kernel,
-        out_shape=[
-            jax.ShapeDtypeStruct(a.shape, jnp.bfloat16),
-            jax.ShapeDtypeStruct(MARK, jnp.float32),
-        ],
-        in_specs=[pl.BlockSpec(memory_space=pl.ANY)] + [in_vmem()] * 2,
-        out_specs=[in_vmem()] * 2,
-        compiler_params=pltpu.CompilerParams(vmem_limit_bytes=SMALL_LIMIT),
-        cost_estimate=cost(ADD_COST),
-    )(mark, a, b)
-
-
-def grow_kernel(count, _, *refs):
-    terms, total_ref, mark = refs[:count], refs[count], refs[count + 1]
-    total_ref[...] = sum(t[...].astype(jnp.float32) for t in terms)
-    mark[...] = jnp.zeros(mark.shape, mark.dtype)
-
-
-def grow(mark, terms):
-    return pl.pallas_call(
-        functools.partial(grow_kernel, len(terms)),
-        out_shape=[
-            jax.ShapeDtypeStruct(terms[0].shape, jnp.float32),
-            jax.ShapeDtypeStruct(MARK, jnp.float32),
-        ],
-        in_specs=[pl.BlockSpec(memory_space=pl.ANY)] + [in_vmem()] * len(terms),
-        out_specs=[in_vmem()] * 2,
-        compiler_params=pltpu.CompilerParams(vmem_limit_bytes=SMALL_LIMIT),
-        cost_estimate=cost(ADD_COST),
-    )(mark, *terms)
-
-
-def collect_kernel(count, head_ref, *refs):
+def collect_kernel(count, head_ref, _, *refs):
     terms, keep_ref, send_ref = refs[:count], refs[count], refs[count + 1]
     half = keep_ref.shape[1]
     first = head_ref[0] == 0
@@ -313,16 +271,17 @@
     send_ref[...] = jnp.where(first, right, left)
 
 
-def collect(head, terms):
+def collect(head, mark, terms):
     part, width = terms[0].shape
     return pl.pallas_call(
         functools.partial(collect_kernel, len(terms)),
         out_shape=[jax.ShapeDtypeStruct((part, width // 2), jnp.bfloat16)] * 2,
-        in_specs=[pl.BlockSpec(memory_space=pltpu.SMEM)] + [in_vmem()] * len(terms),
+        in_specs=[pl.BlockSpec(memory_space=pltpu.SMEM), pl.BlockSpec(memory_space=pl.ANY)]
+        + [in_vmem()] * len(terms),
         out_specs=[in_vmem()] * 2,
         compiler_params=pltpu.CompilerParams(vmem_limit_bytes=SMALL_LIMIT),
         cost_estimate=NO_COST,
-    )(head, *terms)
+    )(head, mark, *terms)
 
 
 def place_kernel(head_ref, keep_ref, rest_ref, out_ref):
@@ -410,19 +369,17 @@
             there[k] = pair(there[k])
     returned = {}
     for k in mid:
-        total, mark = add_rows(mark, here[k], there[k])
-        returned[k] = column(total, k)
-        for j in (1, 0):
-            mark, there[j] = after(mark, there[j])
-            there[j] = pair(there[j])
-    total = add(here[last], there[last])
-    returned[last] = column(total, last)
-    total, mark = grow(mark, [here[0]] + [returned[k] for k in mid])
-    first, mark = add_rows(mark, here[1], there[1])
-    returned[1] = column(first, 1)
-    total, mark = grow(mark, [total, there[0]])
-    terms = [total, returned[1], returned[last]]
-    keep, send = collect(head, terms)
+        returned[k] = column(add(here[k], there[k]), k)
+        mark = touch(mark, there[k])
+    for k in (1, 0):
+        mark, there[k] = after(mark, there[k])
+        there[k] = pair(there[k])
+    returned[last] = column(add(here[last], there[last]), last)
+    mark = touch(mark, *[returned[k] for k in mid])
+    mark, there[1] = after(mark, there[1])
+    returned[1] = column(add(here[1], there[1]), 1)
+    terms = [here[0], there[0], *returned.values()]
+    keep, send = collect(head, mark, terms)
     rest = lax.ppermute(send, "head", swap)
     return place(head, keep, rest)
 

time: 46.7 us -> 46.7 us (level)
  Pallas kernels: 9.61 us -> 8.95 us
  waiting for transfers between devices: 10.4 us -> 11 us
    ppermute x6, waiting for transfers between devices: 3.81 us -> 5.09 us  [column(): return lax.ppermute(v, 'wide', [(w, w ^ 2 * k) for w in range(n)])]
    pallas_call x4 -> x0, Pallas kernels: 0.71 us -> none  [the longest x2 0.64 us: grow(): pl.pallas_call(functools.partial(grow_kernel, len(terms)), out_shape=[jax...]
    ppermute x8, waiting for transfers between devices: 5.06 us -> 4.38 us  [pair(): return lax.ppermute(v, 'wide', [(w, w ^ 1) for w in range(n)])]
  transfers between devices with their start and end apart: 19 -> 19, of which waited for: 10 -> 11; matrix products, arithmetic and copies ran while one was open for 0% -> 0% of each run, Pallas kernels for 19% -> 18%
where the time goes in v7:
time: 46.7 us; the launch traced here: 46.6 us
  starting transfers between devices  26.4 us (57%)
  waiting for transfers between devices  11 us (24%)
  Pallas kernels  8.95 us (19%)
    ppermute x6, starting transfers between devices, column(): return lax.ppermute(v, 'wide', [(w, w ^ 2 * k) for w in range(n)])  16.6 us
    ppermute x8, starting transfers between devices, pair(): return lax.ppermute(v, 'wide', [(w, w ^ 1) for w in range(n)])  8.45 us
    ppermute x6, waiting for transfers between devices, column(): return lax.ppermute(v, 'wide', [(w, w ^ 2 * k) for w in range(n)])  5.09 us
    pallas_call x2, Pallas kernels, run_expert(): pl.pallas_call(functools.partial(expert_kernel, len(blocks)), out_shape=[...  4.88 us
    ppermute x8, waiting for transfers between devices, pair(): return lax.ppermute(v, 'wide', [(w, w ^ 1) for w in range(n)])  4.38 us
    pallas_call x1, Pallas kernels, gather_weights(): pl.pallas_call(functools.partial(gather_kernel, count), out_shape=[jax.Sh...  2.39 us
    ppermute x1, waiting for transfers between devices, dense_local(): rest = lax.ppermute(send, 'head', swap)  1.24 us
  transfers between devices with their start and end apart: 19, of which 11 were waited for; matrix products, arithmetic and copies ran while one was open for 0% of the time, Pallas kernels for 18%

profile of v7, /device:TPU:0, one launch (start us, length us, event | category | flops | bytes accessed | tf_op | source)
XLA Modules:
  0.0 46.6 jit_solution(11325788073835772366)
XLA Ops:
  0.0 0.5 collective-permute-start
  0.5 0.9 %shard_map.64 = (bf16[32,1024]{1,0:T(8,128)(2,1)S(1)}, bf16[32,128]{1,0:T(8,128)(2,1)S(1)}, f32[1,128]{1,0:T(1,128)S(1)}) custom-call(s32[1]{0:T(128)} %bitcast.head_ref, s32[1]{0:T(128)} %bitcast.1.expert_ref, bf16[64,1024]{1,0:T(8,128)(2,1)} %tokens_hbm.1, s32[8,64]{1,0:T(8,128)} %bitcast.13, f32[8,64]{1,0:T(8,128)} %bitcast.14), custom_call_target="tpu_custom_call" | custom-call | bytes 1 | tf_op jit(solution)/shard_map/pallas_call | solution.py:129
  1.4 0.3 collective-permute-done.got_ref
  1.7 0.4 collective-permute-start.2
  2.0 0.1 collective-permute-start.3
  2.2 0.4 collective-permute-start.5
  2.5 2.8 %collective-permute-start.1 = (bf16[32,2176]{1,0:T(8,128)(2,1)S(1)}, bf16[32,2176]{1,0:T(8,128)(2,1)S(1)}, u32[]{:S(2)}, u32[]{:S(2)}) collective-permute-start(bf16[32,2176]{1,0:T(8,128)(2,1)S(1)} %shard_map.65.refs_0_), channel_id=1, source_target_pairs={{0,4},{2,6},{4,0},{6,2},{8,12},{10,14},{12,8},{14,10},{1,5},{3,7},... | collective-permute-start | bytes 417800 | tf_op jit(solution)/shard_map/ppermute | solution.py:323
  5.3 2.5 %collective-permute-start.4 = (bf16[32,2176]{1,0:T(8,128)(2,1)S(1)}, bf16[32,2176]{1,0:T(8,128)(2,1)S(1)}, u32[]{:S(2)}, u32[]{:S(2)}) collective-permute-start(bf16[32,2176]{1,0:T(8,128)(2,1)S(1)} %shard_map.65.refs_0_), channel_id=1, source_target_pairs={{0,12},{2,14},{4,8},{6,10},{8,4},{10,6},{12,0},{14,2},{1,13},{3,15... | collective-permute-start | bytes 417800 | tf_op jit(solution)/shard_map/ppermute | solution.py:323
  7.8 1.7 %collective-permute-done.1.refs_0_.refs_1_ = bf16[32,2176]{1,0:T(8,128)(2,1)S(1)} collective-permute-done((bf16[32,2176]{1,0:T(8,128)(2,1)S(1)}, bf16[32,2176]{1,0:T(8,128)(2,1)S(1)}, u32[]{:S(2)}, u32[]{:S(2)}) %collective-permute-start.1) | collective-permute-done | bytes 139296 | tf_op jit(solution)/shard_map/ppermute | solution.py:323
  9.5 3.3 %collective-permute-start.6 = (bf16[32,2176]{1,0:T(8,128)(2,1)S(1)}, bf16[32,2176]{1,0:T(8,128)(2,1)S(1)}, u32[]{:S(2)}, u32[]{:S(2)}) collective-permute-start(bf16[32,2176]{1,0:T(8,128)(2,1)S(1)} %shard_map.65.refs_0_), channel_id=1, source_target_pairs={{0,8},{2,10},{4,12},{6,14},{8,0},{10,2},{12,4},{14,6},{1,9},{3,11}... | collective-permute-start | bytes 417800 | tf_op jit(solution)/shard_map/ppermute | solution.py:323
  12.8 0.0 collective-permute-done.2.refs_1_.refs_3_
  12.8 1.5 %collective-permute-start.7 = (bf16[32,2176]{1,0:T(8,128)(2,1)S(1)}, bf16[32,2176]{1,0:T(8,128)(2,1)S(1)}, u32[]{:S(2)}, u32[]{:S(2)}) collective-permute-start(bf16[32,2176]{1,0:T(8,128)(2,1)S(1)} %shard_map.65.refs_0_), channel_id=1, source_target_pairs={{0,2},{2,0},{4,6},{6,4},{8,10},{10,8},{12,14},{14,12},{1,3},{3,1},... | collective-permute-start | bytes 417800 | tf_op jit(solution)/shard_map/ppermute | solution.py:320
  14.3 0.0 collective-permute-done.3.refs_2_.refs_4_
  14.3 0.5 %collective-permute-start.8 = (bf16[32,2176]{1,0:T(8,128)(2,1)S(1)}, bf16[32,2176]{1,0:T(8,128)(2,1)S(1)}, u32[]{:S(2)}, u32[]{:S(2)}) collective-permute-start(bf16[32,2176]{1,0:T(8,128)(2,1)S(1)} %collective-permute-done.1.refs_0_.refs_1_), channel_id=1, source_target_pairs={{0,2},{2,0},{4,6},{6,4},{8,10},{10,8},{12,14},{14,12},{1,3},{3,1},... | collective-permute-start | bytes 417800 | tf_op jit(solution)/shard_map/ppermute | solution.py:320
  14.9 0.5 %collective-permute-done.4.refs_2_ = bf16[32,2176]{1,0:T(8,128)(2,1)S(1)} collective-permute-done((bf16[32,2176]{1,0:T(8,128)(2,1)S(1)}, bf16[32,2176]{1,0:T(8,128)(2,1)S(1)}, u32[]{:S(2)}, u32[]{:S(2)}) %collective-permute-start.4) | collective-permute-done | bytes 139296 | tf_op jit(solution)/shard_map/ppermute | solution.py:323
  15.4 1.5 %collective-permute-start.9 = (bf16[32,2176]{1,0:T(8,128)(2,1)S(1)}, bf16[32,2176]{1,0:T(8,128)(2,1)S(1)}, u32[]{:S(2)}, u32[]{:S(2)}) collective-permute-start(bf16[32,2176]{1,0:T(8,128)(2,1)S(1)} %collective-permute-done.4.refs_2_), channel_id=1, source_target_pairs={{0,2},{2,0},{4,6},{6,4},{8,10},{10,8},{12,14},{14,12},{1,3},{3,1},... | collective-permute-start | bytes 417800 | tf_op jit(solution)/shard_map/ppermute | solution.py:320
  16.9 0.0 collective-permute-done.5.refs_5_
  16.9 2.4 %shard_map.67 = (bf16[704,2048]{1,0:T(8,128)(2,1)S(1)}, bf16[704,2048]{1,0:T(8,128)(2,1)S(1)}, bf16[704,2048]{1,0:T(8,128)(2,1)S(1)}, f32[8,128]{1,0:T(8,128)S(1)}) custom-call(f32[8,128]{1,0:T(8,128)S(1)} %shard_map.66._, bf16[352,2048]{1,0:T(8,128)(2,1)} %bitcast.8, bf16[352,2048]{1,0:T(8,128)(2,1)} %bitcast.10, bf16[352,2048]{1,0:T(8,128)(2,1)} %bitcast.12, ...), custom_call_target="tpu_custom_call" | custom-call | bytes 1 | tf_op jit(solution)/shard_map/pallas_call | solution.py:194
  19.3 1.5 %collective-permute-done.6.refs_0_ = bf16[32,2176]{1,0:T(8,128)(2,1)S(1)} collective-permute-done((bf16[32,2176]{1,0:T(8,128)(2,1)S(1)}, bf16[32,2176]{1,0:T(8,128)(2,1)S(1)}, u32[]{:S(2)}, u32[]{:S(2)}) %collective-permute-start.6) | collective-permute-done | bytes 139296 | tf_op jit(solution)/shard_map/ppermute | solution.py:323
  20.7 1.5 %collective-permute-start.10 = (bf16[32,2176]{1,0:T(8,128)(2,1)S(1)}, bf16[32,2176]{1,0:T(8,128)(2,1)S(1)}, u32[]{:S(2)}, u32[]{:S(2)}) collective-permute-start(bf16[32,2176]{1,0:T(8,128)(2,1)S(1)} %collective-permute-done.6.refs_0_), channel_id=1, source_target_pairs={{0,2},{2,0},{4,6},{6,4},{8,10},{10,8},{12,14},{14,12},{1,3},{3,1},... | collective-permute-start | bytes 417800 | tf_op jit(solution)/shard_map/ppermute | solution.py:320
  22.2 0.0 collective-permute-done.7.refs_3_
  22.2 0.0 collective-permute-done.8.refs_4_
  22.2 0.9 %collective-permute-done.9.refs_5_ = bf16[32,2176]{1,0:T(8,128)(2,1)S(1)} collective-permute-done((bf16[32,2176]{1,0:T(8,128)(2,1)S(1)}, bf16[32,2176]{1,0:T(8,128)(2,1)S(1)}, u32[]{:S(2)}, u32[]{:S(2)}) %collective-permute-start.9) | collective-permute-done | bytes 139296 | tf_op jit(solution)/shard_map/ppermute | solution.py:320
  23.1 2.5 %shard_map.68 = (bf16[32,2048]{1,0:T(8,128)(2,1)S(1)}, bf16[32,2048]{1,0:T(8,128)(2,1)S(1)}, bf16[32,2048]{1,0:T(8,128)(2,1)S(1)}, bf16[32,2048]{1,0:T(8,128)(2,...) custom-call(f32[8,128]{1,0:T(8,128)S(1)} %get-tuple-element.52._, ...), custom_call_target="tpu_custom_call" | custom-call | bytes 1 | tf_op jit(solution)/shard_map/pallas_call | solution.py:251
  25.6 1.6 %collective-permute-start.11 = (bf16[32,2048]{1,0:T(8,128)(2,1)S(1)}, bf16[32,2048]{1,0:T(8,128)(2,1)S(1)}, u32[]{:S(2)}, u32[]{:S(2)}) collective-permute-start(bf16[32,2048]{1,0:T(8,128)(2,1)S(1)} %get-tuple-element.61), channel_id=1, source_target_pairs={{0,2},{2,0},{4,6},{6,4},{8,10},{10,8},{12,14},{14,12},{1,3},{3,1},... | collective-permute-start | bytes 393224 | tf_op jit(solution)/shard_map/ppermute | solution.py:320
  27.2 0.0 collective-permute-done.10.refs_1_
  27.2 2.3 %shard_map.69 = (bf16[32,2048]{1,0:T(8,128)(2,1)S(1)}, bf16[32,2048]{1,0:T(8,128)(2,1)S(1)}, f32[8,128]{1,0:T(8,128)S(1)}) custom-call(f32[8,128]{1,0:T(8,128)S(1)} %get-tuple-element.58._, f32[1,128]{1,0:T(1,128)S(1)} %get-tuple-element.53.select_ref, bf16[32,2176]{1,0:T(8,128)(2,1)S(1)} %collective-permute-done.6.refs_0_, ...), custom_call_target="tpu_custom_call" | custom-call | bytes 1 | tf_op jit(solution)/shard_map/pallas_call | solution.py:251
  29.5 0.8 %collective-permute-start.15 = (bf16[32,2048]{1,0:T(8,128)(2,1)S(1)}, bf16[32,2048]{1,0:T(8,128)(2,1)S(1)}, u32[]{:S(2)}, u32[]{:S(2)}) collective-permute-start(bf16[32,2048]{1,0:T(8,128)(2,1)S(1)} %get-tuple-element.72), channel_id=1, source_target_pairs={{0,2},{2,0},{4,6},{6,4},{8,10},{10,8},{12,14},{14,12},{1,3},{3,1},... | collective-permute-start | bytes 393224 | tf_op jit(solution)/shard_map/ppermute | solution.py:320
  30.4 0.3 collective-permute-done.11.refs_1_
  30.7 2.7 %collective-permute-start.12 = (bf16[32,2048]{1,0:T(8,128)(2,1)S(1)}, bf16[32,2048]{1,0:T(8,128)(2,1)S(1)}, u32[]{:S(2)}, u32[]{:S(2)}) collective-permute-start(bf16[32,2048]{1,0:T(8,128)(2,1)S(1)} %add_convert_fusion.2), channel_id=1, source_target_pairs={{0,12},{2,14},{4,8},{6,10},{8,4},{10,6},{12,0},{14,2},{1,13},{3,15... | collective-permute-start | bytes 393224 | tf_op jit(solution)/shard_map/ppermute | solution.py:323
  33.4 0.8 %collective-permute-start.13 = (bf16[32,2048]{1,0:T(8,128)(2,1)S(1)}, bf16[32,2048]{1,0:T(8,128)(2,1)S(1)}, u32[]{:S(2)}, u32[]{:S(2)}) collective-permute-start(bf16[32,2048]{1,0:T(8,128)(2,1)S(1)} %get-tuple-element.67), channel_id=1, source_target_pairs={{0,2},{2,0},{4,6},{6,4},{8,10},{10,8},{12,14},{14,12},{1,3},{3,1},... | collective-permute-start | bytes 393224 | tf_op jit(solution)/shard_map/ppermute | solution.py:320
  34.2 1.7 %collective-permute-done.15 = bf16[32,2048]{1,0:T(8,128)(2,1)S(1)} collective-permute-done((bf16[32,2048]{1,0:T(8,128)(2,1)S(1)}, bf16[32,2048]{1,0:T(8,128)(2,1)S(1)}, u32[]{:S(2)}, u32[]{:S(2)}) %collective-permute-start.15) | collective-permute-done | bytes 131104 | tf_op jit(solution)/shard_map/ppermute | solution.py:320
  35.9 2.9 %collective-permute-start.16 = (bf16[32,2048]{1,0:T(8,128)(2,1)S(1)}, bf16[32,2048]{1,0:T(8,128)(2,1)S(1)}, u32[]{:S(2)}, u32[]{:S(2)}) collective-permute-start(bf16[32,2048]{1,0:T(8,128)(2,1)S(1)} %add_convert_fusion.1), channel_id=1, source_target_pairs={{0,8},{2,10},{4,12},{6,14},{8,0},{10,2},{12,4},{14,6},{1,9},{3,11}... | collective-permute-start | bytes 393224 | tf_op jit(solution)/shard_map/ppermute | solution.py:323
  38.8 0.3 collective-permute-start.14
  39.1 0.0 collective-permute-done.12.refs_1_.refs_2_
  39.1 0.0 collective-permute-done.13
  39.2 2.4 %collective-permute-start.17 = (bf16[32,2048]{1,0:T(8,128)(2,1)S(1)}, bf16[32,2048]{1,0:T(8,128)(2,1)S(1)}, u32[]{:S(2)}, u32[]{:S(2)}) collective-permute-start(bf16[32,2048]{1,0:T(8,128)(2,1)S(1)} %add_convert_fusion), channel_id=1, source_target_pairs={{0,4},{2,6},{4,0},{6,2},{8,12},{10,14},{12,8},{14,10},{1,5},{3,7},... | collective-permute-start | bytes 393224 | tf_op jit(solution)/shard_map/ppermute | solution.py:323
  41.5 0.7 %collective-permute-done.16.refs_3_ = bf16[32,2048]{1,0:T(8,128)(2,1)S(1)} collective-permute-done((bf16[32,2048]{1,0:T(8,128)(2,1)S(1)}, bf16[32,2048]{1,0:T(8,128)(2,1)S(1)}, u32[]{:S(2)}, u32[]{:S(2)}) %collective-permute-start.16) | collective-permute-done | bytes 131104 | tf_op jit(solution)/shard_map/ppermute | solution.py:323
  42.3 1.5 %collective-permute-done.14.refs_1_ = bf16[32,2048]{1,0:T(8,128)(2,1)S(1)} collective-permute-done((bf16[32,2048]{1,0:T(8,128)(2,1)S(1)}, bf16[32,2048]{1,0:T(8,128)(2,1)S(1)}, u32[]{:S(2)}, u32[]{:S(2)}) %collective-permute-start.14) | collective-permute-done | bytes 131104 | tf_op jit(solution)/shard_map/ppermute | solution.py:320
  43.8 0.7 %collective-permute-done.17.refs_4_ = bf16[32,2048]{1,0:T(8,128)(2,1)S(1)} collective-permute-done((bf16[32,2048]{1,0:T(8,128)(2,1)S(1)}, bf16[32,2048]{1,0:T(8,128)(2,1)S(1)}, u32[]{:S(2)}, u32[]{:S(2)}) %collective-permute-start.17) | collective-permute-done | bytes 131104 | tf_op jit(solution)/shard_map/ppermute | solution.py:323
  44.5 0.1 shard_map.72
  44.6 0.1 collective-permute-start.18
  44.7 1.2 %collective-permute-done.18.rest_ref = bf16[32,1024]{1,0:T(8,128)(2,1)S(1)} collective-permute-done((bf16[32,1024]{1,0:T(8,128)(2,1)S(1)}, bf16[32,1024]{1,0:T(8,128)(2,1)S(1)}, u32[]{:S(2)}, u32[]{:S(2)}) %collective-permute-start.18) | collective-permute-done | bytes 65568 | tf_op jit(solution)/shard_map/ppermute | solution.py:383
  45.9 0.7 %shard_map.73 = bf16[64,1024]{1,0:T(8,128)(2,1)} custom-call(s32[1]{0:T(128)} %bitcast.head_ref, bf16[32,1024]{1,0:T(8,128)(2,1)S(1)} %get-tuple-element.75.keep_ref, bf16[32,1024]{1,0:T(8,128)(2,1)S(1)} %collective-permute-done.18.rest_ref), custom_call_target="tpu_custom_call" | custom-call | bytes 1 | tf_op jit(solution)/shard_map/pallas_call | solution.py:297
  (7 shorter events, 0.1 us)
Async XLA Ops:
  0.0 1.6 %collective-permute-start = (bf16[64,1024]{1,0:T(8,128)(2,1)}, bf16[64,1024]{1,0:T(8,128)(2,1)S(1)}, u32[]{:S(2)}, u32[]{:S(2)}) collective-permute-start(bf16[64,1024]{1,0:T(8,128)(2,1)} %tokens_hbm.1), channel_id=1, source_target_pairs={{0,1},{1,0},{2,3},{3,2},{4,5},{5,4},{6,7},{7,6},{8,9},{9,8},{10,11... | collective-permute-start | bytes 393224 | tf_op jit(solution)/shard_map/ppermute | solution.py:328
  1.7 11.2 %collective-permute-start.2 = (bf16[352,2048]{1,0:T(8,128)(2,1)}, bf16[352,2048]{1,0:T(8,128)(2,1)S(1)}, u32[]{:S(2)}, u32[]{:S(2)}) collective-permute-start(bf16[352,2048]{1,0:T(8,128)(2,1)} %bitcast.7), channel_id=1, source_target_pairs={{0,1},{1,0},{2,3},{3,2},{4,5},{5,4},{6,7},{7,6},{8,9},{9,8},{10,11... | collective-permute-start | bytes 4325384 | tf_op jit(solution)/shard_map/ppermute | solution.py:337
  2.0 12.3 %collective-permute-start.3 = (bf16[352,2048]{1,0:T(8,128)(2,1)}, bf16[352,2048]{1,0:T(8,128)(2,1)S(1)}, u32[]{:S(2)}, u32[]{:S(2)}) collective-permute-start(bf16[352,2048]{1,0:T(8,128)(2,1)} %bitcast.9), channel_id=1, source_target_pairs={{0,1},{1,0},{2,3},{3,2},{4,5},{5,4},{6,7},{7,6},{8,9},{9,8},{10,11... | collective-permute-start | bytes 4325384 | tf_op jit(solution)/shard_map/ppermute | solution.py:337
  2.2 14.7 %collective-permute-start.5 = (bf16[352,2048]{1,0:T(8,128)(2,1)}, bf16[352,2048]{1,0:T(8,128)(2,1)S(1)}, u32[]{:S(2)}, u32[]{:S(2)}) collective-permute-start(bf16[352,2048]{1,0:T(8,128)(2,1)} %bitcast.11), channel_id=1, source_target_pairs={{0,1},{1,0},{2,3},{3,2},{4,5},{5,4},{6,7},{7,6},{8,9},{9,8},{10,11... | collective-permute-start | bytes 4325384 | tf_op jit(solution)/shard_map/ppermute | solution.py:337
  2.5 7.0 %collective-permute-start.1 = (bf16[32,2176]{1,0:T(8,128)(2,1)S(1)}, bf16[32,2176]{1,0:T(8,128)(2,1)S(1)}, u32[]{:S(2)}, u32[]{:S(2)}) collective-permute-start(bf16[32,2176]{1,0:T(8,128)(2,1)S(1)} %shard_map.65.refs_0_), channel_id=1, source_target_pairs={{0,4},{2,6},{4,0},{6,2},{8,12},{10,14},{12,8},{14,10},{1,5},{3,7},... | collective-permute-start | bytes 417800 | tf_op jit(solution)/shard_map/ppermute | solution.py:323
  5.3 10.0 %collective-permute-start.4 = (bf16[32,2176]{1,0:T(8,128)(2,1)S(1)}, bf16[32,2176]{1,0:T(8,128)(2,1)S(1)}, u32[]{:S(2)}, u32[]{:S(2)}) collective-permute-start(bf16[32,2176]{1,0:T(8,128)(2,1)S(1)} %shard_map.65.refs_0_), channel_id=1, source_target_pairs={{0,12},{2,14},{4,8},{6,10},{8,4},{10,6},{12,0},{14,2},{1,13},{3,15... | collective-permute-start | bytes 417800 | tf_op jit(solution)/shard_map/ppermute | solution.py:323
  9.5 11.2 %collective-permute-start.6 = (bf16[32,2176]{1,0:T(8,128)(2,1)S(1)}, bf16[32,2176]{1,0:T(8,128)(2,1)S(1)}, u32[]{:S(2)}, u32[]{:S(2)}) collective-permute-start(bf16[32,2176]{1,0:T(8,128)(2,1)S(1)} %shard_map.65.refs_0_), channel_id=1, source_target_pairs={{0,8},{2,10},{4,12},{6,14},{8,0},{10,2},{12,4},{14,6},{1,9},{3,11}... | collective-permute-start | bytes 417800 | tf_op jit(solution)/shard_map/ppermute | solution.py:323
  12.8 9.4 %collective-permute-start.7 = (bf16[32,2176]{1,0:T(8,128)(2,1)S(1)}, bf16[32,2176]{1,0:T(8,128)(2,1)S(1)}, u32[]{:S(2)}, u32[]{:S(2)}) collective-permute-start(bf16[32,2176]{1,0:T(8,128)(2,1)S(1)} %shard_map.65.refs_0_), channel_id=1, source_target_pairs={{0,2},{2,0},{4,6},{6,4},{8,10},{10,8},{12,14},{14,12},{1,3},{3,1},... | collective-permute-start | bytes 417800 | tf_op jit(solution)/shard_map/ppermute | solution.py:320
  14.3 7.9 %collective-permute-start.8 = (bf16[32,2176]{1,0:T(8,128)(2,1)S(1)}, bf16[32,2176]{1,0:T(8,128)(2,1)S(1)}, u32[]{:S(2)}, u32[]{:S(2)}) collective-permute-start(bf16[32,2176]{1,0:T(8,128)(2,1)S(1)} %collective-permute-done.1.refs_0_.refs_1_), channel_id=1, source_target_pairs={{0,2},{2,0},{4,6},{6,4},{8,10},{10,8},{12,14},{14,12},{1,3},{3,1},... | collective-permute-start | bytes 417800 | tf_op jit(solution)/shard_map/ppermute | solution.py:320
  15.4 7.7 %collective-permute-start.9 = (bf16[32,2176]{1,0:T(8,128)(2,1)S(1)}, bf16[32,2176]{1,0:T(8,128)(2,1)S(1)}, u32[]{:S(2)}, u32[]{:S(2)}) collective-permute-start(bf16[32,2176]{1,0:T(8,128)(2,1)S(1)} %collective-permute-done.4.refs_2_), channel_id=1, source_target_pairs={{0,2},{2,0},{4,6},{6,4},{8,10},{10,8},{12,14},{14,12},{1,3},{3,1},... | collective-permute-start | bytes 417800 | tf_op jit(solution)/shard_map/ppermute | solution.py:320
  20.7 6.5 %collective-permute-start.10 = (bf16[32,2176]{1,0:T(8,128)(2,1)S(1)}, bf16[32,2176]{1,0:T(8,128)(2,1)S(1)}, u32[]{:S(2)}, u32[]{:S(2)}) collective-permute-start(bf16[32,2176]{1,0:T(8,128)(2,1)S(1)} %collective-permute-done.6.refs_0_), channel_id=1, source_target_pairs={{0,2},{2,0},{4,6},{6,4},{8,10},{10,8},{12,14},{14,12},{1,3},{3,1},... | collective-permute-start | bytes 417800 | tf_op jit(solution)/shard_map/ppermute | solution.py:320
  25.6 5.0 %collective-permute-start.11 = (bf16[32,2048]{1,0:T(8,128)(2,1)S(1)}, bf16[32,2048]{1,0:T(8,128)(2,1)S(1)}, u32[]{:S(2)}, u32[]{:S(2)}) collective-permute-start(bf16[32,2048]{1,0:T(8,128)(2,1)S(1)} %get-tuple-element.61), channel_id=1, source_target_pairs={{0,2},{2,0},{4,6},{6,4},{8,10},{10,8},{12,14},{14,12},{1,3},{3,1},... | collective-permute-start | bytes 393224 | tf_op jit(solution)/shard_map/ppermute | solution.py:320
  29.5 6.3 %collective-permute-start.15 = (bf16[32,2048]{1,0:T(8,128)(2,1)S(1)}, bf16[32,2048]{1,0:T(8,128)(2,1)S(1)}, u32[]{:S(2)}, u32[]{:S(2)}) collective-permute-start(bf16[32,2048]{1,0:T(8,128)(2,1)S(1)} %get-tuple-element.72), channel_id=1, source_target_pairs={{0,2},{2,0},{4,6},{6,4},{8,10},{10,8},{12,14},{14,12},{1,3},{3,1},... | collective-permute-start | bytes 393224 | tf_op jit(solution)/shard_map/ppermute | solution.py:320
  30.7 8.4 %collective-permute-start.12 = (bf16[32,2048]{1,0:T(8,128)(2,1)S(1)}, bf16[32,2048]{1,0:T(8,128)(2,1)S(1)}, u32[]{:S(2)}, u32[]{:S(2)}) collective-permute-start(bf16[32,2048]{1,0:T(8,128)(2,1)S(1)} %add_convert_fusion.2), channel_id=1, source_target_pairs={{0,12},{2,14},{4,8},{6,10},{8,4},{10,6},{12,0},{14,2},{1,13},{3,15... | collective-permute-start | bytes 393224 | tf_op jit(solution)/shard_map/ppermute | solution.py:323
  33.4 5.7 %collective-permute-start.13 = (bf16[32,2048]{1,0:T(8,128)(2,1)S(1)}, bf16[32,2048]{1,0:T(8,128)(2,1)S(1)}, u32[]{:S(2)}, u32[]{:S(2)}) collective-permute-start(bf16[32,2048]{1,0:T(8,128)(2,1)S(1)} %get-tuple-element.67), channel_id=1, source_target_pairs={{0,2},{2,0},{4,6},{6,4},{8,10},{10,8},{12,14},{14,12},{1,3},{3,1},... | collective-permute-start | bytes 393224 | tf_op jit(solution)/shard_map/ppermute | solution.py:320
  35.9 6.3 %collective-permute-start.16 = (bf16[32,2048]{1,0:T(8,128)(2,1)S(1)}, bf16[32,2048]{1,0:T(8,128)(2,1)S(1)}, u32[]{:S(2)}, u32[]{:S(2)}) collective-permute-start(bf16[32,2048]{1,0:T(8,128)(2,1)S(1)} %add_convert_fusion.1), channel_id=1, source_target_pairs={{0,8},{2,10},{4,12},{6,14},{8,0},{10,2},{12,4},{14,6},{1,9},{3,11}... | collective-permute-start | bytes 393224 | tf_op jit(solution)/shard_map/ppermute | solution.py:323
  38.8 5.0 %collective-permute-start.14 = (bf16[32,2048]{1,0:T(8,128)(2,1)S(1)}, bf16[32,2048]{1,0:T(8,128)(2,1)S(1)}, u32[]{:S(2)}, u32[]{:S(2)}) collective-permute-start(bf16[32,2048]{1,0:T(8,128)(2,1)S(1)} %get-tuple-element.70), channel_id=1, source_target_pairs={{0,2},{2,0},{4,6},{6,4},{8,10},{10,8},{12,14},{14,12},{1,3},{3,1},... | collective-permute-start | bytes 393224 | tf_op jit(solution)/shard_map/ppermute | solution.py:320
  39.2 5.3 %collective-permute-start.17 = (bf16[32,2048]{1,0:T(8,128)(2,1)S(1)}, bf16[32,2048]{1,0:T(8,128)(2,1)S(1)}, u32[]{:S(2)}, u32[]{:S(2)}) collective-permute-start(bf16[32,2048]{1,0:T(8,128)(2,1)S(1)} %add_convert_fusion), channel_id=1, source_target_pairs={{0,4},{2,6},{4,0},{6,2},{8,12},{10,14},{12,8},{14,10},{1,5},{3,7},... | collective-permute-start | bytes 393224 | tf_op jit(solution)/shard_map/ppermute | solution.py:323
  44.6 1.3 %collective-permute-start.18 = (bf16[32,1024]{1,0:T(8,128)(2,1)S(1)}, bf16[32,1024]{1,0:T(8,128)(2,1)S(1)}, u32[]{:S(2)}, u32[]{:S(2)}) collective-permute-start(bf16[32,1024]{1,0:T(8,128)(2,1)S(1)} %get-tuple-element.76), channel_id=1, source_target_pairs={{0,1},{1,0},{2,3},{3,2},{4,5},{5,4},{6,7},{7,6},{8,9},{9,8},{10,11... | collective-permute-start | bytes 196616 | tf_op jit(solution)/shard_map/ppermute | solution.py:383

commit v8 on v7

--- a/solution.py
+++ b/solution.py
@@ -351,7 +351,7 @@
     over[last] = pair(block[last])
 
     here, there = {}, {}
-    keys = [0] + [1] + mid
+    keys = [0] + mid
     groups = [[v[k]] for v in (block, over) for k in keys]
     done, mark = run_expert(mark, groups, select, weights)
     here.update(zip(keys, done))
@@ -359,7 +359,7 @@
         there[k] = done[len(keys) + j]
         if k >= 2:
             there[k] = pair(there[k])
-    keys = [last]
+    keys = [last] + [1]
     groups = [[v[k]] for v in (block, over) for k in keys]
     done, mark = run_expert(mark, groups, select, weights)
     here.update(zip(keys, done))

time: 46.7 us -> 48.3 us (1.034)
  starting transfers between devices: 26.4 us -> 27.5 us
  waiting for transfers between devices: 11 us -> 11.6 us
    ppermute x6, waiting for transfers between devices: 5.09 us -> 7.22 us  [column(): return lax.ppermute(v, 'wide', [(w, w ^ 2 * k) for w in range(n)])]
    ppermute x8, starting transfers between devices: 8.45 us -> 10.2 us  [pair(): return lax.ppermute(v, 'wide', [(w, w ^ 1) for w in range(n)])]
    ppermute x8, waiting for transfers between devices: 4.38 us -> 2.82 us  [pair(): return lax.ppermute(v, 'wide', [(w, w ^ 1) for w in range(n)])]
    ppermute x6, starting transfers between devices: 16.6 us -> 15.9 us  [column(): return lax.ppermute(v, 'wide', [(w, w ^ 2 * k) for w in range(n)])]
  transfers between devices with their start and end apart: 19 -> 19, of which waited for: 11 -> 9; matrix products, arithmetic and copies ran while one was open for 0% -> 0% of each run, Pallas kernels for 18% -> 17%
where the time goes in v8:
time: 48.3 us; the launch traced here: 48.1 us
  starting transfers between devices  27.5 us (57%)
  waiting for transfers between devices  11.6 us (24%)
  Pallas kernels  8.87 us (18%)
    ppermute x6, starting transfers between devices, column(): return lax.ppermute(v, 'wide', [(w, w ^ 2 * k) for w in range(n)])  15.9 us
    ppermute x8, starting transfers between devices, pair(): return lax.ppermute(v, 'wide', [(w, w ^ 1) for w in range(n)])  10.2 us
    ppermute x6, waiting for transfers between devices, column(): return lax.ppermute(v, 'wide', [(w, w ^ 2 * k) for w in range(n)])  7.22 us
    pallas_call x2, Pallas kernels, run_expert(): pl.pallas_call(functools.partial(expert_kernel, len(blocks)), out_shape=[...  4.8 us
    ppermute x8, waiting for transfers between devices, pair(): return lax.ppermute(v, 'wide', [(w, w ^ 1) for w in range(n)])  2.82 us
    pallas_call x1, Pallas kernels, gather_weights(): pl.pallas_call(functools.partial(gather_kernel, count), out_shape=[jax.Sh...  2.39 us
    ppermute x1, waiting for transfers between devices, dense_local(): rest = lax.ppermute(send, 'head', swap)  1.24 us
  transfers between devices with their start and end apart: 19, of which 9 were waited for; matrix products, arithmetic and copies ran while one was open for 0% of the time, Pallas kernels for 17%

profile of v8, /device:TPU:0, one launch (start us, length us, event | category | flops | bytes accessed | tf_op | source)
XLA Modules:
  0.0 48.1 jit_solution(16873047171059323893)
XLA Ops:
  0.0 0.5 collective-permute-start
  0.5 0.9 %shard_map.64 = (bf16[32,1024]{1,0:T(8,128)(2,1)S(1)}, bf16[32,128]{1,0:T(8,128)(2,1)S(1)}, f32[1,128]{1,0:T(1,128)S(1)}) custom-call(s32[1]{0:T(128)} %bitcast.head_ref, s32[1]{0:T(128)} %bitcast.1.expert_ref, bf16[64,1024]{1,0:T(8,128)(2,1)} %tokens_hbm.1, s32[8,64]{1,0:T(8,128)} %bitcast.13, f32[8,64]{1,0:T(8,128)} %bitcast.14), custom_call_target="tpu_custom_call" | custom-call | bytes 1 | tf_op jit(solution)/shard_map/pallas_call | solution.py:129
  1.4 0.3 collective-permute-done.got_ref
  1.7 0.4 collective-permute-start.2
  2.0 0.1 collective-permute-start.3
  2.2 0.4 collective-permute-start.5
  2.5 2.8 %collective-permute-start.1 = (bf16[32,2176]{1,0:T(8,128)(2,1)S(1)}, bf16[32,2176]{1,0:T(8,128)(2,1)S(1)}, u32[]{:S(2)}, u32[]{:S(2)}) collective-permute-start(bf16[32,2176]{1,0:T(8,128)(2,1)S(1)} %shard_map.65.refs_0_), channel_id=1, source_target_pairs={{0,4},{2,6},{4,0},{6,2},{8,12},{10,14},{12,8},{14,10},{1,5},{3,7},... | collective-permute-start | bytes 417800 | tf_op jit(solution)/shard_map/ppermute | solution.py:323
  5.3 2.5 %collective-permute-start.4 = (bf16[32,2176]{1,0:T(8,128)(2,1)S(1)}, bf16[32,2176]{1,0:T(8,128)(2,1)S(1)}, u32[]{:S(2)}, u32[]{:S(2)}) collective-permute-start(bf16[32,2176]{1,0:T(8,128)(2,1)S(1)} %shard_map.65.refs_0_), channel_id=1, source_target_pairs={{0,12},{2,14},{4,8},{6,10},{8,4},{10,6},{12,0},{14,2},{1,13},{3,15... | collective-permute-start | bytes 417800 | tf_op jit(solution)/shard_map/ppermute | solution.py:323
  7.8 1.7 %collective-permute-done.1.refs_0_.refs_1_ = bf16[32,2176]{1,0:T(8,128)(2,1)S(1)} collective-permute-done((bf16[32,2176]{1,0:T(8,128)(2,1)S(1)}, bf16[32,2176]{1,0:T(8,128)(2,1)S(1)}, u32[]{:S(2)}, u32[]{:S(2)}) %collective-permute-start.1) | collective-permute-done | bytes 139296 | tf_op jit(solution)/shard_map/ppermute | solution.py:323
  9.5 3.3 %collective-permute-start.6 = (bf16[32,2176]{1,0:T(8,128)(2,1)S(1)}, bf16[32,2176]{1,0:T(8,128)(2,1)S(1)}, u32[]{:S(2)}, u32[]{:S(2)}) collective-permute-start(bf16[32,2176]{1,0:T(8,128)(2,1)S(1)} %shard_map.65.refs_0_), channel_id=1, source_target_pairs={{0,8},{2,10},{4,12},{6,14},{8,0},{10,2},{12,4},{14,6},{1,9},{3,11}... | collective-permute-start | bytes 417800 | tf_op jit(solution)/shard_map/ppermute | solution.py:323
  12.8 0.0 collective-permute-done.2.refs_1_.refs_3_
  12.8 1.5 %collective-permute-start.7 = (bf16[32,2176]{1,0:T(8,128)(2,1)S(1)}, bf16[32,2176]{1,0:T(8,128)(2,1)S(1)}, u32[]{:S(2)}, u32[]{:S(2)}) collective-permute-start(bf16[32,2176]{1,0:T(8,128)(2,1)S(1)} %shard_map.65.refs_0_), channel_id=1, source_target_pairs={{0,2},{2,0},{4,6},{6,4},{8,10},{10,8},{12,14},{14,12},{1,3},{3,1},... | collective-permute-start | bytes 417800 | tf_op jit(solution)/shard_map/ppermute | solution.py:320
  14.3 0.0 collective-permute-done.3.refs_2_.refs_4_
  14.3 1.0 %collective-permute-done.4.refs_1_ = bf16[32,2176]{1,0:T(8,128)(2,1)S(1)} collective-permute-done((bf16[32,2176]{1,0:T(8,128)(2,1)S(1)}, bf16[32,2176]{1,0:T(8,128)(2,1)S(1)}, u32[]{:S(2)}, u32[]{:S(2)}) %collective-permute-start.4) | collective-permute-done | bytes 139296 | tf_op jit(solution)/shard_map/ppermute | solution.py:323
  15.4 1.5 %collective-permute-start.8 = (bf16[32,2176]{1,0:T(8,128)(2,1)S(1)}, bf16[32,2176]{1,0:T(8,128)(2,1)S(1)}, u32[]{:S(2)}, u32[]{:S(2)}) collective-permute-start(bf16[32,2176]{1,0:T(8,128)(2,1)S(1)} %collective-permute-done.4.refs_1_), channel_id=1, source_target_pairs={{0,2},{2,0},{4,6},{6,4},{8,10},{10,8},{12,14},{14,12},{1,3},{3,1},... | collective-permute-start | bytes 417800 | tf_op jit(solution)/shard_map/ppermute | solution.py:320
  16.9 0.5 %collective-permute-start.10 = (bf16[32,2176]{1,0:T(8,128)(2,1)S(1)}, bf16[32,2176]{1,0:T(8,128)(2,1)S(1)}, u32[]{:S(2)}, u32[]{:S(2)}) collective-permute-start(bf16[32,2176]{1,0:T(8,128)(2,1)S(1)} %collective-permute-done.1.refs_0_.refs_1_), channel_id=1, source_target_pairs={{0,2},{2,0},{4,6},{6,4},{8,10},{10,8},{12,14},{14,12},{1,3},{3,1},... | collective-permute-start | bytes 417800 | tf_op jit(solution)/shard_map/ppermute | solution.py:320
  17.4 0.0 collective-permute-done.5.refs_5_
  17.4 2.4 %shard_map.67 = (bf16[704,2048]{1,0:T(8,128)(2,1)S(1)}, bf16[704,2048]{1,0:T(8,128)(2,1)S(1)}, bf16[704,2048]{1,0:T(8,128)(2,1)S(1)}, f32[8,128]{1,0:T(8,128)S(1)}) custom-call(f32[8,128]{1,0:T(8,128)S(1)} %shard_map.66._, bf16[352,2048]{1,0:T(8,128)(2,1)} %bitcast.8, bf16[352,2048]{1,0:T(8,128)(2,1)} %bitcast.10, bf16[352,2048]{1,0:T(8,128)(2,1)} %bitcast.12, ...), custom_call_target="tpu_custom_call" | custom-call | bytes 1 | tf_op jit(solution)/shard_map/pallas_call | solution.py:194
  19.8 0.9 %collective-permute-done.6.refs_0_ = bf16[32,2176]{1,0:T(8,128)(2,1)S(1)} collective-permute-done((bf16[32,2176]{1,0:T(8,128)(2,1)S(1)}, bf16[32,2176]{1,0:T(8,128)(2,1)S(1)}, u32[]{:S(2)}, u32[]{:S(2)}) %collective-permute-start.6) | collective-permute-done | bytes 139296 | tf_op jit(solution)/shard_map/ppermute | solution.py:323
  20.7 1.5 %collective-permute-start.9 = (bf16[32,2176]{1,0:T(8,128)(2,1)S(1)}, bf16[32,2176]{1,0:T(8,128)(2,1)S(1)}, u32[]{:S(2)}, u32[]{:S(2)}) collective-permute-start(bf16[32,2176]{1,0:T(8,128)(2,1)S(1)} %collective-permute-done.6.refs_0_), channel_id=1, source_target_pairs={{0,2},{2,0},{4,6},{6,4},{8,10},{10,8},{12,14},{14,12},{1,3},{3,1},... | collective-permute-start | bytes 417800 | tf_op jit(solution)/shard_map/ppermute | solution.py:320
  22.2 0.0 collective-permute-done.7.refs_2_
  22.2 0.0 collective-permute-done.8.refs_3_
  22.2 2.4 %shard_map.68 = (bf16[32,2048]{1,0:T(8,128)(2,1)S(1)}, bf16[32,2048]{1,0:T(8,128)(2,1)S(1)}, bf16[32,2048]{1,0:T(8,128)(2,1)S(1)}, bf16[32,2048]{1,0:T(8,128)(2,1)S(1)}, f32[8,128]{1,0:T(8,128)S(1)}) custom-call(f32[8,128]{1,0:T(8,128)S(1)} %get-tuple-element.52._, f32[1,128]{1,0:T(1,128)S(1)} %get-tuple-element.53.select_ref, ...), custom_call_target="tpu_custom_call" | custom-call | bytes 1 | tf_op jit(solution)/shard_map/pallas_call | solution.py:251
  24.6 1.3 %collective-permute-start.11 = (bf16[32,2048]{1,0:T(8,128)(2,1)S(1)}, bf16[32,2048]{1,0:T(8,128)(2,1)S(1)}, u32[]{:S(2)}, u32[]{:S(2)}) collective-permute-start(bf16[32,2048]{1,0:T(8,128)(2,1)S(1)} %get-tuple-element.61), channel_id=1, source_target_pairs={{0,2},{2,0},{4,6},{6,4},{8,10},{10,8},{12,14},{14,12},{1,3},{3,1},... | collective-permute-start | bytes 393224 | tf_op jit(solution)/shard_map/ppermute | solution.py:320
  25.9 0.0 collective-permute-done.10.refs_3_
  25.9 0.9 %collective-permute-done.9.refs_2_ = bf16[32,2176]{1,0:T(8,128)(2,1)S(1)} collective-permute-done((bf16[32,2176]{1,0:T(8,128)(2,1)S(1)}, bf16[32,2176]{1,0:T(8,128)(2,1)S(1)}, u32[]{:S(2)}, u32[]{:S(2)}) %collective-permute-start.9) | collective-permute-done | bytes 139296 | tf_op jit(solution)/shard_map/ppermute | solution.py:320
  26.9 2.4 %shard_map.69 = (bf16[32,2048]{1,0:T(8,128)(2,1)S(1)}, bf16[32,2048]{1,0:T(8,128)(2,1)S(1)}, bf16[32,2048]{1,0:T(8,128)(2,1)S(1)}, bf16[32,2048]{1,0:T(8,128)(2,1)S(1)}, f32[8,128]{1,0:T(8,128)S(1)}) custom-call(f32[8,128]{1,0:T(8,128)S(1)} %get-tuple-element.58._, f32[1,128]{1,0:T(1,128)S(1)} %get-tuple-element.53.select_ref, ...), custom_call_target="tpu_custom_call" | custom-call | bytes 1 | tf_op jit(solution)/shard_map/pallas_call | solution.py:251
  29.3 2.0 %collective-permute-start.15 = (bf16[32,2048]{1,0:T(8,128)(2,1)S(1)}, bf16[32,2048]{1,0:T(8,128)(2,1)S(1)}, u32[]{:S(2)}, u32[]{:S(2)}) collective-permute-start(bf16[32,2048]{1,0:T(8,128)(2,1)S(1)} %get-tuple-element.72), channel_id=1, source_target_pairs={{0,2},{2,0},{4,6},{6,4},{8,10},{10,8},{12,14},{14,12},{1,3},{3,1},... | collective-permute-start | bytes 393224 | tf_op jit(solution)/shard_map/ppermute | solution.py:320
  31.2 0.0 collective-permute-done.11.refs_1_
  31.3 2.2 %collective-permute-start.12 = (bf16[32,2048]{1,0:T(8,128)(2,1)S(1)}, bf16[32,2048]{1,0:T(8,128)(2,1)S(1)}, u32[]{:S(2)}, u32[]{:S(2)}) collective-permute-start(bf16[32,2048]{1,0:T(8,128)(2,1)S(1)} %add_convert_fusion.2), channel_id=1, source_target_pairs={{0,12},{2,14},{4,8},{6,10},{8,4},{10,6},{12,0},{14,2},{1,13},{3,15... | collective-permute-start | bytes 393224 | tf_op jit(solution)/shard_map/ppermute | solution.py:323
  33.5 0.0 collective-permute-start.13
  33.5 1.9 %collective-permute-done.15 = bf16[32,2048]{1,0:T(8,128)(2,1)S(1)} collective-permute-done((bf16[32,2048]{1,0:T(8,128)(2,1)S(1)}, bf16[32,2048]{1,0:T(8,128)(2,1)S(1)}, u32[]{:S(2)}, u32[]{:S(2)}) %collective-permute-start.15) | collective-permute-done | bytes 131104 | tf_op jit(solution)/shard_map/ppermute | solution.py:320
  35.4 3.3 %collective-permute-start.16 = (bf16[32,2048]{1,0:T(8,128)(2,1)S(1)}, bf16[32,2048]{1,0:T(8,128)(2,1)S(1)}, u32[]{:S(2)}, u32[]{:S(2)}) collective-permute-start(bf16[32,2048]{1,0:T(8,128)(2,1)S(1)} %add_convert_fusion.1), channel_id=1, source_target_pairs={{0,8},{2,10},{4,12},{6,14},{8,0},{10,2},{12,4},{14,6},{1,9},{3,11}... | collective-permute-start | bytes 393224 | tf_op jit(solution)/shard_map/ppermute | solution.py:323
  38.7 1.9 %collective-permute-start.14 = (bf16[32,2048]{1,0:T(8,128)(2,1)S(1)}, bf16[32,2048]{1,0:T(8,128)(2,1)S(1)}, u32[]{:S(2)}, u32[]{:S(2)}) collective-permute-start(bf16[32,2048]{1,0:T(8,128)(2,1)S(1)} %get-tuple-element.70), channel_id=1, source_target_pairs={{0,2},{2,0},{4,6},{6,4},{8,10},{10,8},{12,14},{14,12},{1,3},{3,1},... | collective-permute-start | bytes 393224 | tf_op jit(solution)/shard_map/ppermute | solution.py:320
  40.6 0.0 collective-permute-done.12.refs_1_.refs_2_
  40.6 0.0 collective-permute-done.13
  40.7 1.8 %collective-permute-start.17 = (bf16[32,2048]{1,0:T(8,128)(2,1)S(1)}, bf16[32,2048]{1,0:T(8,128)(2,1)S(1)}, u32[]{:S(2)}, u32[]{:S(2)}) collective-permute-start(bf16[32,2048]{1,0:T(8,128)(2,1)S(1)} %add_convert_fusion), channel_id=1, source_target_pairs={{0,4},{2,6},{4,0},{6,2},{8,12},{10,14},{12,8},{14,10},{1,5},{3,7},... | collective-permute-start | bytes 393224 | tf_op jit(solution)/shard_map/ppermute | solution.py:323
  42.5 2.2 %collective-permute-done.16.refs_3_ = bf16[32,2048]{1,0:T(8,128)(2,1)S(1)} collective-permute-done((bf16[32,2048]{1,0:T(8,128)(2,1)S(1)}, bf16[32,2048]{1,0:T(8,128)(2,1)S(1)}, u32[]{:S(2)}, u32[]{:S(2)}) %collective-permute-start.16) | collective-permute-done | bytes 131104 | tf_op jit(solution)/shard_map/ppermute | solution.py:323
  44.6 0.0 collective-permute-done.14.refs_1_
  44.6 1.4 %collective-permute-done.17.refs_4_ = bf16[32,2048]{1,0:T(8,128)(2,1)S(1)} collective-permute-done((bf16[32,2048]{1,0:T(8,128)(2,1)S(1)}, bf16[32,2048]{1,0:T(8,128)(2,1)S(1)}, u32[]{:S(2)}, u32[]{:S(2)}) %collective-permute-start.17) | collective-permute-done | bytes 131104 | tf_op jit(solution)/shard_map/ppermute | solution.py:323
  46.0 0.1 shard_map.72
  46.1 0.1 collective-permute-start.18
  46.2 1.2 %collective-permute-done.18.rest_ref = bf16[32,1024]{1,0:T(8,128)(2,1)S(1)} collective-permute-done((bf16[32,1024]{1,0:T(8,128)(2,1)S(1)}, bf16[32,1024]{1,0:T(8,128)(2,1)S(1)}, u32[]{:S(2)}, u32[]{:S(2)}) %collective-permute-start.18) | collective-permute-done | bytes 65568 | tf_op jit(solution)/shard_map/ppermute | solution.py:383
  47.4 0.7 %shard_map.73 = bf16[64,1024]{1,0:T(8,128)(2,1)} custom-call(s32[1]{0:T(128)} %bitcast.head_ref, bf16[32,1024]{1,0:T(8,128)(2,1)S(1)} %get-tuple-element.75.keep_ref, bf16[32,1024]{1,0:T(8,128)(2,1)S(1)} %collective-permute-done.18.rest_ref), custom_call_target="tpu_custom_call" | custom-call | bytes 1 | tf_op jit(solution)/shard_map/pallas_call | solution.py:297
  (7 shorter events, 0.1 us)
Async XLA Ops:
  0.0 1.6 %collective-permute-start = (bf16[64,1024]{1,0:T(8,128)(2,1)}, bf16[64,1024]{1,0:T(8,128)(2,1)S(1)}, u32[]{:S(2)}, u32[]{:S(2)}) collective-permute-start(bf16[64,1024]{1,0:T(8,128)(2,1)} %tokens_hbm.1), channel_id=1, source_target_pairs={{0,1},{1,0},{2,3},{3,2},{4,5},{5,4},{6,7},{7,6},{8,9},{9,8},{10,11... | collective-permute-start | bytes 393224 | tf_op jit(solution)/shard_map/ppermute | solution.py:328
  1.7 11.2 %collective-permute-start.2 = (bf16[352,2048]{1,0:T(8,128)(2,1)}, bf16[352,2048]{1,0:T(8,128)(2,1)S(1)}, u32[]{:S(2)}, u32[]{:S(2)}) collective-permute-start(bf16[352,2048]{1,0:T(8,128)(2,1)} %bitcast.7), channel_id=1, source_target_pairs={{0,1},{1,0},{2,3},{3,2},{4,5},{5,4},{6,7},{7,6},{8,9},{9,8},{10,11... | collective-permute-start | bytes 4325384 | tf_op jit(solution)/shard_map/ppermute | solution.py:337
  2.0 12.3 %collective-permute-start.3 = (bf16[352,2048]{1,0:T(8,128)(2,1)}, bf16[352,2048]{1,0:T(8,128)(2,1)S(1)}, u32[]{:S(2)}, u32[]{:S(2)}) collective-permute-start(bf16[352,2048]{1,0:T(8,128)(2,1)} %bitcast.9), channel_id=1, source_target_pairs={{0,1},{1,0},{2,3},{3,2},{4,5},{5,4},{6,7},{7,6},{8,9},{9,8},{10,11... | collective-permute-start | bytes 4325384 | tf_op jit(solution)/shard_map/ppermute | solution.py:337
  2.2 15.2 %collective-permute-start.5 = (bf16[352,2048]{1,0:T(8,128)(2,1)}, bf16[352,2048]{1,0:T(8,128)(2,1)S(1)}, u32[]{:S(2)}, u32[]{:S(2)}) collective-permute-start(bf16[352,2048]{1,0:T(8,128)(2,1)} %bitcast.11), channel_id=1, source_target_pairs={{0,1},{1,0},{2,3},{3,2},{4,5},{5,4},{6,7},{7,6},{8,9},{9,8},{10,11... | collective-permute-start | bytes 4325384 | tf_op jit(solution)/shard_map/ppermute | solution.py:337
  2.5 7.0 %collective-permute-start.1 = (bf16[32,2176]{1,0:T(8,128)(2,1)S(1)}, bf16[32,2176]{1,0:T(8,128)(2,1)S(1)}, u32[]{:S(2)}, u32[]{:S(2)}) collective-permute-start(bf16[32,2176]{1,0:T(8,128)(2,1)S(1)} %shard_map.65.refs_0_), channel_id=1, source_target_pairs={{0,4},{2,6},{4,0},{6,2},{8,12},{10,14},{12,8},{14,10},{1,5},{3,7},... | collective-permute-start | bytes 417800 | tf_op jit(solution)/shard_map/ppermute | solution.py:323
  5.3 10.0 %collective-permute-start.4 = (bf16[32,2176]{1,0:T(8,128)(2,1)S(1)}, bf16[32,2176]{1,0:T(8,128)(2,1)S(1)}, u32[]{:S(2)}, u32[]{:S(2)}) collective-permute-start(bf16[32,2176]{1,0:T(8,128)(2,1)S(1)} %shard_map.65.refs_0_), channel_id=1, source_target_pairs={{0,12},{2,14},{4,8},{6,10},{8,4},{10,6},{12,0},{14,2},{1,13},{3,15... | collective-permute-start | bytes 417800 | tf_op jit(solution)/shard_map/ppermute | solution.py:323
  9.5 11.2 %collective-permute-start.6 = (bf16[32,2176]{1,0:T(8,128)(2,1)S(1)}, bf16[32,2176]{1,0:T(8,128)(2,1)S(1)}, u32[]{:S(2)}, u32[]{:S(2)}) collective-permute-start(bf16[32,2176]{1,0:T(8,128)(2,1)S(1)} %shard_map.65.refs_0_), channel_id=1, source_target_pairs={{0,8},{2,10},{4,12},{6,14},{8,0},{10,2},{12,4},{14,6},{1,9},{3,11}... | collective-permute-start | bytes 417800 | tf_op jit(solution)/shard_map/ppermute | solution.py:323
  12.8 9.4 %collective-permute-start.7 = (bf16[32,2176]{1,0:T(8,128)(2,1)S(1)}, bf16[32,2176]{1,0:T(8,128)(2,1)S(1)}, u32[]{:S(2)}, u32[]{:S(2)}) collective-permute-start(bf16[32,2176]{1,0:T(8,128)(2,1)S(1)} %shard_map.65.refs_0_), channel_id=1, source_target_pairs={{0,2},{2,0},{4,6},{6,4},{8,10},{10,8},{12,14},{14,12},{1,3},{3,1},... | collective-permute-start | bytes 417800 | tf_op jit(solution)/shard_map/ppermute | solution.py:320
  15.4 6.9 %collective-permute-start.8 = (bf16[32,2176]{1,0:T(8,128)(2,1)S(1)}, bf16[32,2176]{1,0:T(8,128)(2,1)S(1)}, u32[]{:S(2)}, u32[]{:S(2)}) collective-permute-start(bf16[32,2176]{1,0:T(8,128)(2,1)S(1)} %collective-permute-done.4.refs_1_), channel_id=1, source_target_pairs={{0,2},{2,0},{4,6},{6,4},{8,10},{10,8},{12,14},{14,12},{1,3},{3,1},... | collective-permute-start | bytes 417800 | tf_op jit(solution)/shard_map/ppermute | solution.py:320
  16.9 9.1 %collective-permute-start.10 = (bf16[32,2176]{1,0:T(8,128)(2,1)S(1)}, bf16[32,2176]{1,0:T(8,128)(2,1)S(1)}, u32[]{:S(2)}, u32[]{:S(2)}) collective-permute-start(bf16[32,2176]{1,0:T(8,128)(2,1)S(1)} %collective-permute-done.1.refs_0_.refs_1_), channel_id=1, source_target_pairs={{0,2},{2,0},{4,6},{6,4},{8,10},{10,8},{12,14},{14,12},{1,3},{3,1},... | collective-permute-start | bytes 417800 | tf_op jit(solution)/shard_map/ppermute | solution.py:320
  20.7 6.1 %collective-permute-start.9 = (bf16[32,2176]{1,0:T(8,128)(2,1)S(1)}, bf16[32,2176]{1,0:T(8,128)(2,1)S(1)}, u32[]{:S(2)}, u32[]{:S(2)}) collective-permute-start(bf16[32,2176]{1,0:T(8,128)(2,1)S(1)} %collective-permute-done.6.refs_0_), channel_id=1, source_target_pairs={{0,2},{2,0},{4,6},{6,4},{8,10},{10,8},{12,14},{14,12},{1,3},{3,1},... | collective-permute-start | bytes 417800 | tf_op jit(solution)/shard_map/ppermute | solution.py:320
  24.6 6.6 %collective-permute-start.11 = (bf16[32,2048]{1,0:T(8,128)(2,1)S(1)}, bf16[32,2048]{1,0:T(8,128)(2,1)S(1)}, u32[]{:S(2)}, u32[]{:S(2)}) collective-permute-start(bf16[32,2048]{1,0:T(8,128)(2,1)S(1)} %get-tuple-element.61), channel_id=1, source_target_pairs={{0,2},{2,0},{4,6},{6,4},{8,10},{10,8},{12,14},{14,12},{1,3},{3,1},... | collective-permute-start | bytes 393224 | tf_op jit(solution)/shard_map/ppermute | solution.py:320
  29.3 6.1 %collective-permute-start.15 = (bf16[32,2048]{1,0:T(8,128)(2,1)S(1)}, bf16[32,2048]{1,0:T(8,128)(2,1)S(1)}, u32[]{:S(2)}, u32[]{:S(2)}) collective-permute-start(bf16[32,2048]{1,0:T(8,128)(2,1)S(1)} %get-tuple-element.72), channel_id=1, source_target_pairs={{0,2},{2,0},{4,6},{6,4},{8,10},{10,8},{12,14},{14,12},{1,3},{3,1},... | collective-permute-start | bytes 393224 | tf_op jit(solution)/shard_map/ppermute | solution.py:320
  31.3 9.4 %collective-permute-start.12 = (bf16[32,2048]{1,0:T(8,128)(2,1)S(1)}, bf16[32,2048]{1,0:T(8,128)(2,1)S(1)}, u32[]{:S(2)}, u32[]{:S(2)}) collective-permute-start(bf16[32,2048]{1,0:T(8,128)(2,1)S(1)} %add_convert_fusion.2), channel_id=1, source_target_pairs={{0,12},{2,14},{4,8},{6,10},{8,4},{10,6},{12,0},{14,2},{1,13},{3,15... | collective-permute-start | bytes 393224 | tf_op jit(solution)/shard_map/ppermute | solution.py:323
  33.5 7.2 %collective-permute-start.13 = (bf16[32,2048]{1,0:T(8,128)(2,1)S(1)}, bf16[32,2048]{1,0:T(8,128)(2,1)S(1)}, u32[]{:S(2)}, u32[]{:S(2)}) collective-permute-start(bf16[32,2048]{1,0:T(8,128)(2,1)S(1)} %get-tuple-element.67), channel_id=1, source_target_pairs={{0,2},{2,0},{4,6},{6,4},{8,10},{10,8},{12,14},{14,12},{1,3},{3,1},... | collective-permute-start | bytes 393224 | tf_op jit(solution)/shard_map/ppermute | solution.py:320
  35.4 9.2 %collective-permute-start.16 = (bf16[32,2048]{1,0:T(8,128)(2,1)S(1)}, bf16[32,2048]{1,0:T(8,128)(2,1)S(1)}, u32[]{:S(2)}, u32[]{:S(2)}) collective-permute-start(bf16[32,2048]{1,0:T(8,128)(2,1)S(1)} %add_convert_fusion.1), channel_id=1, source_target_pairs={{0,8},{2,10},{4,12},{6,14},{8,0},{10,2},{12,4},{14,6},{1,9},{3,11}... | collective-permute-start | bytes 393224 | tf_op jit(solution)/shard_map/ppermute | solution.py:323
  38.7 5.9 %collective-permute-start.14 = (bf16[32,2048]{1,0:T(8,128)(2,1)S(1)}, bf16[32,2048]{1,0:T(8,128)(2,1)S(1)}, u32[]{:S(2)}, u32[]{:S(2)}) collective-permute-start(bf16[32,2048]{1,0:T(8,128)(2,1)S(1)} %get-tuple-element.70), channel_id=1, source_target_pairs={{0,2},{2,0},{4,6},{6,4},{8,10},{10,8},{12,14},{14,12},{1,3},{3,1},... | collective-permute-start | bytes 393224 | tf_op jit(solution)/shard_map/ppermute | solution.py:320
  40.7 5.3 %collective-permute-start.17 = (bf16[32,2048]{1,0:T(8,128)(2,1)S(1)}, bf16[32,2048]{1,0:T(8,128)(2,1)S(1)}, u32[]{:S(2)}, u32[]{:S(2)}) collective-permute-start(bf16[32,2048]{1,0:T(8,128)(2,1)S(1)} %add_convert_fusion), channel_id=1, source_target_pairs={{0,4},{2,6},{4,0},{6,2},{8,12},{10,14},{12,8},{14,10},{1,5},{3,7},... | collective-permute-start | bytes 393224 | tf_op jit(solution)/shard_map/ppermute | solution.py:323
  46.1 1.3 %collective-permute-start.18 = (bf16[32,1024]{1,0:T(8,128)(2,1)S(1)}, bf16[32,1024]{1,0:T(8,128)(2,1)S(1)}, u32[]{:S(2)}, u32[]{:S(2)}) collective-permute-start(bf16[32,1024]{1,0:T(8,128)(2,1)S(1)} %get-tuple-element.76), channel_id=1, source_target_pairs={{0,1},{1,0},{2,3},{3,2},{4,5},{5,4},{6,7},{7,6},{8,9},{9,8},{10,11... | collective-permute-start | bytes 196616 | tf_op jit(solution)/shard_map/ppermute | solution.py:383
